TPU v7x, 32 devices: a whole 2x2x4 slice. The times are simulated.
32 devices in a mesh: replica: 4 (over x, core), shard: 8 (over z, y).
Axes of the slice: x: 2, y: 2, z: 4, core: 2. Of those that a mesh axis runs over, the one named last changes fastest.
Arguments:
- hidden_in: bfloat16 [8192, 2048], P(('replica', 'shard')), may hold values from -6 to 6
- out_grad: bfloat16 [8192, 2048], P(('replica', 'shard')), may hold values from -6 to 6
- routes: int32 [8192, 6], P(('replica', 'shard')), may hold values from 0 to 15, all different within a row; in each aligned block of 256 rows (0 to 255, 256 to 511, ...) at most 128 rows name the same one
- seq_adapter: int32 [4], P('replica'), may hold values from 0 to 7
- attn_gain: float32 [2048], replicated, may hold values from 0.5 to 1.5
- latent_gain: float32 [512], replicated, may hold values from 0.5 to 1.5
- ffn_gain: float32 [2048], replicated, may hold values from 0.5 to 1.5
- w_qa: bfloat16 [2048, 3648], P('shard'), may hold values from -0.125 to 0.125
- w_kvb: bfloat16 [512, 4096], P('shard'), may hold values from -0.25 to 0.25
- w_out: bfloat16 [2048, 2048], P('shard'), may hold values from -2 to 2
- w_router: bfloat16 [2048, 16], replicated, may hold values from -0.0625 to 0.0625
- w_shared_in: bfloat16 [2048, 5632], P('shard'), may hold values from -0.125 to 0.125
- w_shared_out: bfloat16 [2816, 2048], P('shard'), may hold values from -0.109375 to 0.109375
- w_expert_in: bfloat16 [16, 2048, 2816], P('shard'), may hold values from -0.125 to 0.125
- w_expert_out: bfloat16 [16, 1408, 2048], P('shard'), may hold values from -1 to 1
- qa_down: bfloat16 [8, 16, 2048], P('shard'), may hold values from -0.125 to 0.125
- qa_up: bfloat16 [8, 16, 3648], P('shard'), may hold values from -0.4375 to 0.4375
- kvb_down: bfloat16 [8, 16, 512], P('shard'), may hold values from -0.25 to 0.25
- kvb_up: bfloat16 [8, 16, 4096], P('shard'), may hold values from -0.4375 to 0.4375
- out_down: bfloat16 [8, 16, 2048], P('shard'), may hold values from -2 to 2
- out_up: bfloat16 [8, 16, 2048], P('shard'), may hold values from -0.75 to 0.75
- gu_down: bfloat16 [8, 16, 2048], P('shard'), may hold values from -0.125 to 0.125
- gu_up: bfloat16 [8, 16, 5632], P('shard'), may hold values from -0.4375 to 0.4375
- dn_down: bfloat16 [8, 16, 2816], P('shard'), may hold values from -0.109375 to 0.109375
- dn_up: bfloat16 [8, 16, 2048], P('shard'), may hold values from -0.4375 to 0.4375
Outputs:
- block_out: bfloat16 [8192, 2048], P(('replica', 'shard'))
- hidden_grad: float32 [8192, 2048], P(('replica', 'shard'))
- qa_down_grad: float32 [8, 16, 2048], P('shard')
- qa_up_grad: float32 [8, 16, 3648], P('shard')
- kvb_down_grad: float32 [8, 16, 512], P('shard')
- kvb_up_grad: float32 [8, 16, 4096], P('shard')
- out_down_grad: float32 [8, 16, 2048], P('shard')
- out_up_grad: float32 [8, 16, 2048], P('shard')
- gu_down_grad: float32 [8, 16, 2048], P('shard')
- gu_up_grad: float32 [8, 16, 5632], P('shard')
- dn_down_grad: float32 [8, 16, 2816], P('shard')
- dn_up_grad: float32 [8, 16, 2048], P('shard')
Inputs may be any that keep to these rules, and one draw needn't show every extreme that they name: `routes`: each row names 6 different experts; in each aligned block of 256 rows (the rows of one device) no expert is named by more than 128 rows.
All inputs are finite; a program needn't handle non-finite values.
Results may differ from a plain program's by a relative error of at most 0.025.
Values may be sent and summed in bfloat16 or wider, within the bound.
No kernel may reach another device: no remote copies, remote signals or barrier semaphores. Data moves between devices by JAX's collectives and lax.ppermute only.
A program may use at most 384 MiB of HBM per device.

v0:
```python
import functools
import math

import jax
import jax.numpy as jnp
from jax import lax
from jax.experimental import pallas as pl
from jax.experimental.pallas import tpu as pltpu
from jax.sharding import PartitionSpec as P

D = 2048
HEADS = 16
NOPE = 128
ROPE = 64
VDIM = 128
LATENT = 512
TOPK = 6
RANK = 16
ADAPTERS = 8
BLOCK = 256
QW = HEADS * (NOPE + ROPE)
LW = LATENT + 2 * ROPE
LANES = 128
VMEM_LIMIT = 60 * 1024 * 1024
SCALE = (NOPE + ROPE) ** (-0.5)
EPS = 1e-06
f32 = jnp.float32
bf16 = jnp.bfloat16

NN = (((1,), (0,)), ((), ()))
NT = (((1,), (1,)), ((), ()))
TN = (((0,), (0,)), ((), ()))


def dot(a, b, dims=NN):
    return lax.dot_general(a, b, dims, preferred_element_type=f32)


def params(n):
    return pltpu.CompilerParams(
        dimension_semantics=("arbitrary",) * n, vmem_limit_bytes=VMEM_LIMIT
    )


def cost(flops, nbytes):
    return pl.CostEstimate(flops=int(flops), bytes_accessed=int(nbytes), transcendentals=0)


def gate_kernel(*refs):
    del refs


def gate(values, marks):
    anywhere = pl.BlockSpec(memory_space=pl.ANY)
    values, marks = tuple(values), tuple(marks)
    return pl.pallas_call(
        gate_kernel,
        in_specs=[anywhere] * len(values + marks),
        out_specs=[anywhere] * len(values),
        out_shape=[jax.ShapeDtypeStruct(v.shape, v.dtype) for v in values],
        input_output_aliases={i: i for i in range(len(values))},
        cost_estimate=cost(0, 0),
        name="gate",
    )(*values, *marks)


def zero_kernel(*refs):
    refs[-1][0] = 0


def zero_after(*marks):
    anywhere = pl.BlockSpec(memory_space=pl.ANY)
    return pl.pallas_call(
        zero_kernel,
        in_specs=[anywhere] * len(marks),
        out_specs=pl.BlockSpec(memory_space=pltpu.SMEM),
        out_shape=jax.ShapeDtypeStruct((1,), jnp.int32),
        cost_estimate=cost(0, 0),
        name="zero_after",
    )(*marks)[0]


def ring_of(count):
    return list(range(0, count, 2)) + list(range(count - 1, 0, -2))


class Ring:
    def __init__(self, count):
        order = ring_of(count)
        place_of = [order.index(i) for i in range(count)]
        self.count = count
        pos = jnp.asarray(place_of, jnp.int32)[lax.axis_index("shard")]
        self.owners = jnp.asarray(order, jnp.int32)[(pos + jnp.arange(count)) % count]
        self.right = [(order[i], order[(i + 1) % count]) for i in range(count)]
        self.left = [(order[i], order[(i - 1) % count]) for i in range(count)]

    def owner(self, off):
        return self.owners[off % self.count]

    def send_right(self, v):
        return lax.ppermute(v, "shard", self.right)

    def send_left(self, v):
        return lax.ppermute(v, "shard", self.left)

    def scatter_sum(self, piece, holds):
        half = self.count // 2
        far = piece(half)
        n = far.shape[0] // 2
        r, l = far[:n], far[n:]
        if half in holds:
            r, l = gate((r, l), holds[half]())
        r, l = self.send_right(r), self.send_left(l)
        for h in range(half - 1, 0, -1):
            up, down = piece(h), piece(-h)
            if h in holds:
                r, l = gate((r, l), holds[h](r, l))
            if r.shape[0] == n:
                up = jnp.concatenate([up[:n].astype(f32) + r.astype(f32), up[n:].astype(f32)], 0)
                down = jnp.concatenate([down[:n].astype(f32), down[n:].astype(f32) + l.astype(f32)], 0)
            else:
                up = up.astype(f32) + r.astype(f32)
                down = down.astype(f32) + l.astype(f32)
            r, l = self.send_right(up.astype(bf16)), self.send_left(down.astype(bf16))
        return piece(0).astype(f32) + r.astype(f32) + l.astype(f32)


class Walk:
    def __init__(self, ring, *arrays):
        self.ring, self.own, self.pairs, self.halves = ring, list(arrays), [], None

    def hop(self, *marks):
        half, k = self.ring.count // 2, len(self.own)
        if self.pairs:
            held = gate(self.pairs[-1], marks)
            self.pairs[-1] = held
            r, l = held[:k], held[k:]
        else:
            if marks:
                self.own = gate(self.own, marks)
            r = l = self.own
        if len(self.pairs) < half - 1:
            right = [self.ring.send_right(v) for v in r]
            left = [self.ring.send_left(v) for v in l]
            self.pairs.append(right + left)
            return self.pairs[-1]
        right = [self.ring.send_right(v[: v.shape[0] // 2]) for v in r]
        left = [self.ring.send_left(v[v.shape[0] // 2 :]) for v in l]
        self.halves = right + left
        return self.halves

    def blocks(self, i=0):
        k = len(self.own)
        out = [(0, 0, self.own[i])]
        for h, pair in enumerate(self.pairs):
            out += [(-h - 1, 0, pair[i]), (h + 1, 0, pair[k + i])]
        far = self.ring.count // 2
        n = self.own[i].shape[0] // 2
        return out + [(far, 0, self.halves[i]), (far, n, self.halves[k + i])]


def pair_swap(v, replicas):
    return lax.ppermute(v, "replica", [(i, i ^ 1) for i in range(replicas)])


def fill_rows(info, places, blocks, out):
    count = info.shape[0] - 1
    for (off, n, row, half, other), block in zip(places, blocks):
        core = info[count]
        at = info[off % count] * n + row + half * (1 - core if other else core)
        out[pl.ds(pl.multiple_of(at, 16), block.shape[0]), :] = block[...]


def place_kernel(info, *refs, places):
    fill_rows(info, places, refs[:-1], refs[-1])


def place_rows(info, places, blocks, height, first=0, width=None, cut=None):
    width = width or blocks[0].shape[1]
    cut = cut or next((c for c in (2048, 1024) if width % c == 0 and height * c <= 1 << 21), width)
    at = first // cut
    spec = pltpu.PrefetchScalarGridSpec(
        num_scalar_prefetch=1,
        grid=(width // cut,),
        in_specs=[pl.BlockSpec((b.shape[0], cut), lambda i, s: (0, at + i)) for b in blocks],
        out_specs=pl.BlockSpec((height, cut), lambda i, s: (0, i)),
    )
    return pl.pallas_call(
        functools.partial(place_kernel, places=places),
        grid_spec=spec,
        out_shape=jax.ShapeDtypeStruct((height, width), blocks[0].dtype),
        compiler_params=params(1),
        cost_estimate=cost(0, height * width * 4),
        name="place_rows",
    )(info, *blocks)


def whole_rows(info, blocks, n):
    places = [(off, n, row, 0, False) for off, row, _ in blocks]
    return place_rows(info, places, [v for _, _, v in blocks], (info.shape[0] - 1) * n)


def pack_kernel(core, qa_ref, kvb_ref, out_ref, all_ref, *, fold):
    del core
    rows, wide = kvb_ref.shape[0], kvb_ref.shape[1] // fold
    all_ref[:, :QW] = qa_ref[:, :QW]
    for i in range(fold):
        all_ref[i * rows : (i + 1) * rows, QW : QW + wide] = kvb_ref[:, i * wide : (i + 1) * wide]
    all_ref[:, QW + wide : QW + wide + D] = out_ref[...]
    rest = jnp.zeros((all_ref.shape[0], LW - LATENT - ROPE), all_ref.dtype)
    all_ref[:, QW + wide + D :] = jnp.concatenate([qa_ref[:, QW:], rest], 1)


def pack_weights(core, w_qa, w_kvb, w_out, replicas):
    parts = 2 if replicas % 2 == 0 else 1
    height, kvb_rows = w_out.shape[0] // parts, w_kvb.shape[0] // parts
    fold = height // kvb_rows
    wide = w_kvb.shape[1] // fold
    width = QW + wide + D + LW
    mine = (core % parts).reshape(1)
    share = lambda n, w: pl.BlockSpec((n, w.shape[1]), lambda i, s: (s[0], 0))
    spec = pltpu.PrefetchScalarGridSpec(
        num_scalar_prefetch=1,
        grid=(1,),
        in_specs=[share(height, w_qa), share(kvb_rows, w_kvb), share(height, w_out)],
        out_specs=pl.BlockSpec((height, width), lambda i, s: (0, 0)),
    )
    packed = pl.pallas_call(
        functools.partial(pack_kernel, fold=fold),
        grid_spec=spec,
        out_shape=jax.ShapeDtypeStruct((height, width), bf16),
        compiler_params=params(1),
        cost_estimate=cost(0, height * width * 4),
        name="pack_weights",
    )(mine, w_qa, w_kvb, w_out)
    return kvb_rows, fold, wide, packed


def own_share(w, replicas, zero=0):
    if replicas % 2:
        return w
    half = w.shape[0] // 2
    return lax.dynamic_slice_in_dim(w, lax.axis_index("replica") % 2 * half + zero, half, 0)


class Swaps:
    def __init__(self, ring, walk, replicas):
        self.ring, self.walk, self.replicas = ring, walk, replicas
        self.pairs = []

    def swap(self, blocks):
        got = [pair_swap(v, self.replicas) for v in blocks] if self.replicas % 2 == 0 else []
        self.pairs.append(got)
        return got

    def rows(self, i, n):
        walk, k = self.walk, len(self.walk.own)
        paired = self.replicas % 2 == 0
        far = self.ring.count // 2
        half = walk.own[i].shape[0] // 2
        got = [(0, 0, walk.own, i)]
        for h, pair in enumerate(walk.pairs):
            got += [(-h - 1, 0, pair, i), (h + 1, 0, pair, k + i)]
        got += [(far, 0, walk.halves, i), (far, half, walk.halves, k + i)]
        sets = [walk.own] + list(walk.pairs) + [walk.halves]
        places, out = [], []
        for off, row, blocks, j in got:
            where = next(m for m, v in enumerate(sets) if v is blocks)
            step = n // 2 if paired else 0
            places.append((off, n, row, step, False))
            out.append(blocks[j])
            if paired:
                places.append((off, n, row, step, True))
                out.append(self.pairs[where][j])
        return places, out


def rotate_pair(lane, v):
    half = ROPE // 2
    return jnp.where(lane < half, -pltpu.roll(v, LANES - half, 1), pltpu.roll(v, half, 1))


def unrotate_pair(lane, v):
    half = ROPE // 2
    return jnp.where(lane < half, pltpu.roll(v, LANES - half, 1), -pltpu.roll(v, half, 1))


def query_kernel(info, hb_ref, r_ref, up_ref, cos_ref, sin_ref, *rest, places):
    blocks, q_ref, w_ref = rest[:-2], rest[-2], rest[-1]
    fill_rows(info, places, blocks, w_ref)
    acc = dot(hb_ref[...], w_ref[...]) + dot(r_ref[...], up_ref[...])
    lane = lax.broadcasted_iota(jnp.int32, (acc.shape[0], LANES), 1)
    for i in range(2):
        own = acc if i == 0 else pltpu.roll(acc, NOPE + ROPE, 1)
        rope = own[:, LANES : 2 * LANES]
        turned = rope * cos_ref[...] + rotate_pair(lane, rope) * sin_ref[...]
        turned = jnp.where(lane == LANES - 1, 1.0, turned)
        q_ref[i] = jnp.concatenate([own[:, :LANES], turned], 1).astype(bf16)


def query_heads(info, hb, r, places, blocks, up, cos, sin):
    tokens = hb.shape[0]
    width = 2 * (NOPE + ROPE)
    whole = lambda a: pl.BlockSpec(a.shape, lambda i, s: (0,) * a.ndim)
    column = lambda a: pl.BlockSpec((a.shape[0], width), lambda i, s: (0, i))
    spec = pltpu.PrefetchScalarGridSpec(
        num_scalar_prefetch=1,
        grid=(HEADS // 2,),
        in_specs=[whole(hb), whole(r), column(up), whole(cos), whole(sin)]
        + [column(block) for block in blocks],
        out_specs=pl.BlockSpec((2, tokens, 2 * LANES), lambda i, s: (i, 0, 0)),
        scratch_shapes=[pltpu.VMEM((D, width), bf16)],
    )
    return pl.pallas_call(
        functools.partial(query_kernel, places=places),
        grid_spec=spec,
        out_shape=jax.ShapeDtypeStruct((HEADS, tokens, 2 * LANES), bf16),
        compiler_params=params(1),
        cost_estimate=cost(2 * tokens * D * QW, D * QW * 2),
        name="query_heads",
    )(info, hb, r, up, cos, sin, *blocks)


def query_back_kernel(info, dq_ref, up_ref, rt_ref, *rest, places):
    blocks = rest[:-6]
    dhb_ref, dr_ref, dup_ref, acc, racc, w_ref = rest[-6:]
    i = pl.program_id(0)
    tokens = dq_ref.shape[1]

    @pl.when(i == 0)
    def _():
        acc[...] = jnp.zeros_like(acc)
        racc[...] = jnp.zeros_like(racc)

    fill_rows(info, places, blocks, w_ref)
    pad = jnp.zeros((tokens, LANES), f32)
    first = jnp.concatenate([dq_ref[0].astype(f32), pad], 1)
    second = jnp.concatenate([dq_ref[1].astype(f32), pad], 1)
    both = (first + pltpu.roll(second, NOPE + ROPE, 1)).astype(bf16)
    acc[...] += dot(both, w_ref[...], NT)
    racc[...] += dot(both, up_ref[...], NT)
    dup_ref[...] = dot(rt_ref[...], both)

    @pl.when(i == pl.num_programs(0) - 1)
    def _():
        dhb_ref[...] = acc[...]
        dr_ref[...] = racc[...]


def query_back(info, dq, places, blocks, up, rt):
    tokens = dq.shape[1]
    width = 2 * (NOPE + ROPE)
    column = lambda a: pl.BlockSpec((a.shape[0], width), lambda i, s: (0, i))
    still = lambda *shape: pl.BlockSpec(shape, lambda i, s: (0, 0))
    spec = pltpu.PrefetchScalarGridSpec(
        num_scalar_prefetch=1,
        grid=(HEADS // 2,),
        in_specs=[
            pl.BlockSpec((2, tokens, 2 * LANES), lambda i, s: (i, 0, 0)),
            column(up),
            still(*rt.shape),
        ]
        + [column(block) for block in blocks],
        out_specs=[still(tokens, D), still(tokens, LANES), column(up)],
        scratch_shapes=[
            pltpu.VMEM((tokens, D), f32),
            pltpu.VMEM((tokens, LANES), f32),
            pltpu.VMEM((D, width), bf16),
        ],
    )
    return pl.pallas_call(
        functools.partial(query_back_kernel, places=places),
        grid_spec=spec,
        out_shape=[
            jax.ShapeDtypeStruct((tokens, D), f32),
            jax.ShapeDtypeStruct((tokens, LANES), f32),
            jax.ShapeDtypeStruct((LANES, QW), f32),
        ],
        compiler_params=params(1),
        cost_estimate=cost(2 * tokens * D * QW, D * QW * 2),
        name="query_back",
    )(info, dq, up, rt, *blocks)


LOG2E = math.log2(math.e)


def attend_kernel(l_ref, w_ref, u_ref, q_ref, mix_ref, lse_ref, kv_ref):
    w = w_ref[...].reshape(LATENT, NOPE + VDIM)
    kv = dot(l_ref[:, :LATENT], w) + dot(l_ref[:, LATENT:], u_ref[...])
    kv = kv.astype(bf16)
    kv_ref[...] = kv
    keys = jnp.concatenate([kv[:, :NOPE], l_ref[:, LATENT:]], 1)
    values = jnp.concatenate([kv[:, NOPE:], jnp.ones((kv.shape[0], LANES), bf16)], 1)
    scores = dot(q_ref[0], keys, NT)
    top = jnp.max(scores, axis=1, keepdims=True)
    weights = jnp.exp2((scores - top) * (SCALE * LOG2E)).astype(bf16)
    both = dot(weights, values)
    total = both[:, VDIM:]
    mix_ref[...] = (both[:, :VDIM] / total).astype(bf16)
    lse = top * (SCALE * LOG2E) + jnp.log2(total)
    lse_ref[0] = lse.T[:8]


def folded(w_kvb, at):
    pieces, _, rows, width = w_kvb.shape
    wide = NOPE + VDIM
    per = width // wide
    return pl.BlockSpec(
        (pieces, 1, rows, wide), lambda h: (0, (at + h) // per, 0, (at + h) % per)
    )


def attend(l_all, w_kvb, u_kvb, q):
    length = l_all.shape[0]
    tokens = q.shape[1]
    wide = NOPE + VDIM
    return pl.pallas_call(
        attend_kernel,
        grid=(HEADS,),
        in_specs=[
            pl.BlockSpec((length, LW), lambda h: (0, 0)),
            folded(w_kvb, 0),
            pl.BlockSpec((LANES, wide), lambda h: (0, h)),
            pl.BlockSpec((1, tokens, 2 * LANES), lambda h: (h, 0, 0)),
        ],
        out_specs=[
            pl.BlockSpec((tokens, VDIM), lambda h: (0, h)),
            pl.BlockSpec((1, 8, tokens), lambda h: (h, 0, 0)),
            pl.BlockSpec((length, wide), lambda h: (0, h)),
        ],
        out_shape=[
            jax.ShapeDtypeStruct((tokens, HEADS * VDIM), bf16),
            jax.ShapeDtypeStruct((HEADS, 8, tokens), f32),
            jax.ShapeDtypeStruct((length, HEADS * wide), bf16),
        ],
        compiler_params=params(1),
        cost_estimate=cost(HEADS * 2 * length * (LW * 256 + tokens * 512), 8e6),
        name="attend",
    )(l_all, w_kvb, u_kvb, q)


def attend_back_kernel(
    l_ref,
    lt_ref,
    w_ref,
    u_ref,
    kv_ref,
    q_ref,
    lse_ref,
    delta_ref,
    dm_ref,
    cos_ref,
    sin_ref,
    was_ref,
    dq_ref,
    dl_ref,
    du_ref,
    acc,
):
    h = pl.program_id(0)

    @pl.when(h == 0)
    def _():
        if was_ref.shape == acc.shape:
            acc[...] = was_ref[...].astype(f32)
        else:
            acc[...] = jnp.zeros_like(acc)

    keys = jnp.concatenate([kv_ref[:, :NOPE], l_ref[:, LATENT:]], 1)
    values = kv_ref[:, NOPE:]
    scores = dot(keys, q_ref[0], NT)
    probs = jnp.exp2(scores * (SCALE * LOG2E) - lse_ref[0, :1])
    dvalues = dot(probs.astype(bf16), dm_ref[...])
    dprobs = dot(values, dm_ref[...], NT)
    dscores = (probs * (dprobs - delta_ref[0, :1])).astype(bf16)
    dq = dot(dscores, keys, TN) * SCALE
    lane = lax.broadcasted_iota(jnp.int32, (dq.shape[0], LANES), 1)
    rope = dq[:, LANES:]
    rope = rope * cos_ref[...] + unrotate_pair(lane, rope) * sin_ref[...]
    dq_ref[0] = jnp.concatenate([dq[:, :LANES], rope], 1).astype(bf16)
    dkeys = dot(dscores, q_ref[0]) * SCALE
    dkv = jnp.concatenate([dkeys[:, :NOPE], dvalues], 1).astype(bf16)
    acc[:, :LATENT] += dot(dkv, w_ref[...].reshape(LATENT, NOPE + VDIM), NT)
    acc[:, LATENT:] += dot(dkv, u_ref[...], NT) + dkeys[:, NOPE:]
    du_ref[...] = dot(lt_ref[...], dkv)

    @pl.when(h == pl.num_programs(0) - 1)
    def _():
        dl_ref[...] = acc[...].astype(bf16)


def attend_back(part, l_all, lt, w_kvb, u_kvb, kv, q, lse, delta, dmix, cos, sin, was):
    length = l_all.shape[0]
    tokens = q.shape[1]
    wide = NOPE + VDIM
    heads = HEADS // 2
    at = part * heads
    still = lambda a: pl.BlockSpec(a.shape, lambda h: (0, 0))
    column = lambda n, w: pl.BlockSpec((n, w), lambda h: (0, at + h))
    head = lambda *shape: pl.BlockSpec((1,) + shape, lambda h: (at + h, 0, 0))
    return pl.pallas_call(
        attend_back_kernel,
        grid=(heads,),
        in_specs=[
            still(l_all),
            still(lt),
            folded(w_kvb, at),
            column(LANES, wide),
            column(length, wide),
            head(tokens, 2 * LANES),
            head(8, tokens),
            head(8, tokens),
            column(tokens, VDIM),
            still(cos),
            still(sin),
            still(was),
        ],
        out_specs=[
            pl.BlockSpec((1, tokens, 2 * LANES), lambda h: (h, 0, 0)),
            pl.BlockSpec((length, LW), lambda h: (0, 0)),
            pl.BlockSpec((LANES, wide), lambda h: (0, h)),
        ],
        out_shape=[
            jax.ShapeDtypeStruct((heads, tokens, 2 * LANES), bf16),
            jax.ShapeDtypeStruct((length, LW), bf16),
            jax.ShapeDtypeStruct((LANES, heads * wide), f32),
        ],
        scratch_shapes=[pltpu.VMEM((length, LW), f32)],
        compiler_params=params(1),
        cost_estimate=cost(heads * 2 * length * (LW * 256 + tokens * 1024), 30e6),
        name="attend_back",
    )(l_all, lt, w_kvb, u_kvb, kv, q, lse, delta, dmix, cos, sin, was)


def picks(slot_row, slots):
    row = lax.broadcasted_iota(jnp.int32, (slots, slot_row.shape[1]), 0)
    return jnp.where(row == slot_row, 1.0, 0.0).astype(bf16)


def silu_parts(gate):
    sig = 1.0 / (1.0 + jnp.exp(-gate))
    return gate * sig, sig * (1.0 + gate * (1.0 - sig))


def router_probs(logits, experts):
    lane = lax.broadcasted_iota(jnp.int32, logits.shape, 1)
    logits = jnp.where(lane < experts, logits, -1e30)
    odds = jnp.exp(logits - jnp.max(logits, axis=1, keepdims=True))
    return odds / jnp.sum(odds, axis=1, keepdims=True)


def routed_kernel(info, slot_ref, wr_ref, w_in, w_out, *rest, offs, slots, wide, experts):
    chunks, count = len(offs), info.shape[0] - 1
    x_refs, g_refs = rest[:chunks], rest[chunks : 2 * chunks]
    y_ref, dx_ref, pull_ref, rows, grads, hidden, dacts = rest[2 * chunks :]
    e = pl.program_id(0)
    ff = w_out.shape[1]
    weights = []
    for c in range(chunks):
        pick = picks(slot_ref[info[1 + offs[c] % count], pl.ds(e, 1), :], slots)
        at = pl.ds(c * slots, slots)
        x = dot(pick, x_refs[c][...]).astype(bf16)
        rows[at, :] = x
        weight = router_probs(dot(x, wr_ref[...]), experts)
        lane = lax.broadcasted_iota(jnp.int32, weight.shape, 1)
        weight = jnp.sum(jnp.where(lane == info[0] + e, weight, 0.0), axis=1, keepdims=True)
        weights.append(weight)
        grads[at, :] = (dot(pick, g_refs[c][...]) * weight).astype(bf16)
    weight = jnp.concatenate(weights, 0)
    for a in range(0, ff, wide):
        b = min(a + wide, ff)
        gate = dot(rows[...], w_in[0, :, a:b])
        up = dot(rows[...], w_in[0, :, ff + a : ff + b])
        dhid = dot(grads[...], w_out[0, a:b, :], NT)
        silu, slope = silu_parts(gate)
        hidden[:, a:b] = (silu * up).astype(bf16)
        dacts[:, a:b] = (dhid * up * slope).astype(bf16)
        dacts[:, ff + a : ff + b] = (dhid * silu).astype(bf16)
    pull = jnp.zeros((rows.shape[0], 1), f32)
    step = 2 * wide
    for a in range(0, D, step):
        y = dot(hidden[...], w_out[0, :, a : a + step])
        pull += jnp.sum(y * grads[:, a : a + step].astype(f32), axis=1, keepdims=True)
        y_ref[0, :, a : a + step] = (y * weight).astype(bf16)
        dx_ref[0, :, a : a + step] = dot(dacts[...], w_in[0, a : a + step, :], NT).astype(bf16)
    lane = lax.broadcasted_iota(jnp.int32, (rows.shape[0], LANES), 1)
    pull_ref[0] = jnp.where(lane == info[0] + e, pull, 0.0).astype(bf16)


def routed(info, offs, xs, gs, slot_all, w_router, experts, w_in, w_out):
    chunks, tokens = len(xs), xs[0].shape[0]
    local = w_in.shape[0]
    ff = w_out.shape[1]
    slots = tokens // 2
    rows = chunks * slots
    once = pl.Buffered(1)
    whole = lambda a: pl.BlockSpec(a.shape, lambda e, s: (0,) * a.ndim, pipeline_mode=once)
    out = pl.BlockSpec((1, rows, D), lambda e, s: (e, 0, 0))
    spec = pltpu.PrefetchScalarGridSpec(
        num_scalar_prefetch=1,
        grid=(local,),
        in_specs=[
            whole(slot_all),
            whole(w_router),
            pl.BlockSpec((1, D, 2 * ff), lambda e, s: (e, 0, 0)),
            pl.BlockSpec((1, ff, D), lambda e, s: (e, 0, 0)),
        ]
        + [whole(v) for v in (*xs, *gs)],
        out_specs=[out, out, pl.BlockSpec((1, rows, LANES), lambda e, s: (e, 0, 0))],
        scratch_shapes=[
            pltpu.VMEM((rows, D), bf16),
            pltpu.VMEM((rows, D), bf16),
            pltpu.VMEM((rows, ff), bf16),
            pltpu.VMEM((rows, 2 * ff), bf16),
        ],
    )
    shape = jax.ShapeDtypeStruct((local, rows, D), bf16)
    return pl.pallas_call(
        functools.partial(
            routed_kernel, offs=offs, slots=slots, wide=2 * LANES, experts=experts
        ),
        grid_spec=spec,
        out_shape=[shape, shape, jax.ShapeDtypeStruct((local, rows, LANES), bf16)],
        compiler_params=params(1),
        cost_estimate=cost(local * rows * D * ff * 12, local * D * ff * 6),
        name="routed",
    )(info, slot_all, w_router, w_in, w_out, *xs, *gs)


def shared_kernel(
    info,
    slot_ref,
    y_ref,
    dx_ref,
    pull_ref,
    wi_ref,
    wo_ref,
    u_ref,
    dn_ref,
    *rest,
    offs,
    slots,
    experts,
):
    blocks = rest[:-8]
    out_ref, dout_ref, gu_up_ref, gu_down_ref, dn_up_ref, dn_down_ref, x_ref, g_ref = rest[-8:]
    c = pl.program_id(0)
    chunks, count = len(offs), info.shape[0] - 1
    spot = sum(jnp.where(c == i, off % count, 0) for i, off in enumerate(offs))
    owner = info[1 + spot]
    for i in range(chunks):

        @pl.when(c == i)
        def _(i=i):
            x_ref[...] = blocks[i][...]
            g_ref[...] = blocks[chunks + i][...]

    local = y_ref.shape[0]
    half = dn_ref.shape[0]
    x, g = x_ref[...], g_ref[...]
    proj = dot(x, wi_ref[...])
    r = proj[:, 2 * half :].astype(bf16)
    prob = router_probs(proj[:, 2 * half :], experts)
    acts = proj[:, : 2 * half] + dot(r, u_ref[...])
    gate, up = acts[:, :half], acts[:, half:]
    silu, slope = silu_parts(gate)
    inner = (silu * up).astype(bf16)
    rdn = dot(inner, dn_ref[...]).astype(bf16)
    back = dot(g, wo_ref[...], NT)
    drdn = back[:, half:].astype(bf16)
    dinner = back[:, :half] + dot(drdn, dn_ref[...], NT)
    dboth = jnp.concatenate([dinner * up * slope, dinner * silu], 1).astype(bf16)
    dr = dot(dboth, u_ref[...], NT)

    pick = jnp.concatenate([picks(slot_ref[owner, e : e + 1, :], slots) for e in range(local)], 0)
    rows = lambda ref: jnp.concatenate([ref[e] for e in range(local)], 0)
    out = dot(jnp.concatenate([inner, rdn], 1), wo_ref[...]) + dot(pick, rows(y_ref), TN)
    out_ref[0] = out.astype(bf16)
    pulls = dot(pick, rows(pull_ref), TN)
    dlogit = pulls - prob * jnp.sum(pulls, axis=1, keepdims=True)
    dsmall = (dr + dlogit).astype(bf16)
    dx = dot(jnp.concatenate([dboth, dsmall], 1), wi_ref[...], NT)
    dout_ref[0] = (dx + dot(pick, rows(dx_ref), TN)).astype(bf16)

    @pl.when(c == 0)
    def _():
        gu_up_ref[...] = jnp.zeros_like(gu_up_ref)
        gu_down_ref[...] = jnp.zeros_like(gu_down_ref)
        dn_up_ref[...] = jnp.zeros_like(dn_up_ref)
        dn_down_ref[...] = jnp.zeros_like(dn_down_ref)

    gu_up_ref[...] += dot(r, dboth, TN)
    gu_down_ref[...] += dot(dr.astype(bf16), x, TN)
    dn_up_ref[...] += dot(rdn, g, TN)
    dn_down_ref[...] += dot(drdn, inner, TN)


def shared(info, offs, xs, gs, slot_all, experts, y, dx, pull, wi, wo, u, dn):
    chunks, tokens = len(xs), xs[0].shape[0]
    local = y.shape[0]
    slots = tokens // 2
    half = dn.shape[0]
    whole = lambda a: pl.BlockSpec(a.shape, lambda c, s: (0,) * a.ndim)
    one = pl.BlockSpec((1, tokens, D), lambda c, s: (c, 0, 0))
    rows = lambda a: pl.BlockSpec((local, slots, a.shape[2]), lambda c, s: (0, c, 0))
    still = lambda *shape: pl.BlockSpec(shape, lambda c, s: (0, 0))
    operands = [slot_all, y, dx, pull, wi, wo, u, dn, *xs, *gs]
    specs = [whole(slot_all), rows(y), rows(dx), rows(pull)]
    specs += [whole(a) for a in operands[4:]]
    spec = pltpu.PrefetchScalarGridSpec(
        num_scalar_prefetch=1,
        grid=(chunks,),
        in_specs=specs,
        out_specs=[
            one,
            one,
            still(LANES, 2 * half),
            still(LANES, D),
            still(LANES, D),
            still(LANES, half),
        ],
        scratch_shapes=[pltpu.VMEM((tokens, D), bf16)] * 2,
    )
    return pl.pallas_call(
        functools.partial(shared_kernel, offs=offs, slots=slots, experts=experts),
        grid_spec=spec,
        out_shape=[
            jax.ShapeDtypeStruct((chunks, tokens, D), bf16),
            jax.ShapeDtypeStruct((chunks, tokens, D), bf16),
            jax.ShapeDtypeStruct((LANES, 2 * half), f32),
            jax.ShapeDtypeStruct((LANES, D), f32),
            jax.ShapeDtypeStruct((LANES, D), f32),
            jax.ShapeDtypeStruct((LANES, half), f32),
        ],
        compiler_params=params(1),
        cost_estimate=cost(chunks * 4e9, chunks * 8e6),
        name="shared",
    )(info, *operands)


def rms_scale(v):
    return lax.rsqrt(jnp.mean(v * v, axis=-1, keepdims=True) + EPS)


def rms_back(v, scale, gain, dy):
    unit = v * scale
    gdy = gain * dy
    return (gdy - unit * jnp.mean(unit * gdy, axis=-1, keepdims=True)) * scale


def angles(positions):
    half = ROPE // 2
    ladder = jnp.arange(half).astype(f32)
    frequency = jnp.exp(ladder * (-2.0 * math.log(10000.0) / ROPE))
    turn = positions.astype(f32)[:, None] * frequency[None, :]
    return jnp.cos(turn), jnp.sin(turn)


def pad_lanes(v, width, before=0):
    return jnp.pad(v, ((0, 0), (before, width - before - v.shape[1])))


def pad_rows(v, height, before=0):
    return jnp.pad(v, ((before, height - before - v.shape[0]), (0, 0)))


def round_up(n, m):
    return -(-n // m) * m


def pack(parts, unit=LANES):
    return jnp.concatenate([pad_lanes(v, round_up(v.shape[1], unit)) for v in parts], 1)


def unpack(v, widths, unit=LANES):
    out, at = [], 0
    for w in widths:
        out.append(v[:, at : at + w])
        at += round_up(w, unit)
    return out


class Totals:
    def __init__(self, parts, shards):
        self.shards = shards
        self.widths = [v.shape[1] for v in parts]
        packed = pack(parts)
        self.columns = round_up(packed.shape[1], shards * LANES)
        packed = pad_lanes(packed, self.columns).astype(bf16)
        self.cut = self.columns // shards
        self.packed = packed.reshape(RANK, shards, self.cut).transpose(1, 0, 2)

    def deal(self):
        mine = lax.all_to_all(self.packed, "shard", split_axis=0, concat_axis=0, tiled=True)
        self.mine = jnp.sum(mine.astype(f32), axis=0).astype(bf16)
        return self.mine

    def gather(self, ids):
        seqs = lax.all_gather(self.mine, "replica", axis=0)
        chosen = (ids[None, :] == jnp.arange(ADAPTERS)[:, None]).astype(f32)
        sums = jnp.sum(chosen[:, :, None, None] * seqs.astype(f32)[None], axis=1).astype(bf16)
        self.sums = sums.reshape(self.shards, ADAPTERS // self.shards, RANK, self.cut)
        return self.sums

    def home(self):
        full = lax.all_to_all(self.sums, "shard", split_axis=0, concat_axis=0, tiled=True)
        full = full.transpose(1, 2, 0, 3).reshape(ADAPTERS // self.shards, RANK, self.columns)
        out, at = [], 0
        for w in self.widths:
            out.append(full[:, :, at : at + w].astype(f32))
            at += round_up(w, LANES)
        return out


def body(
    hidden_in,
    out_grad,
    routes,
    seq_adapter,
    attn_gain,
    latent_gain,
    ffn_gain,
    w_qa,
    w_kvb,
    w_out,
    w_router,
    w_shared_in,
    w_shared_out,
    w_expert_in,
    w_expert_out,
    qa_down,
    qa_up,
    kvb_down,
    kvb_up,
    out_down,
    out_up,
    gu_down,
    gu_up,
    dn_down,
    dn_up,
):
    shards = lax.axis_size("shard")
    replicas = lax.axis_size("replica")
    place = lax.axis_index("shard")
    tokens = hidden_in.shape[0]
    local = w_expert_in.shape[0]
    experts = local * shards
    ring = Ring(shards)
    adapter_id = seq_adapter[0]
    core = (lax.axis_index("replica") % 2).astype(jnp.int32)
    spots = jnp.concatenate([ring.owners, core.reshape(1)])
    ids = lax.all_gather(seq_adapter, "replica", axis=0, tiled=True)
    first = (place * local).astype(jnp.int32).reshape(1)

    tables = [qa_down, qa_up[:, :, :QW], qa_up[:, :, QW:], kvb_down, kvb_up, out_down, out_up]
    tables = [t[0] for t in tables + [gu_down, gu_up, dn_down, dn_up]]
    dealt = pack(tables)
    cut = round_up(dealt.shape[1], shards * LANES) // shards
    dealt = pad_lanes(dealt, cut * shards).reshape(RANK, shards, cut).transpose(1, 0, 2)
    dealt = lax.all_to_all(dealt, "shard", split_axis=0, concat_axis=0, tiled=True)
    dealt = lax.dynamic_index_in_dim(dealt, adapter_id, 0, keepdims=True)
    dealt = jnp.broadcast_to(dealt, (shards, RANK, cut))
    dealt = lax.all_to_all(dealt, "shard", split_axis=0, concat_axis=0, tiled=True)
    dealt = dealt.transpose(1, 0, 2).reshape(RANK, shards * cut)
    a_qd, a_quq, a_qul, a_kd, a_ku, a_od, a_ou, a_gd, a_gu, a_nd, a_nu = unpack(
        dealt, [t.shape[1] for t in tables]
    )

    kvb_rows, fold, kvb_wide, own_weights = pack_weights(core, w_qa, w_kvb, w_out, replicas)
    w_walk = Walk(ring, own_weights)
    w_swaps = Swaps(ring, w_walk, replicas)
    w1 = w_walk.hop()
    own_swap = w_swaps.swap(w_walk.own)
    w2 = w_walk.hop(*own_swap)
    u_q = pad_rows(a_quq, LANES)
    u_kvb = pad_rows(a_ku, LANES, ROPE)
    wr = pad_lanes(w_router, LANES)
    width = w_shared_out.shape[0]
    half = round_up(width, LANES)
    rows_in = w_shared_in.shape[0]
    if replicas % 2 == 0:
        core = lax.axis_index("replica") % 2
    mine = own_share(w_shared_in, replicas, zero_after(*w1))
    mine = mine.reshape(mine.shape[0], 2, shards, width).transpose(2, 0, 1, 3)
    mine = jnp.pad(mine, ((0, 0), (0, 0), (0, 0), (0, half - width)))
    mine = mine.reshape(shards, mine.shape[1], 2 * half)
    ready = mine
    mine = lax.all_to_all(mine, "shard", split_axis=0, concat_axis=0, tiled=True)
    if replicas % 2 == 0:
        other = pair_swap(mine, replicas)
        w_si = jnp.concatenate(
            [jnp.where(core == 0, mine, other), jnp.where(core == 0, other, mine)], 1
        )
    else:
        w_si = mine
    w_si = w_si.reshape(shards * rows_in, 2 * half)

    w_i = jnp.concatenate([w_si, pad_lanes(jnp.concatenate([w_router, a_gd.T], 1), LANES)], 1)
    w_o = jnp.concatenate([pad_rows(w_shared_out, half), pad_rows(a_nu, LANES)], 0)
    gu_g = lax.dynamic_slice_in_dim(a_gu, place * width, width, 1)
    gu_u = lax.dynamic_slice_in_dim(a_gu, shards * width + place * width, width, 1)
    u_gu = jnp.concatenate([pad_lanes(gu_g, half), pad_lanes(gu_u, half)], 1)
    u_gu = pad_rows(u_gu, LANES, experts)
    nd_own = lax.dynamic_slice_in_dim(a_nd, place * width, width, 1)
    dn_own = pad_rows(pad_lanes(nd_own.T, LANES), half)

    inputs = hidden_in.astype(f32)
    in_scale = rms_scale(inputs)
    hb = (inputs * in_scale * attn_gain).astype(bf16)
    r_qa = dot(hb, a_qd, NT).astype(bf16)
    swap1 = w_swaps.swap(w_walk.pairs[0])
    w3 = w_walk.hop(*swap1, ready)
    swap2 = w_swaps.swap(w_walk.pairs[1])
    w4 = w_walk.hop(*swap2, wr, w_o, u_gu, dn_own, r_qa, u_q, u_kvb, ids)
    w_swaps.swap(w_walk.pairs[2])
    w_swaps.swap(w_walk.halves)
    w_at, w_blocks = w_swaps.rows(0, w_out.shape[0])
    kvb_at, out_at, lat_at = QW, QW + kvb_wide, QW + kvb_wide + D
    w_lat = place_rows(spots, w_at, w_blocks, D, lat_at, LW, LANES)[:, : LATENT + ROPE]
    full_kvb = place_rows(spots, w_at, w_blocks, D, kvb_at, kvb_wide, kvb_wide)
    full_kvb = full_kvb.reshape(LATENT // kvb_rows, fold, kvb_rows, kvb_wide)
    full_out = place_rows(spots, w_at, w_blocks, D, out_at, D, D // 2)

    lat_raw = dot(hb, w_lat) + dot(r_qa, a_qul)
    latent_raw, rope_raw = lat_raw[:, :LATENT], lat_raw[:, LATENT:]
    lat_scale = rms_scale(latent_raw)
    latent = (latent_raw * lat_scale * latent_gain).astype(bf16)
    positions = place * tokens + jnp.arange(tokens)
    cos_half, sin_half = angles(positions)
    rh = ROPE // 2
    rope_a, rope_b = rope_raw[:, :rh], rope_raw[:, rh:]
    rope = jnp.concatenate(
        [rope_a * cos_half - rope_b * sin_half, rope_b * cos_half + rope_a * sin_half], 1
    ).astype(bf16)
    r_kv = dot(latent, a_kd, NT).astype(bf16)
    l_own = jnp.concatenate([latent, rope, r_kv, routes.astype(bf16)], 1)
    l_own = pad_lanes(l_own, LW)
    l_walk = Walk(ring, l_own)
    l_walk.hop()
    l_walk.hop()
    l_walk.hop()
    l4 = l_walk.hop()
    g_walk = Walk(ring, out_grad)
    g_walk.hop(*l4)
    last_lane = jnp.arange(LW) == LW - 1
    l_blocks = []
    for off, row, block in l_walk.blocks():
        hide = jnp.where(ring.owner(off) > place, -1e30, 0.0).astype(bf16)
        l_blocks.append((off, row, jnp.where(last_lane, hide, block)))
    l_all = whole_rows(spots, l_blocks, tokens)
    cos = pad_lanes(jnp.concatenate([cos_half, cos_half], 1), LANES)
    sin = pad_lanes(jnp.concatenate([sin_half, sin_half], 1), LANES)
    q = query_heads(
        spots, hb, pad_lanes(r_qa, LANES), w_at, w_blocks, u_q, cos, sin
    )

    mixture, lse, kv = attend(l_all, full_kvb, u_kvb, q)
    r_out = dot(mixture, a_od, NT).astype(bf16)
    after_attn = inputs + dot(mixture, full_out) + dot(r_out, a_ou)
    ffn_scale = rms_scale(after_attn)
    ffn_low = (after_attn * ffn_scale * ffn_gain).astype(bf16)

    at = LATENT + ROPE + RANK
    routes_all = l_all[:, at : at + TOPK].astype(jnp.int32).reshape(shards, tokens, TOPK)
    wanted = first[0] + jnp.arange(local)
    mask = jnp.any(routes_all[:, None, :, :] == wanted[None, :, None, None], axis=-1)
    before = jnp.triu(jnp.ones((tokens, tokens), bf16), 1)
    rank = lax.dot_general(
        mask.astype(bf16), before, (((2,), (0,)), ((), ())), preferred_element_type=f32
    )
    slot_all = jnp.where(mask, rank.astype(jnp.int32), -1)

    out_piece, dx_piece, small = {}, {}, []


    info = jnp.concatenate([first, ring.owners])

    def run_routed(members, *after):
        offs, xs, gs = ([m[i] for m in members] for i in range(3))
        if after:
            xs = gate(xs, after)
        return offs, xs, gs, *routed(
            info, offs, xs, gs, slot_all, wr, experts, w_expert_in, w_expert_out
        )

    def run_shared(offs, xs, gs, y, dxr, pull):
        out, dx, *grads = shared(
            info, offs, xs, gs, slot_all, experts, y, dxr, pull, w_i, w_o, u_gu, dn_own
        )
        small.append(grads)
        for i, off in enumerate(offs):
            out_piece[off], dx_piece[off] = out[i], dx[i]
        return grads[-1]

    far = shards // 2
    walk = Walk(ring, ffn_low)
    members = lambda h: [
        (off, x, g) for off, x, g in zip((-h, h), walk.pairs[h - 1], g_walk.pairs[h - 1])
    ]
    g_walk.hop(mixture)
    x1 = walk.hop()
    done = run_routed([(0, ffn_low, out_grad)])
    walk.hop(done[3])
    g_walk.hop(*x1)
    mark = run_shared(*done)
    done = run_routed(members(1), mark)
    x3 = walk.hop(done[3])
    g_walk.hop(*walk.pairs[1])
    mark = run_shared(*done)
    done = run_routed(members(2), mark)
    walk.hop(done[3])
    mark = run_shared(*done)
    opposite = (far, jnp.concatenate(walk.halves, 0), jnp.concatenate(g_walk.halves, 0))
    run_shared(*run_routed(members(3) + [opposite], mark))
    out_piece[-far], dx_piece[-far] = out_piece[far], dx_piece[far]
    small = [sum(parts[1:], parts[0]) for parts in zip(*small)]

    def spread(v, cols):
        return jnp.concatenate(
            [
                lax.dynamic_update_slice_in_dim(
                    jnp.zeros((RANK, cols), f32), part, place * width, 1
                )
                for part in v
            ],
            1,
        )

    g_gu_up = small[0][experts : experts + RANK]
    g_gu_up = spread([g_gu_up[:, :width], g_gu_up[:, half : half + width]], shards * width)
    g_gu_down = small[1][experts : experts + RANK]
    g_dn_up = small[2][:RANK]
    g_dn_down = spread([small[3][:RANK, :width]], shards * width)

    t_ffn, seen = Totals([g_gu_down, g_gu_up, g_dn_down, g_dn_up], shards), {}

    def late_hold(r, l):
        seen["near"] = (r, l)
        return (t_ffn.gather(ids),)

    ffn_grad = ring.scatter_sum(
        lambda off: dx_piece[off],
        {
            far - 1: lambda r, l: (t_ffn.packed,),
            far - 2: lambda r, l: (t_ffn.deal(),),
            far - 3: late_hold,
        },
    )

    d_after = out_grad.astype(f32) + rms_back(after_attn, ffn_scale, ffn_gain, ffn_grad)
    d_after_low = d_after.astype(bf16)
    dr_out = dot(d_after_low, a_ou, NT).astype(bf16)
    dmix = (dot(d_after_low, full_out, NT) + dot(dr_out, a_od)).astype(bf16)
    g_out_up = dot(r_out, d_after_low, TN)
    g_out_down = dot(dr_out, mixture, TN)
    delta = (dmix.astype(f32) * mixture.astype(f32)).reshape(tokens, HEADS, VDIM).sum(-1).T
    delta = jnp.broadcast_to(delta[:, None, :], (HEADS, 8, tokens))
    lt = l_all[:, LATENT:].T
    parts = []

    def back(*marks):
        was = parts[-1][1] if parts else jnp.zeros((8, LANES), bf16)
        (marked,) = gate((lse,), marks) if not parts else gate((lse + 0.0,), marks)
        parts.append(
            attend_back(
                len(parts), l_all, lt, full_kvb, u_kvb, kv, q, marked, delta, dmix, cos, sin, was
            )
        )
        return (parts[-1][2],)

    def first_arrived(r, l):
        seen["far"] = (r[:16], l[:16])
        return ()

    def next_arrived(r, l):
        seen["next"] = (r[:16], l[:16])
        return back(*seen["far"])

    out_sum = ring.scatter_sum(
        lambda off: out_piece[off],
        {
            far: lambda: (ffn_grad,),
            far - 1: first_arrived,
            far - 2: next_arrived,
            far - 3: lambda r, l: back(*seen["next"]),
        },
    )
    block_out = (after_attn + out_sum).astype(bf16)
    dq = jnp.concatenate([part[0] for part in parts], 0)
    dl = parts[-1][1]
    g_ku = jnp.concatenate([part[2] for part in parts], 1)
    g_kvb_up = g_ku[ROPE : ROPE + RANK]
    dhb_q, dr_q, g_qu = query_back(spots, dq, w_at, w_blocks, u_q, pad_lanes(r_qa, LANES).T)
    dl_own = ring.scatter_sum(
        lambda off: lax.dynamic_slice_in_dim(dl, ring.owner(off) * tokens, tokens, 0),
        {far - 2: lambda r, l: (dr_q,)},
    )
    dr_kv = dl_own[:, LATENT + ROPE : LATENT + ROPE + RANK].astype(bf16)
    d_latent = dl_own[:, :LATENT] + dot(dr_kv, a_kd)
    g_kvb_down = dot(dr_kv, latent, TN)
    d_latent = rms_back(latent_raw, lat_scale, latent_gain, d_latent)
    drope = dl_own[:, LATENT : LATENT + ROPE]
    drope_a, drope_b = drope[:, :rh], drope[:, rh:]
    drope = jnp.concatenate(
        [drope_a * cos_half + drope_b * sin_half, drope_b * cos_half - drope_a * sin_half], 1
    )
    d_lat = jnp.concatenate([d_latent, drope], 1).astype(bf16)
    dr_qa = (dr_q[:, :RANK] + dot(d_lat, a_qul, NT)).astype(bf16)
    dhb = dhb_q + dot(d_lat, w_lat, NT) + dot(dr_qa, a_qd)
    g_qa_up = jnp.concatenate([g_qu[:RANK], dot(r_qa, d_lat, TN)], 1)
    g_qa_down = dot(dr_qa, hb, TN)
    hidden_grad = d_after + rms_back(inputs, in_scale, attn_gain, dhb)

    t_attn = Totals(
        [g_qa_down, g_qa_up, g_kvb_down, g_kvb_up, g_out_down, g_out_up], shards
    )
    t_attn.deal()
    t_attn.gather(ids)
    return (block_out, hidden_grad, *t_attn.home(), *t_ffn.home())


def solution(mesh):
    rows = P(("replica", "shard"), None)
    cut2 = P("shard", None)
    cut3 = P("shard", None, None)
    in_specs = (
        (rows, rows, rows, P("replica"), P(), P(), P())
        + (cut2, cut2, cut2, P(), cut2, cut2, cut3, cut3)
        + (cut3,) * 10
    )
    out_specs = (rows, rows) + (cut3,) * 10
    return jax.shard_map(body, mesh=mesh, in_specs=in_specs, out_specs=out_specs, check_vma=False)
```

profile of v0, /device:TPU:0, one launch (start us, length us, event | category | flops | bytes accessed | tf_op | source)
XLA Modules:
  0.0 936.8 jit_solution(10092756522367546806)
XLA Ops:
  12.2 6.3 all-to-all-start
  18.4 31.3 %collective-permute-done.1.refs_0_ = bf16[128,6784]{1,0:T(8,128)(2,1)} collective-permute-done((bf16[128,6784]{1,0:T(8,128)(2,1)}, bf16[128,6784]{1,0:T(8,128)(2,1)}, u32[]{:S(2)}, u32[]{:S(2)}) %collective-permute-start.1) | collective-permute-done | bytes 1736736 | tf_op jit(solution)/shard_map/ppermute | solution.py:101
  63.7 8.1 all-to-all-done
  103.3 15.2 %collective-permute-start.9 = (bf16[128,6784]{1,0:T(8,128)(2,1)}, bf16[128,6784]{1,0:T(8,128)(2,1)}, u32[]{:S(2)}, u32[]{:S(2)}) collective-permute-start(bf16[128,6784]{1,0:T(8,128)(2,1)} %get-tuple-element.109.refs_6_.rest_6_), channel_id=1, source_target_pairs={{0,2},{2,4},{4,6},{6,7},{7,5},{5,3},{3,1},{1,0},{8,10},{10,12},{12... | collective-permute-start | bytes 5210120 | tf_op jit(solution)/shard_map/ppermute | solution.py:101
  120.1 7.9 all-to-all-done.1
  139.1 15.2 %collective-permute-done.10.refs_1_ = bf16[128,6784]{1,0:T(8,128)(2,1)S(1)} collective-permute-done((bf16[128,6784]{1,0:T(8,128)(2,1)}, bf16[128,6784]{1,0:T(8,128)(2,1)S(1)}, u32[]{:S(2)}, u32[]{:S(2)}) %collective-permute-start.10) | collective-permute-done | bytes 1736736 | tf_op jit(solution)/shard_map/ppermute | solution.py:104
  160.2 7.6 collective-permute-start.13
  170.5 14.9 %collective-permute-done.13.refs_14_.rest_14_ = bf16[64,6784]{1,0:T(8,128)(2,1)S(1)} collective-permute-done((bf16[64,6784]{1,0:T(8,128)(2,1)}, bf16[64,6784]{1,0:T(8,128)(2,1)S(1)}, u32[]{:S(2)}, u32[]{:S(2)}) %collective-permute-start.13) | collective-permute-done | bytes 868384 | tf_op jit(solution)/shard_map/ppermute | solution.py:101
  216.4 13.1 %collective-permute-done.17.refs_0_ = bf16[256,640]{1,0:T(8,128)(2,1)S(1)} collective-permute-done((bf16[256,640]{1,0:T(8,128)(2,1)}, bf16[256,640]{1,0:T(8,128)(2,1)S(1)}, u32[]{:S(2)}, u32[]{:S(2)}) %collective-permute-start.17) | collective-permute-done | bytes 327712 | tf_op jit(solution)/shard_map/ppermute | solution.py:101
  230.9 10.0 %collective-permute-start.19 = (bf16[256,640]{1,0:T(8,128)(2,1)}, bf16[256,640]{1,0:T(8,128)(2,1)S(1)}, u32[]{:S(2)}, u32[]{:S(2)}) collective-permute-start(bf16[256,640]{1,0:T(8,128)(2,1)} %get-tuple-element.113), channel_id=1, source_target_pairs={{0,2},{2,4},{4,6},{6,7},{7,5},{5,3},{3,1},{1,0},{8,10},{10,12},{12... | collective-permute-start | bytes 983048 | tf_op jit(solution)/shard_map/ppermute | solution.py:101
  242.0 6.2 collective-permute-done.19.refs_0_
  254.5 6.6 place_rows.7
  266.2 13.8 %query_heads.1.q_ref = bf16[16,256,256]{2,1,0:T(8,128)(2,1)} custom-call(s32[9]{0:T(128)} %get-tuple-element.262.info, bf16[256,2048]{1,0:T(8,128)(2,1)} %copy-done.10, bf16[256,128]{1,0:T(8,128)(2,1)} %pad.100.clone.r_ref, bf16[128,3072]{1,0:T(8,128)(2,1)} %pad.97.refs_9_.up_ref, f32[256,128]{1,0:T(8,128)} %get-tuple-element.278.cos_ref, ...), custom_call_target="tpu_custom_call" | custom-call | flops 3221225472 | bytes 12582912 | tf_op jit(solution)/shard_map/query_heads/pallas_call | solution.py:314
  299.0 41.8 %attend.1 = (bf16[256,2048]{1,0:T(8,128)(2,1)}, f32[16,8,256]{2,1,0:T(8,128)}, bf16[2048,4096]{1,0:T(8,128)(2,1)}) custom-call(bf16[2048,640]{1,0:T(8,128)(2,1)} %place_rows.5.l_ref, bf16[16,4,32,1024]{3,2,1,0:T(8,128)(2,1)} %bitcast.202, bf16[128,4096]{1,0:T(8,128)(2,1)} %pad.98.refs_10_.u_ref, bf16[16,256,256]{2,1,0:T(8,128)(2,1)} %query_heads.1.q_ref), custom_call_target="tpu_custom_call" | custom-call | flops 19327352832 | bytes 8000000 | tf_op jit(solution)/shard_map/attend/pallas_call | solution.py:418
  360.8 24.9 %routed.4 = (bf16[2,128,2048]{2,1,0:T(8,128)(2,1)}, bf16[2,128,2048]{2,1,0:T(8,128)(2,1)}, bf16[2,128,128]{2,1,0:T(8,128)(2,1)}) custom-call(s32[9]{0:T(128)} %get-tuple-element.261.info, s32[8,2,256]{2,1,0:T(2,128)} %copy_select_fusion.slot_ref, bf16[2048,128]{1,0:T(8,128)(2,1)} %pad.87.refs_4_.wr_ref, bf16[2,2048,2816]{2,1,0:T(8,128)(2,1)} %w_in.7, ...), custom_call_target="tpu_custom_call" | custom-call | flops 8858370048 | bytes 34603008 | tf_op jit(solution)/shard_map/routed/pallas_call | solution.py:619
  385.7 11.9 %collective-permute-done.32.refs_0_ = bf16[256,2048]{1,0:T(8,128)(2,1)} collective-permute-done((bf16[256,2048]{1,0:T(8,128)(2,1)}, bf16[256,2048]{1,0:T(8,128)(2,1)}, u32[]{:S(2)}, u32[]{:S(2)}) %collective-permute-start.32) | collective-permute-done | bytes 1048608 | tf_op jit(solution)/shard_map/ppermute | solution.py:101
  405.8 11.3 %shared.4 = (bf16[1,256,2048]{2,1,0:T(8,128)(2,1)}, bf16[1,256,2048]{2,1,0:T(8,128)(2,1)}, f32[128,768]{1,0:T(8,128)}, f32[128,2048]{1,0:T(8,128)}, f32[128,2048]{1,0:T(8,128)}, /*index=5*/f32[128,384]{1,0:T(8,128)}) custom-call(s32[9]{0:T(128)} %get-tuple-element.261.info, s32[8,2,256]{2,1,0:T(2,128)} %copy_select_fusion.slot_ref, ...), custom_call_target="tpu_custom_call" | custom-call | flops 4000000000 | bytes 8000000 | tf_op jit(solution)/shard_map/shared/pallas_call | solution.py:725
  426.5 30.2 %routed.5 = (bf16[2,256,2048]{2,1,0:T(8,128)(2,1)}, bf16[2,256,2048]{2,1,0:T(8,128)(2,1)}, bf16[2,256,128]{2,1,0:T(8,128)(2,1)}) custom-call(s32[9]{0:T(128)} %get-tuple-element.261.info, s32[8,2,256]{2,1,0:T(2,128)} %copy_select_fusion.slot_ref, bf16[2048,128]{1,0:T(8,128)(2,1)} %pad.87.refs_4_.wr_ref, bf16[2,2048,2816]{2,1,0:T(8,128)(2,1)} %w_in.7, ...), custom_call_target="tpu_custom_call" | custom-call | flops 17716740096 | bytes 34603008 | tf_op jit(solution)/shard_map/routed/pallas_call | solution.py:619
  464.2 18.7 %shared.5 = (bf16[2,256,2048]{2,1,0:T(8,128)(2,1)}, bf16[2,256,2048]{2,1,0:T(8,128)(2,1)}, f32[128,768]{1,0:T(8,128)}, f32[128,2048]{1,0:T(8,128)}, f32[128,2048]{1,0:T(8,128)}, /*index=5*/f32[128,384]{1,0:T(8,128)}) custom-call(s32[9]{0:T(128)} %get-tuple-element.261.info, s32[8,2,256]{2,1,0:T(2,128)} %copy_select_fusion.slot_ref, ...), custom_call_target="tpu_custom_call" | custom-call | flops 8000000000 | bytes 16000000 | tf_op jit(solution)/shard_map/shared/pallas_call | solution.py:725
  484.2 30.4 %routed.6 = (bf16[2,256,2048]{2,1,0:T(8,128)(2,1)}, bf16[2,256,2048]{2,1,0:T(8,128)(2,1)}, bf16[2,256,128]{2,1,0:T(8,128)(2,1)}) custom-call(s32[9]{0:T(128)} %get-tuple-element.261.info, s32[8,2,256]{2,1,0:T(2,128)} %copy_select_fusion.slot_ref, bf16[2048,128]{1,0:T(8,128)(2,1)} %pad.87.refs_4_.wr_ref, bf16[2,2048,2816]{2,1,0:T(8,128)(2,1)} %w_in.7, ...), custom_call_target="tpu_custom_call" | custom-call | flops 17716740096 | bytes 34603008 | tf_op jit(solution)/shard_map/routed/pallas_call | solution.py:619
  518.9 19.1 %shared.6 = (bf16[2,256,2048]{2,1,0:T(8,128)(2,1)}, bf16[2,256,2048]{2,1,0:T(8,128)(2,1)}, f32[128,768]{1,0:T(8,128)}, f32[128,2048]{1,0:T(8,128)}, f32[128,2048]{1,0:T(8,128)}, /*index=5*/f32[128,384]{1,0:T(8,128)}) custom-call(s32[9]{0:T(128)} %get-tuple-element.261.info, s32[8,2,256]{2,1,0:T(2,128)} %copy_select_fusion.slot_ref, ...), custom_call_target="tpu_custom_call" | custom-call | flops 8000000000 | bytes 16000000 | tf_op jit(solution)/shard_map/shared/pallas_call | solution.py:725
  540.2 41.8 %routed.7 = (bf16[2,384,2048]{2,1,0:T(8,128)(2,1)}, bf16[2,384,2048]{2,1,0:T(8,128)(2,1)}, bf16[2,384,128]{2,1,0:T(8,128)(2,1)}) custom-call(s32[9]{0:T(128)} %get-tuple-element.261.info, s32[8,2,256]{2,1,0:T(2,128)} %copy_select_fusion.slot_ref, bf16[2048,128]{1,0:T(8,128)(2,1)} %pad.87.refs_4_.wr_ref, bf16[2,2048,2816]{2,1,0:T(8,128)(2,1)} %w_in.7, ...), custom_call_target="tpu_custom_call" | custom-call | flops 26575110144 | bytes 34603008 | tf_op jit(solution)/shard_map/routed/pallas_call | solution.py:619
  582.1 25.5 %shared.7 = (bf16[3,256,2048]{2,1,0:T(8,128)(2,1)}, bf16[3,256,2048]{2,1,0:T(8,128)(2,1)}, f32[128,768]{1,0:T(8,128)}, f32[128,2048]{1,0:T(8,128)}, f32[128,2048]{1,0:T(8,128)}, /*index=5*/f32[128,384]{1,0:T(8,128)}) custom-call(s32[9]{0:T(128)} %get-tuple-element.261.info, s32[8,2,256]{2,1,0:T(2,128)} %copy_select_fusion.slot_ref, ...), custom_call_target="tpu_custom_call" | custom-call | flops 12000000000 | bytes 24000000 | tf_op jit(solution)/shard_map/shared/pallas_call | solution.py:725
  638.4 15.7 %all-to-all-done.3 = bf16[8,16,1664]{2,1,0:T(8,128)(2,1)S(1)} async-done(((bf16[8,16,1664]{2,1,0:T(8,128)(2,1)}), bf16[8,16,1664]{2,1,0:T(8,128)(2,1)S(1)}, u32[]{:S(2)}, u32[]{:S(2)}) %all-to-all-start.3) | async-done | bytes 426016 | tf_op jit(solution)/shard_map/all_to_all | solution.py:795
  681.8 18.2 %all-to-all-done.6 = bf16[8,1,16,1664]{3,2,1,0:T(8,128)(2,1)S(1)} async-done(((bf16[8,1,16,1664]{3,2,1,0:T(8,128)(2,1)}), bf16[8,1,16,1664]{3,2,1,0:T(8,128)(2,1)S(1)}, u32[]{:S(2)}, u32[]{:S(2)}) %all-to-all-start.6) | async-done | bytes 426016 | tf_op jit(solution)/shard_map/all_to_all | solution.py:807
  706.6 20.8 %collective-permute-done.48 = bf16[256,2048]{1,0:T(8,128)(2,1)S(1)} collective-permute-done((bf16[256,2048]{1,0:T(8,128)(2,1)S(1)}, bf16[256,2048]{1,0:T(8,128)(2,1)S(1)}, u32[]{:S(2)}, u32[]{:S(2)}) %collective-permute-start.48) | collective-permute-done | bytes 1048608 | tf_op jit(solution)/shard_map/ppermute | solution.py:101
  754.4 27.7 %attend_back.2 = (bf16[8,256,256]{2,1,0:T(8,128)(2,1)}, bf16[2048,640]{1,0:T(8,128)(2,1)}, f32[128,2048]{1,0:T(8,128)}) custom-call(bf16[2048,640]{1,0:T(8,128)(2,1)} %place_rows.5.l_ref, bf16[128,2048]{1,0:T(8,128)(2,1)} %bitcast.220, bf16[16,4,32,1024]{3,2,1,0:T(8,128)(2,1)} %bitcast.203, bf16[128,4096]{1,0:T(8,128)(2,1)} %pad.98.refs_10_.u_ref, ...), custom_call_target="tpu_custom_call" | custom-call | flops 13958643712 | bytes 30000000 | tf_op jit(solution)/shard_map/attend_back/pallas_call | solution.py:502
  783.4 28.5 %attend_back.3 = (bf16[8,256,256]{2,1,0:T(8,128)(2,1)}, bf16[2048,640]{1,0:T(8,128)(2,1)}, f32[128,2048]{1,0:T(8,128)}) custom-call(bf16[2048,640]{1,0:T(8,128)(2,1)} %place_rows.5.l_ref, bf16[128,2048]{1,0:T(8,128)(2,1)} %bitcast.221, bf16[16,4,32,1024]{3,2,1,0:T(8,128)(2,1)} %bitcast.204, bf16[128,4096]{1,0:T(8,128)(2,1)} %pad.98.refs_10_.u_ref, ...), custom_call_target="tpu_custom_call" | custom-call | flops 13958643712 | bytes 30000000 | tf_op jit(solution)/shard_map/attend_back/pallas_call | solution.py:502
  826.0 13.9 %query_back.1 = (f32[256,2048]{1,0:T(8,128)}, f32[256,128]{1,0:T(8,128)}, f32[128,3072]{1,0:T(8,128)}) custom-call(s32[9]{0:T(128)} %get-tuple-element.262.info, bf16[16,256,256]{2,1,0:T(8,128)(2,1)} %pad_maximum_fusion.1.dq_ref, bf16[128,3072]{1,0:T(8,128)(2,1)} %pad.97.refs_9_.up_ref, bf16[128,256]{1,0:T(8,128)(2,1)} %pad_bitcast_fusion.rt_ref, ...), custom_call_target="tpu_custom_call" | custom-call | flops 3221225472 | bytes 12582912 | tf_op jit(solution)/shard_map/query_back/pallas_call | solution.py:371
  839.9 8.9 collective-permute-done.61.refs_1_
  899.4 9.3 all-to-all-done.4
  926.4 7.3 all-to-all-done.5
  (578 shorter events, 360.6 us)
Async XLA Ops:
  7.7 42.0 %collective-permute-start.1 = (bf16[128,6784]{1,0:T(8,128)(2,1)}, bf16[128,6784]{1,0:T(8,128)(2,1)}, u32[]{:S(2)}, u32[]{:S(2)}) collective-permute-start(bf16[128,6784]{1,0:T(8,128)(2,1)} %pack_weights.1.refs_0_.rest_0_), channel_id=1, source_target_pairs={{0,2},{2,4},{4,6},{6,7},{7,5},{5,3},{3,1},{1,0},{8,10},{10,12},{12... | collective-permute-start | bytes 5210120 | tf_op jit(solution)/shard_map/ppermute | solution.py:101
  10.7 41.1 %collective-permute-start.2 = (bf16[128,6784]{1,0:T(8,128)(2,1)}, bf16[128,6784]{1,0:T(8,128)(2,1)}, u32[]{:S(2)}, u32[]{:S(2)}) collective-permute-start(bf16[128,6784]{1,0:T(8,128)(2,1)} %pack_weights.1.refs_0_.rest_0_), channel_id=1, source_target_pairs={{0,1},{2,0},{4,2},{6,4},{7,6},{5,7},{3,5},{1,3},{8,9},{10,8},{12,1... | collective-permute-start | bytes 5210120 | tf_op jit(solution)/shard_map/ppermute | solution.py:104
  10.7 41.7 %collective-permute-start = (bf16[128,6784]{1,0:T(8,128)(2,1)}, bf16[128,6784]{1,0:T(8,128)(2,1)}, u32[]{:S(2)}, u32[]{:S(2)}) collective-permute-start(bf16[128,6784]{1,0:T(8,128)(2,1)} %pack_weights.1.refs_0_.rest_0_), channel_id=1, source_target_pairs={{0,8},{8,0},{16,24},{24,16},{1,9},{9,1},{17,25},{25,17},{2,10},{10... | collective-permute-start | bytes 5210120 | tf_op jit(solution)/shard_map/ppermute | solution.py:163
  12.2 59.7 %all-to-all-start = ((bf16[8,16,3456]{2,1,0:T(8,128)(2,1)}), bf16[8,16,3456]{2,1,0:T(8,128)(2,1)}, u32[]{:S(2)}, u32[]{:S(2)}) async-start(bf16[8,16,3456]{2,1,0:T(8,128)(2,1)} %copy.237), calls=%async_computation | async-start | bytes 1769472 | tf_op jit(solution)/shard_map/all_to_all | solution.py:861
  52.4 43.6 %collective-permute-start.3 = (bf16[128,6784]{1,0:T(8,128)(2,1)}, bf16[128,6784]{1,0:T(8,128)(2,1)}, u32[]{:S(2)}, u32[]{:S(2)}) collective-permute-start(bf16[128,6784]{1,0:T(8,128)(2,1)} %get-tuple-element.107.refs_2_.rest_2_), channel_id=1, source_target_pairs={{0,8},{8,0},{16,24},{24,16},{1,9},{9,1},{17,25},{25,17},{2,10},{10... | collective-permute-start | bytes 5210120 | tf_op jit(solution)/shard_map/ppermute | solution.py:163
  52.5 43.5 %collective-permute-start.4 = (bf16[128,6784]{1,0:T(8,128)(2,1)}, bf16[128,6784]{1,0:T(8,128)(2,1)}, u32[]{:S(2)}, u32[]{:S(2)}) collective-permute-start(bf16[128,6784]{1,0:T(8,128)(2,1)} %get-tuple-element.108.refs_4_.rest_4_), channel_id=1, source_target_pairs={{0,8},{8,0},{16,24},{24,16},{1,9},{9,1},{17,25},{25,17},{2,10},{10... | collective-permute-start | bytes 5210120 | tf_op jit(solution)/shard_map/ppermute | solution.py:163
  53.0 47.8 %collective-permute-start.5 = (bf16[128,6784]{1,0:T(8,128)(2,1)}, bf16[128,6784]{1,0:T(8,128)(2,1)}, u32[]{:S(2)}, u32[]{:S(2)}) collective-permute-start(bf16[128,6784]{1,0:T(8,128)(2,1)} %get-tuple-element.107.refs_2_.rest_2_), channel_id=1, source_target_pairs={{0,2},{2,4},{4,6},{6,7},{7,5},{5,3},{3,1},{1,0},{8,10},{10,12},{12... | collective-permute-start | bytes 5210120 | tf_op jit(solution)/shard_map/ppermute | solution.py:101
  54.6 47.5 %collective-permute-start.6 = (bf16[128,6784]{1,0:T(8,128)(2,1)}, bf16[128,6784]{1,0:T(8,128)(2,1)}, u32[]{:S(2)}, u32[]{:S(2)}) collective-permute-start(bf16[128,6784]{1,0:T(8,128)(2,1)} %get-tuple-element.108.refs_4_.rest_4_), channel_id=1, source_target_pairs={{0,1},{2,0},{4,2},{6,4},{7,6},{5,7},{3,5},{1,3},{8,9},{10,8},{12,1... | collective-permute-start | bytes 5210120 | tf_op jit(solution)/shard_map/ppermute | solution.py:104
  73.7 54.3 %all-to-all-start.1 = ((bf16[8,16,3456]{2,1,0:T(8,128)(2,1)}), bf16[8,16,3456]{2,1,0:T(8,128)(2,1)}, u32[]{:S(2)}, u32[]{:S(2)}) async-start(bf16[8,16,3456]{2,1,0:T(8,128)(2,1)} %broadcast_in_dim.110), calls=%async_computation.1 | async-start | bytes 1769472 | tf_op jit(solution)/shard_map/all_to_all | solution.py:864
  102.1 52.1 %collective-permute-start.10 = (bf16[128,6784]{1,0:T(8,128)(2,1)}, bf16[128,6784]{1,0:T(8,128)(2,1)S(1)}, u32[]{:S(2)}, u32[]{:S(2)}) collective-permute-start(bf16[128,6784]{1,0:T(8,128)(2,1)} %get-tuple-element.110.refs_8_.rest_8_), channel_id=1, source_target_pairs={{0,1},{2,0},{4,2},{6,4},{7,6},{5,7},{3,5},{1,3},{8,9},{10,8},{12,1... | collective-permute-start | bytes 5210120 | tf_op jit(solution)/shard_map/ppermute | solution.py:104
  102.8 51.4 %collective-permute-start.8 = (bf16[128,6784]{1,0:T(8,128)(2,1)}, bf16[128,6784]{1,0:T(8,128)(2,1)}, u32[]{:S(2)}, u32[]{:S(2)}) collective-permute-start(bf16[128,6784]{1,0:T(8,128)(2,1)} %get-tuple-element.110.refs_8_.rest_8_), channel_id=1, source_target_pairs={{0,8},{8,0},{16,24},{24,16},{1,9},{9,1},{17,25},{25,17},{2,10},{10... | collective-permute-start | bytes 5210120 | tf_op jit(solution)/shard_map/ppermute | solution.py:163
  102.8 51.4 %collective-permute-start.7 = (bf16[128,6784]{1,0:T(8,128)(2,1)}, bf16[128,6784]{1,0:T(8,128)(2,1)}, u32[]{:S(2)}, u32[]{:S(2)}) collective-permute-start(bf16[128,6784]{1,0:T(8,128)(2,1)} %get-tuple-element.109.refs_6_.rest_6_), channel_id=1, source_target_pairs={{0,8},{8,0},{16,24},{24,16},{1,9},{9,1},{17,25},{25,17},{2,10},{10... | collective-permute-start | bytes 5210120 | tf_op jit(solution)/shard_map/ppermute | solution.py:163
  103.3 54.6 %collective-permute-start.9 = (bf16[128,6784]{1,0:T(8,128)(2,1)}, bf16[128,6784]{1,0:T(8,128)(2,1)}, u32[]{:S(2)}, u32[]{:S(2)}) collective-permute-start(bf16[128,6784]{1,0:T(8,128)(2,1)} %get-tuple-element.109.refs_6_.rest_6_), channel_id=1, source_target_pairs={{0,2},{2,4},{4,6},{6,7},{7,5},{5,3},{3,1},{1,0},{8,10},{10,12},{12... | collective-permute-start | bytes 5210120 | tf_op jit(solution)/shard_map/ppermute | solution.py:101
  190.0 51.9 %all-to-all-start.2 = ((bf16[8,128,768]{2,1,0:T(8,128)(2,1)}), bf16[8,128,768]{2,1,0:T(8,128)(2,1)}, u32[]{:S(2)}, u32[]{:S(2)}) async-start(bf16[8,128,768]{2,1,0:T(8,128)(2,1)} %reshape.261.refs_4_), calls=%async_computation.2 | async-start | bytes 3145728 | tf_op jit(solution)/shard_map/all_to_all | solution.py:889
  241.9 159.4 %collective-permute-start.25 = (bf16[8,128,768]{2,1,0:T(8,128)(2,1)}, bf16[8,128,768]{2,1,0:T(8,128)(2,1)}, u32[]{:S(2)}, u32[]{:S(2)}) collective-permute-start(bf16[8,128,768]{2,1,0:T(8,128)(2,1)} %all-to-all-done.2), channel_id=1, source_target_pairs={{0,8},{8,0},{16,24},{24,16},{1,9},{9,1},{17,25},{25,17},{2,10},{10... | collective-permute-start | bytes 4718600 | tf_op jit(solution)/shard_map/ppermute | solution.py:163
  291.2 66.9 %collective-permute-start.28 = (bf16[256,2048]{1,0:T(8,128)(2,1)}, bf16[256,2048]{1,0:T(8,128)(2,1)}, u32[]{:S(2)}, u32[]{:S(2)}) collective-permute-start(bf16[256,2048]{1,0:T(8,128)(2,1)} %gate.34), channel_id=1, source_target_pairs={{0,2},{2,4},{4,6},{6,7},{7,5},{5,3},{3,1},{1,0},{8,10},{10,12},{12... | collective-permute-start | bytes 3145736 | tf_op jit(solution)/shard_map/ppermute | solution.py:101
  292.2 65.9 %collective-permute-start.29 = (bf16[256,2048]{1,0:T(8,128)(2,1)}, bf16[256,2048]{1,0:T(8,128)(2,1)}, u32[]{:S(2)}, u32[]{:S(2)}) collective-permute-start(bf16[256,2048]{1,0:T(8,128)(2,1)} %gate.34), channel_id=1, source_target_pairs={{0,1},{2,0},{4,2},{6,4},{7,6},{5,7},{3,5},{1,3},{8,9},{10,8},{12,1... | collective-permute-start | bytes 3145736 | tf_op jit(solution)/shard_map/ppermute | solution.py:104
  352.9 32.7 %collective-permute-start.26 = (bf16[256,2048]{1,0:T(8,128)(2,1)}, bf16[256,2048]{1,0:T(8,128)(2,1)}, u32[]{:S(2)}, u32[]{:S(2)}) collective-permute-start(bf16[256,2048]{1,0:T(8,128)(2,1)} %multiply_convert_fusion.rest_0_), channel_id=1, source_target_pairs={{0,2},{2,4},{4,6},{6,7},{7,5},{5,3},{3,1},{1,0},{8,10},{10,12},{12... | collective-permute-start | bytes 3145736 | tf_op jit(solution)/shard_map/ppermute | solution.py:101
  354.0 31.7 %collective-permute-start.27 = (bf16[256,2048]{1,0:T(8,128)(2,1)}, bf16[256,2048]{1,0:T(8,128)(2,1)}, u32[]{:S(2)}, u32[]{:S(2)}) collective-permute-start(bf16[256,2048]{1,0:T(8,128)(2,1)} %multiply_convert_fusion.rest_0_), channel_id=1, source_target_pairs={{0,1},{2,0},{4,2},{6,4},{7,6},{5,7},{3,5},{1,3},{8,9},{10,8},{12,1... | collective-permute-start | bytes 3145736 | tf_op jit(solution)/shard_map/ppermute | solution.py:104
  358.1 39.5 %collective-permute-start.32 = (bf16[256,2048]{1,0:T(8,128)(2,1)}, bf16[256,2048]{1,0:T(8,128)(2,1)}, u32[]{:S(2)}, u32[]{:S(2)}) collective-permute-start(bf16[256,2048]{1,0:T(8,128)(2,1)} %get-tuple-element.129.rest_2_), channel_id=1, source_target_pairs={{0,2},{2,4},{4,6},{6,7},{7,5},{5,3},{3,1},{1,0},{8,10},{10,12},{12... | collective-permute-start | bytes 3145736 | tf_op jit(solution)/shard_map/ppermute | solution.py:101
  359.1 40.2 %collective-permute-start.33 = (bf16[256,2048]{1,0:T(8,128)(2,1)}, bf16[256,2048]{1,0:T(8,128)(2,1)}, u32[]{:S(2)}, u32[]{:S(2)}) collective-permute-start(bf16[256,2048]{1,0:T(8,128)(2,1)} %get-tuple-element.130.rest_3_), channel_id=1, source_target_pairs={{0,1},{2,0},{4,2},{6,4},{7,6},{5,7},{3,5},{1,3},{8,9},{10,8},{12,1... | collective-permute-start | bytes 3145736 | tf_op jit(solution)/shard_map/ppermute | solution.py:104
  417.0 41.7 %collective-permute-start.38 = (bf16[256,2048]{1,0:T(8,128)(2,1)}, bf16[256,2048]{1,0:T(8,128)(2,1)}, u32[]{:S(2)}, u32[]{:S(2)}) collective-permute-start(bf16[256,2048]{1,0:T(8,128)(2,1)} %get-tuple-element.140.rest_2_), channel_id=1, source_target_pairs={{0,2},{2,4},{4,6},{6,7},{7,5},{5,3},{3,1},{1,0},{8,10},{10,12},{12... | collective-permute-start | bytes 3145736 | tf_op jit(solution)/shard_map/ppermute | solution.py:101
  417.8 41.0 %collective-permute-start.39 = (bf16[256,2048]{1,0:T(8,128)(2,1)}, bf16[256,2048]{1,0:T(8,128)(2,1)}, u32[]{:S(2)}, u32[]{:S(2)}) collective-permute-start(bf16[256,2048]{1,0:T(8,128)(2,1)} %get-tuple-element.141.rest_3_), channel_id=1, source_target_pairs={{0,1},{2,0},{4,2},{6,4},{7,6},{5,7},{3,5},{1,3},{8,9},{10,8},{12,1... | collective-permute-start | bytes 3145736 | tf_op jit(solution)/shard_map/ppermute | solution.py:104
  664.3 35.7 %collective-permute-start.46 = (bf16[256,2048]{1,0:T(8,128)(2,1)}, bf16[256,2048]{1,0:T(8,128)(2,1)}, u32[]{:S(2)}, u32[]{:S(2)}) collective-permute-start(bf16[256,2048]{1,0:T(8,128)(2,1)} %get-tuple-element.233), channel_id=1, source_target_pairs={{0,2},{2,4},{4,6},{6,7},{7,5},{5,3},{3,1},{1,0},{8,10},{10,12},{12... | collective-permute-start | bytes 3145736 | tf_op jit(solution)/shard_map/ppermute | solution.py:101
  664.5 35.5 %collective-permute-start.47 = (bf16[256,2048]{1,0:T(8,128)(2,1)}, bf16[256,2048]{1,0:T(8,128)(2,1)}, u32[]{:S(2)}, u32[]{:S(2)}) collective-permute-start(bf16[256,2048]{1,0:T(8,128)(2,1)} %get-tuple-element.232), channel_id=1, source_target_pairs={{0,1},{2,0},{4,2},{6,4},{7,6},{5,7},{3,5},{1,3},{8,9},{10,8},{12,1... | collective-permute-start | bytes 3145736 | tf_op jit(solution)/shard_map/ppermute | solution.py:104
  667.6 32.4 %all-to-all-start.6 = ((bf16[8,1,16,1664]{3,2,1,0:T(8,128)(2,1)}), bf16[8,1,16,1664]{3,2,1,0:T(8,128)(2,1)S(1)}, u32[]{:S(2)}, u32[]{:S(2)}) async-start(bf16[8,1,16,1664]{3,2,1,0:T(8,128)(2,1)} %bitcast.156.refs_2_), calls=%async_computation.6 | async-start | bytes 851968 | tf_op jit(solution)/shard_map/all_to_all | solution.py:807
  750.0 32.0 %collective-permute-start.52 = (bf16[256,2048]{1,0:T(8,128)(2,1)}, bf16[256,2048]{1,0:T(8,128)(2,1)S(1)}, u32[]{:S(2)}, u32[]{:S(2)}) collective-permute-start(bf16[256,2048]{1,0:T(8,128)(2,1)} %pad_maximum_fusion.5), channel_id=1, source_target_pairs={{0,2},{2,4},{4,6},{6,7},{7,5},{5,3},{3,1},{1,0},{8,10},{10,12},{12... | collective-permute-start | bytes 3145736 | tf_op jit(solution)/shard_map/ppermute | solution.py:101
  751.6 31.1 %collective-permute-start.53 = (bf16[256,2048]{1,0:T(8,128)(2,1)}, bf16[256,2048]{1,0:T(8,128)(2,1)S(1)}, u32[]{:S(2)}, u32[]{:S(2)}) collective-permute-start(bf16[256,2048]{1,0:T(8,128)(2,1)} %pad_maximum_fusion.6), channel_id=1, source_target_pairs={{0,1},{2,0},{4,2},{6,4},{7,6},{5,7},{3,5},{1,3},{8,9},{10,8},{12,1... | collective-permute-start | bytes 3145736 | tf_op jit(solution)/shard_map/ppermute | solution.py:104
  819.2 45.7 %collective-permute-start.54 = (bf16[256,2048]{1,0:T(8,128)(2,1)}, bf16[256,2048]{1,0:T(8,128)(2,1)}, u32[]{:S(2)}, u32[]{:S(2)}) collective-permute-start(bf16[256,2048]{1,0:T(8,128)(2,1)} %get-tuple-element.229), channel_id=1, source_target_pairs={{0,2},{2,4},{4,6},{6,7},{7,5},{5,3},{3,1},{1,0},{8,10},{10,12},{12... | collective-permute-start | bytes 3145736 | tf_op jit(solution)/shard_map/ppermute | solution.py:101
  819.7 45.2 %collective-permute-start.55 = (bf16[256,2048]{1,0:T(8,128)(2,1)}, bf16[256,2048]{1,0:T(8,128)(2,1)}, u32[]{:S(2)}, u32[]{:S(2)}) collective-permute-start(bf16[256,2048]{1,0:T(8,128)(2,1)} %get-tuple-element.228), channel_id=1, source_target_pairs={{0,1},{2,0},{4,2},{6,4},{7,6},{5,7},{3,5},{1,3},{8,9},{10,8},{12,1... | collective-permute-start | bytes 3145736 | tf_op jit(solution)/shard_map/ppermute | solution.py:104
  876.6 46.5 %collective-permute-start.56 = (bf16[256,2048]{1,0:T(8,128)(2,1)}, bf16[256,2048]{1,0:T(8,128)(2,1)}, u32[]{:S(2)}, u32[]{:S(2)}) collective-permute-start(bf16[256,2048]{1,0:T(8,128)(2,1)} %get-tuple-element.226), channel_id=1, source_target_pairs={{0,2},{2,4},{4,6},{6,7},{7,5},{5,3},{3,1},{1,0},{8,10},{10,12},{12... | collective-permute-start | bytes 3145736 | tf_op jit(solution)/shard_map/ppermute | solution.py:101
  877.1 46.0 %collective-permute-start.57 = (bf16[256,2048]{1,0:T(8,128)(2,1)}, bf16[256,2048]{1,0:T(8,128)(2,1)}, u32[]{:S(2)}, u32[]{:S(2)}) collective-permute-start(bf16[256,2048]{1,0:T(8,128)(2,1)} %get-tuple-element.227), channel_id=1, source_target_pairs={{0,1},{2,0},{4,2},{6,4},{7,6},{5,7},{3,5},{1,3},{8,9},{10,8},{12,1... | collective-permute-start | bytes 3145736 | tf_op jit(solution)/shard_map/ppermute | solution.py:104
  (151 other events, 2259.1 us)
where the time goes:
time: 948 us; the launch traced here: 937 us
  Pallas kernels  352 us (37%)
  waiting for transfers between devices  236 us (25%)
  starting transfers between devices  121 us (13%)
  local copies, waits for them, and re-layouts  81.8 us (9%)
  other arithmetic  81.6 us (9%)
  matrix products  32.9 us (3%)
  blocking collectives  16.9 us (2%)
  between operations  14.2 us (1%)
    pallas_call x4, Pallas kernels, routed(): pl.pallas_call(functools.partial(routed_kernel, offs=offs, slots=slots, w...  127 us
    ppermute x28, waiting for transfers between devices, send_right(): return lax.ppermute(v, 'shard', self.right)  119 us
    pallas_call x4, Pallas kernels, shared(): pl.pallas_call(functools.partial(shared_kernel, offs=offs, slots=slots, e...  74.7 us
    pallas_call x2, Pallas kernels, attend_back(): pl.pallas_call(attend_back_kernel, grid=(heads,), in_specs=[still(l_all),...  56.2 us
    ppermute x28, starting transfers between devices, send_right(): return lax.ppermute(v, 'shard', self.right)  54.9 us
    ppermute x28, waiting for transfers between devices, send_left(): return lax.ppermute(v, 'shard', self.left)  50.9 us
    pallas_call x1, Pallas kernels, attend(): pl.pallas_call(attend_kernel, grid=(HEADS,), in_specs=[pl.BlockSpec((leng...  41.8 us
    ppermute x28, starting transfers between devices, send_left(): return lax.ppermute(v, 'shard', self.left)  33.5 us
  transfers between devices with their start and end apart: 73, of which 31 were waited for; matrix products, arithmetic and copies ran while one was open for 16% of the time, Pallas kernels for 24%

commit v1 on v0

--- a/solution.py
+++ b/solution.py
@@ -195,6 +195,39 @@
     )(info, *blocks)
 
 
+def latents_kernel(info, *refs, places):
+    blocks, out = refs[:-1], refs[-1]
+    count = info.shape[0] - 1
+    for (off, n, row, _, _), block in zip(places, blocks):
+        rows = block.shape[0]
+        at = pl.ds(pl.multiple_of(info[off % count] * n + row, 16), rows)
+        hide = jnp.where(info[off % count] > info[0], -1e30, 0.0)
+        lane = lax.broadcasted_iota(jnp.int32, (rows, LANES), 1)
+        tail = jnp.where(lane == LANES - 1, hide, block[:, LATENT:].astype(f32))
+        out[at, :LATENT] = block[:, :LATENT]
+        out[at, LATENT:] = tail.astype(bf16)
+
+
+def all_latents(info, blocks, n):
+    places = [(off, n, row, 0, False) for off, row, _ in blocks]
+    blocks = [v for _, _, v in blocks]
+    height = (info.shape[0] - 1) * n
+    spec = pltpu.PrefetchScalarGridSpec(
+        num_scalar_prefetch=1,
+        grid=(1,),
+        in_specs=[pl.BlockSpec(b.shape, lambda i, s: (0, 0)) for b in blocks],
+        out_specs=pl.BlockSpec((height, LW), lambda i, s: (0, 0)),
+    )
+    return pl.pallas_call(
+        functools.partial(latents_kernel, places=places),
+        grid_spec=spec,
+        out_shape=jax.ShapeDtypeStruct((height, LW), bf16),
+        compiler_params=params(1),
+        cost_estimate=cost(0, height * LW * 4),
+        name="all_latents",
+    )(info, *blocks)
+
+
 def whole_rows(info, blocks, n):
     places = [(off, n, row, 0, False) for off, row, _ in blocks]
     return place_rows(info, places, [v for _, _, v in blocks], (info.shape[0] - 1) * n)
@@ -385,29 +418,36 @@
 LOG2E = math.log2(math.e)
 
 
+PER_STEP = 2
+
+
 def attend_kernel(l_ref, w_ref, u_ref, q_ref, mix_ref, lse_ref, kv_ref):
-    w = w_ref[...].reshape(LATENT, NOPE + VDIM)
-    kv = dot(l_ref[:, :LATENT], w) + dot(l_ref[:, LATENT:], u_ref[...])
-    kv = kv.astype(bf16)
-    kv_ref[...] = kv
-    keys = jnp.concatenate([kv[:, :NOPE], l_ref[:, LATENT:]], 1)
-    values = jnp.concatenate([kv[:, NOPE:], jnp.ones((kv.shape[0], LANES), bf16)], 1)
-    scores = dot(q_ref[0], keys, NT)
-    top = jnp.max(scores, axis=1, keepdims=True)
-    weights = jnp.exp2((scores - top) * (SCALE * LOG2E)).astype(bf16)
-    both = dot(weights, values)
-    total = both[:, VDIM:]
-    mix_ref[...] = (both[:, :VDIM] / total).astype(bf16)
-    lse = top * (SCALE * LOG2E) + jnp.log2(total)
-    lse_ref[0] = lse.T[:8]
+    wide = NOPE + VDIM
+    w = w_ref[...].reshape(LATENT, PER_STEP * wide)
+    both_kv = dot(l_ref[:, :LATENT], w) + dot(l_ref[:, LATENT:], u_ref[...])
+    both_kv = both_kv.astype(bf16)
+    kv_ref[...] = both_kv
+    ones = jnp.ones((both_kv.shape[0], LANES), bf16)
+    for i in range(PER_STEP):
+        kv = both_kv[:, i * wide : (i + 1) * wide]
+        keys = jnp.concatenate([kv[:, :NOPE], l_ref[:, LATENT:]], 1)
+        values = jnp.concatenate([kv[:, NOPE:], ones], 1)
+        scores = dot(q_ref[i], keys, NT)
+        top = jnp.max(scores, axis=1, keepdims=True)
+        weights = jnp.exp2((scores - top) * (SCALE * LOG2E)).astype(bf16)
+        both = dot(weights, values)
+        total = both[:, VDIM:]
+        mix_ref[:, i * VDIM : (i + 1) * VDIM] = (both[:, :VDIM] / total).astype(bf16)
+        lse = top * (SCALE * LOG2E) + jnp.log2(total)
+        lse_ref[i] = lse.T[:8]
 
 
 def folded(w_kvb, at):
     pieces, _, rows, width = w_kvb.shape
-    wide = NOPE + VDIM
+    wide = PER_STEP * (NOPE + VDIM)
     per = width // wide
     return pl.BlockSpec(
-        (pieces, 1, rows, wide), lambda h: (0, (at + h) // per, 0, (at + h) % per)
+        (pieces, 1, rows, wide), lambda h, *s: (0, (at + h) // per, 0, (at + h) % per)
     )
 
 
@@ -415,20 +455,18 @@
     length = l_all.shape[0]
     tokens = q.shape[1]
     wide = NOPE + VDIM
+    column = lambda n, w: pl.BlockSpec((n, PER_STEP * w), lambda h: (0, h))
+    head = lambda *shape: pl.BlockSpec((PER_STEP,) + shape, lambda h: (h, 0, 0))
     return pl.pallas_call(
         attend_kernel,
-        grid=(HEADS,),
+        grid=(HEADS // PER_STEP,),
         in_specs=[
             pl.BlockSpec((length, LW), lambda h: (0, 0)),
             folded(w_kvb, 0),
-            pl.BlockSpec((LANES, wide), lambda h: (0, h)),
-            pl.BlockSpec((1, tokens, 2 * LANES), lambda h: (h, 0, 0)),
+            column(LANES, wide),
+            head(tokens, 2 * LANES),
         ],
-        out_specs=[
-            pl.BlockSpec((tokens, VDIM), lambda h: (0, h)),
-            pl.BlockSpec((1, 8, tokens), lambda h: (h, 0, 0)),
-            pl.BlockSpec((length, wide), lambda h: (0, h)),
-        ],
+        out_specs=[column(tokens, VDIM), head(8, tokens), column(length, wide)],
         out_shape=[
             jax.ShapeDtypeStruct((tokens, HEADS * VDIM), bf16),
             jax.ShapeDtypeStruct((HEADS, 8, tokens), f32),
@@ -441,6 +479,7 @@
 
 
 def attend_back_kernel(
+    info,
     l_ref,
     lt_ref,
     w_ref,
@@ -459,49 +498,63 @@
     acc,
 ):
     h = pl.program_id(0)
+    wide = NOPE + VDIM
+    count = info.shape[0] - 1
+    rows = acc.shape[0] // count
+    at = lambda k: pl.ds(pl.multiple_of(info[k] * rows, rows), rows)
 
     @pl.when(h == 0)
     def _():
-        if was_ref.shape == acc.shape:
-            acc[...] = was_ref[...].astype(f32)
+        if len(was_ref.shape) == 3:
+            for k in range(count):
+                acc[at(k), :] = was_ref[k].astype(f32)
         else:
             acc[...] = jnp.zeros_like(acc)
 
-    keys = jnp.concatenate([kv_ref[:, :NOPE], l_ref[:, LATENT:]], 1)
-    values = kv_ref[:, NOPE:]
-    scores = dot(keys, q_ref[0], NT)
-    probs = jnp.exp2(scores * (SCALE * LOG2E) - lse_ref[0, :1])
-    dvalues = dot(probs.astype(bf16), dm_ref[...])
-    dprobs = dot(values, dm_ref[...], NT)
-    dscores = (probs * (dprobs - delta_ref[0, :1])).astype(bf16)
-    dq = dot(dscores, keys, TN) * SCALE
-    lane = lax.broadcasted_iota(jnp.int32, (dq.shape[0], LANES), 1)
-    rope = dq[:, LANES:]
-    rope = rope * cos_ref[...] + unrotate_pair(lane, rope) * sin_ref[...]
-    dq_ref[0] = jnp.concatenate([dq[:, :LANES], rope], 1).astype(bf16)
-    dkeys = dot(dscores, q_ref[0]) * SCALE
-    dkv = jnp.concatenate([dkeys[:, :NOPE], dvalues], 1).astype(bf16)
-    acc[:, :LATENT] += dot(dkv, w_ref[...].reshape(LATENT, NOPE + VDIM), NT)
-    acc[:, LATENT:] += dot(dkv, u_ref[...], NT) + dkeys[:, NOPE:]
+    dkvs, drope = [], 0.0
+    for i in range(PER_STEP):
+        kv = kv_ref[:, i * wide : (i + 1) * wide]
+        keys = jnp.concatenate([kv[:, :NOPE], l_ref[:, LATENT:]], 1)
+        values = kv[:, NOPE:]
+        dm = dm_ref[:, i * VDIM : (i + 1) * VDIM]
+        scores = dot(keys, q_ref[i], NT)
+        probs = jnp.exp2(scores * (SCALE * LOG2E) - lse_ref[i, :1])
+        dvalues = dot(probs.astype(bf16), dm)
+        dprobs = dot(values, dm, NT)
+        dscores = (probs * (dprobs - delta_ref[i, :1])).astype(bf16)
+        dq = dot(dscores, keys, TN) * SCALE
+        lane = lax.broadcasted_iota(jnp.int32, (dq.shape[0], LANES), 1)
+        rope = dq[:, LANES:]
+        rope = rope * cos_ref[...] + unrotate_pair(lane, rope) * sin_ref[...]
+        dq_ref[i] = jnp.concatenate([dq[:, :LANES], rope], 1).astype(bf16)
+        dkeys = dot(dscores, q_ref[i]) * SCALE
+        dkvs += [dkeys[:, :NOPE].astype(bf16), dvalues.astype(bf16)]
+        drope += dkeys[:, NOPE:]
+    dkv = jnp.concatenate(dkvs, 1)
+    w = w_ref[...].reshape(LATENT, PER_STEP * wide)
+    acc[:, :LATENT] += dot(dkv, w, NT)
+    acc[:, LATENT:] += dot(dkv, u_ref[...], NT) + drope
     du_ref[...] = dot(lt_ref[...], dkv)
 
     @pl.when(h == pl.num_programs(0) - 1)
     def _():
-        dl_ref[...] = acc[...].astype(bf16)
-
-
-def attend_back(part, l_all, lt, w_kvb, u_kvb, kv, q, lse, delta, dmix, cos, sin, was):
+        for k in range(count):
+            dl_ref[k] = acc[at(k), :].astype(bf16)
+
+
+def attend_back(info, part, l_all, lt, w_kvb, u_kvb, kv, q, lse, delta, dmix, cos, sin, was):
     length = l_all.shape[0]
     tokens = q.shape[1]
     wide = NOPE + VDIM
     heads = HEADS // 2
-    at = part * heads
-    still = lambda a: pl.BlockSpec(a.shape, lambda h: (0, 0))
-    column = lambda n, w: pl.BlockSpec((n, w), lambda h: (0, at + h))
-    head = lambda *shape: pl.BlockSpec((1,) + shape, lambda h: (at + h, 0, 0))
-    return pl.pallas_call(
-        attend_back_kernel,
-        grid=(heads,),
+    count = info.shape[0] - 1
+    at = part * heads // PER_STEP
+    still = lambda a: pl.BlockSpec(a.shape, lambda h, s: (0,) * a.ndim)
+    column = lambda n, w: pl.BlockSpec((n, PER_STEP * w), lambda h, s: (0, at + h))
+    head = lambda *shape: pl.BlockSpec((PER_STEP,) + shape, lambda h, s: (at + h, 0, 0))
+    spec = pltpu.PrefetchScalarGridSpec(
+        num_scalar_prefetch=1,
+        grid=(heads // PER_STEP,),
         in_specs=[
             still(l_all),
             still(lt),
@@ -517,20 +570,24 @@
             still(was),
         ],
         out_specs=[
-            pl.BlockSpec((1, tokens, 2 * LANES), lambda h: (h, 0, 0)),
-            pl.BlockSpec((length, LW), lambda h: (0, 0)),
-            pl.BlockSpec((LANES, wide), lambda h: (0, h)),
+            pl.BlockSpec((PER_STEP, tokens, 2 * LANES), lambda h, s: (h, 0, 0)),
+            pl.BlockSpec((count, length // count, LW), lambda h, s: (0, 0, 0)),
+            pl.BlockSpec((LANES, PER_STEP * wide), lambda h, s: (0, h)),
         ],
+        scratch_shapes=[pltpu.VMEM((length, LW), f32)],
+    )
+    return pl.pallas_call(
+        attend_back_kernel,
+        grid_spec=spec,
         out_shape=[
             jax.ShapeDtypeStruct((heads, tokens, 2 * LANES), bf16),
-            jax.ShapeDtypeStruct((length, LW), bf16),
+            jax.ShapeDtypeStruct((count, length // count, LW), bf16),
             jax.ShapeDtypeStruct((LANES, heads * wide), f32),
         ],
-        scratch_shapes=[pltpu.VMEM((length, LW), f32)],
         compiler_params=params(1),
         cost_estimate=cost(heads * 2 * length * (LW * 256 + tokens * 1024), 30e6),
         name="attend_back",
-    )(l_all, lt, w_kvb, u_kvb, kv, q, lse, delta, dmix, cos, sin, was)
+    )(info, l_all, lt, w_kvb, u_kvb, kv, q, lse, delta, dmix, cos, sin, was)
 
 
 def picks(slot_row, slots):
@@ -873,9 +930,6 @@
     w1 = w_walk.hop()
     own_swap = w_swaps.swap(w_walk.own)
     w2 = w_walk.hop(*own_swap)
-    u_q = pad_rows(a_quq, LANES)
-    u_kvb = pad_rows(a_ku, LANES, ROPE)
-    wr = pad_lanes(w_router, LANES)
     width = w_shared_out.shape[0]
     half = round_up(width, LANES)
     rows_in = w_shared_in.shape[0]
@@ -886,33 +940,17 @@
     mine = jnp.pad(mine, ((0, 0), (0, 0), (0, 0), (0, half - width)))
     mine = mine.reshape(shards, mine.shape[1], 2 * half)
     ready = mine
-    mine = lax.all_to_all(mine, "shard", split_axis=0, concat_axis=0, tiled=True)
-    if replicas % 2 == 0:
-        other = pair_swap(mine, replicas)
-        w_si = jnp.concatenate(
-            [jnp.where(core == 0, mine, other), jnp.where(core == 0, other, mine)], 1
-        )
-    else:
-        w_si = mine
-    w_si = w_si.reshape(shards * rows_in, 2 * half)
-
-    w_i = jnp.concatenate([w_si, pad_lanes(jnp.concatenate([w_router, a_gd.T], 1), LANES)], 1)
-    w_o = jnp.concatenate([pad_rows(w_shared_out, half), pad_rows(a_nu, LANES)], 0)
-    gu_g = lax.dynamic_slice_in_dim(a_gu, place * width, width, 1)
-    gu_u = lax.dynamic_slice_in_dim(a_gu, shards * width + place * width, width, 1)
-    u_gu = jnp.concatenate([pad_lanes(gu_g, half), pad_lanes(gu_u, half)], 1)
-    u_gu = pad_rows(u_gu, LANES, experts)
-    nd_own = lax.dynamic_slice_in_dim(a_nd, place * width, width, 1)
-    dn_own = pad_rows(pad_lanes(nd_own.T, LANES), half)
-
     inputs = hidden_in.astype(f32)
     in_scale = rms_scale(inputs)
     hb = (inputs * in_scale * attn_gain).astype(bf16)
+    swap1 = w_swaps.swap(w_walk.pairs[0])
+    w3 = w_walk.hop(*swap1, ready, hb)
+    swap2 = w_swaps.swap(w_walk.pairs[1])
+    w4 = w_walk.hop(*swap2, ids)
+    u_q = pad_rows(a_quq, LANES)
+    u_kvb = pad_rows(a_ku, LANES, ROPE)
+    wr = pad_lanes(w_router, LANES)
     r_qa = dot(hb, a_qd, NT).astype(bf16)
-    swap1 = w_swaps.swap(w_walk.pairs[0])
-    w3 = w_walk.hop(*swap1, ready)
-    swap2 = w_swaps.swap(w_walk.pairs[1])
-    w4 = w_walk.hop(*swap2, wr, w_o, u_gu, dn_own, r_qa, u_q, u_kvb, ids)
     w_swaps.swap(w_walk.pairs[2])
     w_swaps.swap(w_walk.halves)
     w_at, w_blocks = w_swaps.rows(0, w_out.shape[0])
@@ -938,24 +976,41 @@
     l_own = pad_lanes(l_own, LW)
     l_walk = Walk(ring, l_own)
     l_walk.hop()
-    l_walk.hop()
-    l_walk.hop()
-    l4 = l_walk.hop()
+    l_walk.hop(full_out)
+    l3 = l_walk.hop(full_kvb)
+    l4 = l_walk.hop(u_q, u_kvb)
+    (hb_late,) = gate((hb,), l3)
     g_walk = Walk(ring, out_grad)
-    g_walk.hop(*l4)
-    last_lane = jnp.arange(LW) == LW - 1
-    l_blocks = []
-    for off, row, block in l_walk.blocks():
-        hide = jnp.where(ring.owner(off) > place, -1e30, 0.0).astype(bf16)
-        l_blocks.append((off, row, jnp.where(last_lane, hide, block)))
-    l_all = whole_rows(spots, l_blocks, tokens)
+    g1 = g_walk.hop(*l4)
+    (mine,) = gate((ready,), l4)
+    mine = lax.all_to_all(mine, "shard", split_axis=0, concat_axis=0, tiled=True)
+    if replicas % 2 == 0:
+        other = pair_swap(mine, replicas)
+        w_si = jnp.concatenate(
+            [jnp.where(core == 0, mine, other), jnp.where(core == 0, other, mine)], 1
+        )
+    else:
+        w_si = mine
+    w_si = w_si.reshape(shards * rows_in, 2 * half)
+
+    w_i = jnp.concatenate([w_si, pad_lanes(jnp.concatenate([w_router, a_gd.T], 1), LANES)], 1)
+    w_o = jnp.concatenate([pad_rows(w_shared_out, half), pad_rows(a_nu, LANES)], 0)
+    gu_g = lax.dynamic_slice_in_dim(a_gu, place * width, width, 1)
+    gu_u = lax.dynamic_slice_in_dim(a_gu, shards * width + place * width, width, 1)
+    u_gu = jnp.concatenate([pad_lanes(gu_g, half), pad_lanes(gu_u, half)], 1)
+    u_gu = pad_rows(u_gu, LANES, experts)
+    nd_own = lax.dynamic_slice_in_dim(a_nd, place * width, width, 1)
+    dn_own = pad_rows(pad_lanes(nd_own.T, LANES), half)
+
+    l_all = all_latents(spots, l_walk.blocks(), tokens)
     cos = pad_lanes(jnp.concatenate([cos_half, cos_half], 1), LANES)
     sin = pad_lanes(jnp.concatenate([sin_half, sin_half], 1), LANES)
     q = query_heads(
-        spots, hb, pad_lanes(r_qa, LANES), w_at, w_blocks, u_q, cos, sin
+        spots, hb_late, pad_lanes(r_qa, LANES), w_at, w_blocks, u_q, cos, sin
     )
 
     mixture, lse, kv = attend(l_all, full_kvb, u_kvb, q)
+    (mixture,) = gate((mixture,), g1)
     r_out = dot(mixture, a_od, NT).astype(bf16)
     after_attn = inputs + dot(mixture, full_out) + dot(r_out, a_ou)
     ffn_scale = rms_scale(after_attn)
@@ -998,7 +1053,6 @@
     members = lambda h: [
         (off, x, g) for off, x, g in zip((-h, h), walk.pairs[h - 1], g_walk.pairs[h - 1])
     ]
-    g_walk.hop(mixture)
     x1 = walk.hop()
     done = run_routed([(0, ffn_low, out_grad)])
     walk.hop(done[3])
@@ -1010,6 +1064,7 @@
     mark = run_shared(*done)
     done = run_routed(members(2), mark)
     walk.hop(done[3])
+    g_walk.hop(*walk.pairs[2])
     mark = run_shared(*done)
     opposite = (far, jnp.concatenate(walk.halves, 0), jnp.concatenate(g_walk.halves, 0))
     run_shared(*run_routed(members(3) + [opposite], mark))
@@ -1033,20 +1088,8 @@
     g_dn_up = small[2][:RANK]
     g_dn_down = spread([small[3][:RANK, :width]], shards * width)
 
-    t_ffn, seen = Totals([g_gu_down, g_gu_up, g_dn_down, g_dn_up], shards), {}
-
-    def late_hold(r, l):
-        seen["near"] = (r, l)
-        return (t_ffn.gather(ids),)
-
-    ffn_grad = ring.scatter_sum(
-        lambda off: dx_piece[off],
-        {
-            far - 1: lambda r, l: (t_ffn.packed,),
-            far - 2: lambda r, l: (t_ffn.deal(),),
-            far - 3: late_hold,
-        },
-    )
+    seen = {}
+    ffn_grad = ring.scatter_sum(lambda off: dx_piece[off], {})
 
     d_after = out_grad.astype(f32) + rms_back(after_attn, ffn_scale, ffn_gain, ffn_grad)
     d_after_low = d_after.astype(bf16)
@@ -1064,7 +1107,7 @@
         (marked,) = gate((lse,), marks) if not parts else gate((lse + 0.0,), marks)
         parts.append(
             attend_back(
-                len(parts), l_all, lt, full_kvb, u_kvb, kv, q, marked, delta, dmix, cos, sin, was
+                spots, len(parts), l_all, lt, full_kvb, u_kvb, kv, q, marked, delta, dmix, cos, sin, was
             )
         )
         return (parts[-1][2],)
@@ -1076,6 +1119,24 @@
     def next_arrived(r, l):
         seen["next"] = (r[:16], l[:16])
         return back(*seen["far"])
+
+    def last_arrived(r, l):
+        back(*seen["next"])
+        dl = parts[-1][1]
+        seen["dl"] = ring.scatter_sum(
+            lambda off: dl[off % shards],
+            {far - 2: query_grads, far - 3: dl_arrived},
+        )
+        return seen["dl near"]
+
+    def query_grads(r, l):
+        dq = jnp.concatenate([part[0] for part in parts], 0)
+        seen["q"] = query_back(spots, dq, w_at, w_blocks, u_q, pad_lanes(r_qa, LANES).T)
+        return (seen["q"][1],)
+
+    def dl_arrived(r, l):
+        seen["dl near"] = (r[:16], l[:16])
+        return ()
 
     out_sum = ring.scatter_sum(
         lambda off: out_piece[off],
@@ -1083,19 +1144,14 @@
             far: lambda: (ffn_grad,),
             far - 1: first_arrived,
             far - 2: next_arrived,
-            far - 3: lambda r, l: back(*seen["next"]),
+            far - 3: last_arrived,
         },
     )
     block_out = (after_attn + out_sum).astype(bf16)
-    dq = jnp.concatenate([part[0] for part in parts], 0)
-    dl = parts[-1][1]
     g_ku = jnp.concatenate([part[2] for part in parts], 1)
     g_kvb_up = g_ku[ROPE : ROPE + RANK]
-    dhb_q, dr_q, g_qu = query_back(spots, dq, w_at, w_blocks, u_q, pad_lanes(r_qa, LANES).T)
-    dl_own = ring.scatter_sum(
-        lambda off: lax.dynamic_slice_in_dim(dl, ring.owner(off) * tokens, tokens, 0),
-        {far - 2: lambda r, l: (dr_q,)},
-    )
+    dhb_q, dr_q, g_qu = seen["q"]
+    dl_own = seen["dl"]
     dr_kv = dl_own[:, LATENT + ROPE : LATENT + ROPE + RANK].astype(bf16)
     d_latent = dl_own[:, :LATENT] + dot(dr_kv, a_kd)
     g_kvb_down = dot(dr_kv, latent, TN)
@@ -1113,11 +1169,13 @@
     hidden_grad = d_after + rms_back(inputs, in_scale, attn_gain, dhb)
 
     t_attn = Totals(
-        [g_qa_down, g_qa_up, g_kvb_down, g_kvb_up, g_out_down, g_out_up], shards
+        [g_qa_down, g_qa_up, g_kvb_down, g_kvb_up, g_out_down, g_out_up]
+        + [g_gu_down, g_gu_up, g_dn_down, g_dn_up],
+        shards,
     )
     t_attn.deal()
     t_attn.gather(ids)
-    return (block_out, hidden_grad, *t_attn.home(), *t_ffn.home())
+    return (block_out, hidden_grad, *t_attn.home())
 
 
 def solution(mesh):

time: 948 us -> 901 us (0.950)
  starting transfers between devices: 121 us -> 98.3 us
  local copies, waits for them, and re-layouts: 81.8 us -> 93.2 us
  waiting for transfers between devices: 236 us -> 225 us
  between operations: 14.2 us -> 3.97 us
    all_to_all x2 -> x1, waiting for transfers between devices: 24.9 us -> 0.74 us  [deal(): lax.all_to_all(self.packed, 'shard', split_axis=0, concat_axis=0, tiled=T...]
    ppermute x28, waiting for transfers between devices: 50.9 us -> 65.5 us  [send_left(): return lax.ppermute(v, 'shard', self.left)]
    pallas_call x4, Pallas kernels: 74.7 us -> 86.8 us  [shared(): pl.pallas_call(functools.partial(shared_kernel, offs=offs, slots=slots, e...]
    all_to_all x2 -> x1, waiting for transfers between devices: 25.5 us -> 14.4 us  [home(): lax.all_to_all(self.sums, 'shard', split_axis=0, concat_axis=0, tiled=True)]
    ppermute x28, starting transfers between devices: 54.9 us -> 44.9 us  [send_right(): return lax.ppermute(v, 'shard', self.right)]
    unnamed x246 -> x232, local copies, waits for them, and re-layouts: 30.3 us -> 37.1 us
    pallas_call x3 -> x4, Pallas kernels: 98 us -> 92 us  [the longest x2 54.8 us: attend_back(): pl.pallas_call(attend_back_kernel, grid_spec=spec, out_shape=[jax.ShapeDt...]
    convert_element_type x7 -> x6, other arithmetic: 19.9 us -> 15.8 us  [scatter_sum(): r, l = (self.send_right(up.astype(bf16)), self.send_left(down.astype(bf16)))]
  transfers between devices with their start and end apart: 73 -> 71, of which waited for: 31 -> 34; matrix products, arithmetic and copies ran while one was open for 16% -> 16% of each run, Pallas kernels for 24% -> 28%
where the time goes in v1:
time: 901 us; the launch traced here: 890 us
  Pallas kernels  354 us (39%)
  waiting for transfers between devices  225 us (25%)
  starting transfers between devices  98.3 us (11%)
  local copies, waits for them, and re-layouts  93.2 us (10%)
  other arithmetic  72.5 us (8%)
  matrix products  30.3 us (3%)
  blocking collectives  12.2 us (1%)
    pallas_call x4, Pallas kernels, routed(): pl.pallas_call(functools.partial(routed_kernel, offs=offs, slots=slots, w...  128 us
    ppermute x28, waiting for transfers between devices, send_right(): return lax.ppermute(v, 'shard', self.right)  124 us
    pallas_call x4, Pallas kernels, shared(): pl.pallas_call(functools.partial(shared_kernel, offs=offs, slots=slots, e...  86.8 us
    ppermute x28, waiting for transfers between devices, send_left(): return lax.ppermute(v, 'shard', self.left)  65.5 us
    pallas_call x2, Pallas kernels, attend_back(): pl.pallas_call(attend_back_kernel, grid_spec=spec, out_shape=[jax.ShapeDt...  54.8 us
    ppermute x28, starting transfers between devices, send_right(): return lax.ppermute(v, 'shard', self.right)  44.9 us
    unnamed x232, local copies, waits for them, and re-layouts  37.1 us
    pallas_call x1, Pallas kernels, attend(): pl.pallas_call(attend_kernel, grid=(HEADS // PER_STEP,), in_specs=[pl.Blo...  33.1 us
  transfers between devices with their start and end apart: 71, of which 34 were waited for; matrix products, arithmetic and copies ran while one was open for 16% of the time, Pallas kernels for 28%

profile of v1, /device:TPU:0, one launch (start us, length us, event | category | flops | bytes accessed | tf_op | source)
XLA Modules:
  0.0 889.6 jit_solution(17597635921289100382)
XLA Ops:
  17.1 31.7 %collective-permute-done.1.refs_0_ = bf16[128,6784]{1,0:T(8,128)(2,1)} collective-permute-done((bf16[128,6784]{1,0:T(8,128)(2,1)}, bf16[128,6784]{1,0:T(8,128)(2,1)}, u32[]{:S(2)}, u32[]{:S(2)}) %collective-permute-start.1) | collective-permute-done | bytes 1736736 | tf_op jit(solution)/shard_map/ppermute | solution.py:101
  81.6 10.5 %collective-permute-done.5.refs_0_ = bf16[128,6784]{1,0:T(8,128)(2,1)} collective-permute-done((bf16[128,6784]{1,0:T(8,128)(2,1)}, bf16[128,6784]{1,0:T(8,128)(2,1)}, u32[]{:S(2)}, u32[]{:S(2)}) %collective-permute-start.5) | collective-permute-done | bytes 1736736 | tf_op jit(solution)/shard_map/ppermute | solution.py:101
  97.0 16.9 %all-to-all-done = bf16[8,16,3456]{2,1,0:T(8,128)(2,1)} async-done(((bf16[8,16,3456]{2,1,0:T(8,128)(2,1)}), bf16[8,16,3456]{2,1,0:T(8,128)(2,1)}, u32[]{:S(2)}, u32[]{:S(2)}) %all-to-all-start) | async-done | bytes 884768 | tf_op jit(solution)/shard_map/all_to_all | solution.py:918
  121.4 5.5 all-reduce.20.refs_4_
  126.8 18.3 %collective-permute-done.10.refs_1_ = bf16[128,6784]{1,0:T(8,128)(2,1)S(1)} collective-permute-done((bf16[128,6784]{1,0:T(8,128)(2,1)}, bf16[128,6784]{1,0:T(8,128)(2,1)S(1)}, u32[]{:S(2)}, u32[]{:S(2)}) %collective-permute-start.10) | collective-permute-done | bytes 1736736 | tf_op jit(solution)/shard_map/ppermute | solution.py:104
  148.7 8.9 %collective-permute-start.13 = (bf16[64,6784]{1,0:T(8,128)(2,1)}, bf16[64,6784]{1,0:T(8,128)(2,1)}, u32[]{:S(2)}, u32[]{:S(2)}) collective-permute-start(bf16[64,6784]{1,0:T(8,128)(2,1)} %slice.329), channel_id=1, source_target_pairs={{0,2},{2,4},{4,6},{6,7},{7,5},{5,3},{3,1},{1,0},{8,10},{10,12},{12... | collective-permute-start | bytes 2605064 | tf_op jit(solution)/shard_map/ppermute | solution.py:101
  160.4 15.6 %collective-permute-done.13.refs_14_.rest_14_ = bf16[64,6784]{1,0:T(8,128)(2,1)} collective-permute-done((bf16[64,6784]{1,0:T(8,128)(2,1)}, bf16[64,6784]{1,0:T(8,128)(2,1)}, u32[]{:S(2)}, u32[]{:S(2)}) %collective-permute-start.13) | collective-permute-done | bytes 868384 | tf_op jit(solution)/shard_map/ppermute | solution.py:101
  175.9 7.5 collective-permute-done.15.refs_16_.rest_16_
  213.2 6.6 place_rows.4.refs_2_
  247.5 13.6 %query_heads.1.q_ref = bf16[16,256,256]{2,1,0:T(8,128)(2,1)} custom-call(s32[9]{0:T(128)} %get-tuple-element.246.info, bf16[256,2048]{1,0:T(8,128)(2,1)} %gate.33.hb_ref, bf16[256,128]{1,0:T(8,128)(2,1)} %pad.87.clone.r_ref, bf16[128,3072]{1,0:T(8,128)(2,1)} %pad.85.refs_2_.up_ref, f32[256,128]{1,0:T(8,128)} %get-tuple-element.254.cos_ref, ...), custom_call_target="tpu_custom_call" | custom-call | flops 3221225472 | bytes 12582912 | tf_op jit(solution)/shard_map/query_heads/pallas_call | solution.py:347
  274.8 33.1 %attend.1 = (bf16[256,2048]{1,0:T(8,128)(2,1)}, f32[16,8,256]{2,1,0:T(8,128)}, bf16[2048,4096]{1,0:T(8,128)(2,1)}) custom-call(bf16[2048,640]{1,0:T(8,128)(2,1)} %all_latents.1.l_ref, bf16[16,4,32,1024]{3,2,1,0:T(8,128)(2,1)} %bitcast.190, bf16[128,4096]{1,0:T(8,128)(2,1)} %pad.86.refs_3_.u_ref, bf16[16,256,256]{2,1,0:T(8,128)(2,1)} %query_heads.1.q_ref), custom_call_target="tpu_custom_call" | custom-call | flops 19327352832 | bytes 8000000 | tf_op jit(solution)/shard_map/attend/pallas_call | solution.py:460
  310.3 5.9 multiply_reduce_fusion.2
  322.6 24.9 %routed.4 = (bf16[2,128,2048]{2,1,0:T(8,128)(2,1)}, bf16[2,128,2048]{2,1,0:T(8,128)(2,1)}, bf16[2,128,128]{2,1,0:T(8,128)(2,1)}) custom-call(s32[9]{0:T(128)} %get-tuple-element.245.info, s32[8,2,256]{2,1,0:T(2,128)} %copy_select_fusion.slot_ref, bf16[2048,128]{1,0:T(8,128)(2,1)} %pad.90.wr_ref, bf16[2,2048,2816]{2,1,0:T(8,128)(2,1)} %w_in.7, ...), custom_call_target="tpu_custom_call" | custom-call | flops 8858370048 | bytes 34603008 | tf_op jit(solution)/shard_map/routed/pallas_call | solution.py:676
  356.2 11.2 %shared.4 = (bf16[1,256,2048]{2,1,0:T(8,128)(2,1)}, bf16[1,256,2048]{2,1,0:T(8,128)(2,1)}, f32[128,768]{1,0:T(8,128)}, f32[128,2048]{1,0:T(8,128)}, f32[128,2048]{1,0:T(8,128)}, /*index=5*/f32[128,384]{1,0:T(8,128)}) custom-call(s32[9]{0:T(128)} %get-tuple-element.245.info, s32[8,2,256]{2,1,0:T(2,128)} %copy_select_fusion.slot_ref, ...), custom_call_target="tpu_custom_call" | custom-call | flops 4000000000 | bytes 8000000 | tf_op jit(solution)/shard_map/shared/pallas_call | solution.py:782
  367.4 6.6 collective-permute-done.30.refs_0_
  374.1 30.4 %routed.5 = (bf16[2,256,2048]{2,1,0:T(8,128)(2,1)}, bf16[2,256,2048]{2,1,0:T(8,128)(2,1)}, bf16[2,256,128]{2,1,0:T(8,128)(2,1)}) custom-call(s32[9]{0:T(128)} %get-tuple-element.245.info, s32[8,2,256]{2,1,0:T(2,128)} %copy_select_fusion.slot_ref, bf16[2048,128]{1,0:T(8,128)(2,1)} %pad.90.wr_ref, bf16[2,2048,2816]{2,1,0:T(8,128)(2,1)} %w_in.7, ...), custom_call_target="tpu_custom_call" | custom-call | flops 17716740096 | bytes 34603008 | tf_op jit(solution)/shard_map/routed/pallas_call | solution.py:676
  408.6 18.9 %shared.5 = (bf16[2,256,2048]{2,1,0:T(8,128)(2,1)}, bf16[2,256,2048]{2,1,0:T(8,128)(2,1)}, f32[128,768]{1,0:T(8,128)}, f32[128,2048]{1,0:T(8,128)}, f32[128,2048]{1,0:T(8,128)}, /*index=5*/f32[128,384]{1,0:T(8,128)}) custom-call(s32[9]{0:T(128)} %get-tuple-element.245.info, s32[8,2,256]{2,1,0:T(2,128)} %copy_select_fusion.slot_ref, ...), custom_call_target="tpu_custom_call" | custom-call | flops 8000000000 | bytes 16000000 | tf_op jit(solution)/shard_map/shared/pallas_call | solution.py:782
  431.4 30.5 %routed.6 = (bf16[2,256,2048]{2,1,0:T(8,128)(2,1)}, bf16[2,256,2048]{2,1,0:T(8,128)(2,1)}, bf16[2,256,128]{2,1,0:T(8,128)(2,1)}) custom-call(s32[9]{0:T(128)} %get-tuple-element.245.info, s32[8,2,256]{2,1,0:T(2,128)} %copy_select_fusion.slot_ref, bf16[2048,128]{1,0:T(8,128)(2,1)} %pad.90.wr_ref, bf16[2,2048,2816]{2,1,0:T(8,128)(2,1)} %w_in.7, ...), custom_call_target="tpu_custom_call" | custom-call | flops 17716740096 | bytes 34603008 | tf_op jit(solution)/shard_map/routed/pallas_call | solution.py:676
  473.7 31.3 %shared.6 = (bf16[2,256,2048]{2,1,0:T(8,128)(2,1)}, bf16[2,256,2048]{2,1,0:T(8,128)(2,1)}, f32[128,768]{1,0:T(8,128)}, f32[128,2048]{1,0:T(8,128)}, f32[128,2048]{1,0:T(8,128)}, /*index=5*/f32[128,384]{1,0:T(8,128)}) custom-call(s32[9]{0:T(128)} %get-tuple-element.245.info, s32[8,2,256]{2,1,0:T(2,128)} %copy_select_fusion.slot_ref, ...), custom_call_target="tpu_custom_call" | custom-call | flops 8000000000 | bytes 16000000 | tf_op jit(solution)/shard_map/shared/pallas_call | solution.py:782
  508.3 42.0 %routed.7 = (bf16[2,384,2048]{2,1,0:T(8,128)(2,1)}, bf16[2,384,2048]{2,1,0:T(8,128)(2,1)}, bf16[2,384,128]{2,1,0:T(8,128)(2,1)}) custom-call(s32[9]{0:T(128)} %get-tuple-element.245.info, s32[8,2,256]{2,1,0:T(2,128)} %copy_select_fusion.slot_ref, bf16[2048,128]{1,0:T(8,128)(2,1)} %pad.90.wr_ref, bf16[2,2048,2816]{2,1,0:T(8,128)(2,1)} %w_in.7, ...), custom_call_target="tpu_custom_call" | custom-call | flops 26575110144 | bytes 34603008 | tf_op jit(solution)/shard_map/routed/pallas_call | solution.py:676
  550.4 25.4 %shared.7 = (bf16[3,256,2048]{2,1,0:T(8,128)(2,1)}, bf16[3,256,2048]{2,1,0:T(8,128)(2,1)}, f32[128,768]{1,0:T(8,128)}, f32[128,2048]{1,0:T(8,128)}, f32[128,2048]{1,0:T(8,128)}, /*index=5*/f32[128,384]{1,0:T(8,128)}) custom-call(s32[9]{0:T(128)} %get-tuple-element.245.info, s32[8,2,256]{2,1,0:T(2,128)} %copy_select_fusion.slot_ref, ...), custom_call_target="tpu_custom_call" | custom-call | flops 12000000000 | bytes 24000000 | tf_op jit(solution)/shard_map/shared/pallas_call | solution.py:782
  579.5 9.4 %collective-permute-done.42 = bf16[128,2048]{1,0:T(8,128)(2,1)S(1)} collective-permute-done((bf16[128,2048]{1,0:T(8,128)(2,1)S(1)}, bf16[128,2048]{1,0:T(8,128)(2,1)S(1)}, u32[]{:S(2)}, u32[]{:S(2)}) %collective-permute-start.42) | collective-permute-done | bytes 524320 | tf_op jit(solution)/shard_map/ppermute | solution.py:101
  598.2 18.8 %collective-permute-done.47 = bf16[256,2048]{1,0:T(8,128)(2,1)S(1)} collective-permute-done((bf16[256,2048]{1,0:T(8,128)(2,1)S(1)}, bf16[256,2048]{1,0:T(8,128)(2,1)S(1)}, u32[]{:S(2)}, u32[]{:S(2)}) %collective-permute-start.47) | collective-permute-done | bytes 1048608 | tf_op jit(solution)/shard_map/ppermute | solution.py:104
  621.9 19.9 %collective-permute-done.44 = bf16[256,2048]{1,0:T(8,128)(2,1)S(1)} collective-permute-done((bf16[256,2048]{1,0:T(8,128)(2,1)S(1)}, bf16[256,2048]{1,0:T(8,128)(2,1)S(1)}, u32[]{:S(2)}, u32[]{:S(2)}) %collective-permute-start.44) | collective-permute-done | bytes 1048608 | tf_op jit(solution)/shard_map/ppermute | solution.py:101
  655.1 13.1 %collective-permute-done.45 = bf16[256,2048]{1,0:T(8,128)(2,1)} collective-permute-done((bf16[256,2048]{1,0:T(8,128)(2,1)}, bf16[256,2048]{1,0:T(8,128)(2,1)}, u32[]{:S(2)}, u32[]{:S(2)}) %collective-permute-start.45) | collective-permute-done | bytes 1048608 | tf_op jit(solution)/shard_map/ppermute | solution.py:101
  681.2 5.9 fusion.8.dm_ref
  701.2 26.9 %attend_back.2 = (bf16[8,256,256]{2,1,0:T(8,128)(2,1)}, bf16[8,256,640]{2,1,0:T(8,128)(2,1)}, f32[128,2048]{1,0:T(8,128)}) custom-call(s32[9]{0:T(128)} %get-tuple-element.246.info, bf16[2048,640]{1,0:T(8,128)(2,1)} %all_latents.1.l_ref, bf16[128,2048]{1,0:T(8,128)(2,1)} %bitcast.224, bf16[16,4,32,1024]{3,2,1,0:T(8,128)(2,1)} %bitcast.191, ...), custom_call_target="tpu_custom_call" | custom-call | flops 13958643712 | bytes 30000000 | tf_op jit(solution)/shard_map/attend_back/pallas_call | solution.py:579
  731.1 27.8 %attend_back.3 = (bf16[8,256,256]{2,1,0:T(8,128)(2,1)}, bf16[8,256,640]{2,1,0:T(8,128)(2,1)}, f32[128,2048]{1,0:T(8,128)}) custom-call(s32[9]{0:T(128)} %get-tuple-element.246.info, bf16[2048,640]{1,0:T(8,128)(2,1)} %all_latents.1.l_ref, bf16[128,2048]{1,0:T(8,128)(2,1)} %bitcast.225, bf16[16,4,32,1024]{3,2,1,0:T(8,128)(2,1)} %bitcast.192, ...), custom_call_target="tpu_custom_call" | custom-call | flops 13958643712 | bytes 30000000 | tf_op jit(solution)/shard_map/attend_back/pallas_call | solution.py:579
  770.6 13.7 %query_back.1 = (f32[256,2048]{1,0:T(8,128)}, f32[256,128]{1,0:T(8,128)}, f32[128,3072]{1,0:T(8,128)}) custom-call(s32[9]{0:T(128)} %get-tuple-element.246.info, bf16[16,256,256]{2,1,0:T(8,128)(2,1)} %pad_maximum_fusion.1.dq_ref, bf16[128,3072]{1,0:T(8,128)(2,1)} %pad.85.refs_2_.up_ref, bf16[128,256]{1,0:T(8,128)(2,1)} %pad_bitcast_fusion.rt_ref, ...), custom_call_target="tpu_custom_call" | custom-call | flops 3221225472 | bytes 12582912 | tf_op jit(solution)/shard_map/query_back/pallas_call | solution.py:404
  846.7 6.7 all-gather
  855.0 5.6 all-to-all-start.4
  869.1 14.4 %all-to-all-done.4 = bf16[8,1,16,3456]{3,2,1,0:T(8,128)(2,1)} async-done(((bf16[8,1,16,3456]{3,2,1,0:T(8,128)(2,1)}), bf16[8,1,16,3456]{3,2,1,0:T(8,128)(2,1)}, u32[]{:S(2)}, u32[]{:S(2)}) %all-to-all-start.4) | async-done | bytes 884768 | tf_op jit(solution)/shard_map/all_to_all | solution.py:864
  (549 shorter events, 327.7 us)
Async XLA Ops:
  7.6 41.2 %collective-permute-start.1 = (bf16[128,6784]{1,0:T(8,128)(2,1)}, bf16[128,6784]{1,0:T(8,128)(2,1)}, u32[]{:S(2)}, u32[]{:S(2)}) collective-permute-start(bf16[128,6784]{1,0:T(8,128)(2,1)} %pack_weights.1.refs_0_.rest_0_), channel_id=1, source_target_pairs={{0,2},{2,4},{4,6},{6,7},{7,5},{5,3},{3,1},{1,0},{8,10},{10,12},{12... | collective-permute-start | bytes 5210120 | tf_op jit(solution)/shard_map/ppermute | solution.py:101
  10.6 39.7 %collective-permute-start.2 = (bf16[128,6784]{1,0:T(8,128)(2,1)}, bf16[128,6784]{1,0:T(8,128)(2,1)}, u32[]{:S(2)}, u32[]{:S(2)}) collective-permute-start(bf16[128,6784]{1,0:T(8,128)(2,1)} %pack_weights.1.refs_0_.rest_0_), channel_id=1, source_target_pairs={{0,1},{2,0},{4,2},{6,4},{7,6},{5,7},{3,5},{1,3},{8,9},{10,8},{12,1... | collective-permute-start | bytes 5210120 | tf_op jit(solution)/shard_map/ppermute | solution.py:104
  10.6 40.2 %collective-permute-start = (bf16[128,6784]{1,0:T(8,128)(2,1)}, bf16[128,6784]{1,0:T(8,128)(2,1)}, u32[]{:S(2)}, u32[]{:S(2)}) collective-permute-start(bf16[128,6784]{1,0:T(8,128)(2,1)} %pack_weights.1.refs_0_.rest_0_), channel_id=1, source_target_pairs={{0,8},{8,0},{16,24},{24,16},{1,9},{9,1},{17,25},{25,17},{2,10},{10... | collective-permute-start | bytes 5210120 | tf_op jit(solution)/shard_map/ppermute | solution.py:163
  50.9 30.7 %collective-permute-start.3 = (bf16[128,6784]{1,0:T(8,128)(2,1)}, bf16[128,6784]{1,0:T(8,128)(2,1)}, u32[]{:S(2)}, u32[]{:S(2)}) collective-permute-start(bf16[128,6784]{1,0:T(8,128)(2,1)} %get-tuple-element.103.refs_2_.rest_2_), channel_id=1, source_target_pairs={{0,8},{8,0},{16,24},{24,16},{1,9},{9,1},{17,25},{25,17},{2,10},{10... | collective-permute-start | bytes 5210120 | tf_op jit(solution)/shard_map/ppermute | solution.py:163
  50.9 41.1 %collective-permute-start.5 = (bf16[128,6784]{1,0:T(8,128)(2,1)}, bf16[128,6784]{1,0:T(8,128)(2,1)}, u32[]{:S(2)}, u32[]{:S(2)}) collective-permute-start(bf16[128,6784]{1,0:T(8,128)(2,1)} %get-tuple-element.103.refs_2_.rest_2_), channel_id=1, source_target_pairs={{0,2},{2,4},{4,6},{6,7},{7,5},{5,3},{3,1},{1,0},{8,10},{10,12},{12... | collective-permute-start | bytes 5210120 | tf_op jit(solution)/shard_map/ppermute | solution.py:101
  52.6 29.0 %collective-permute-start.4 = (bf16[128,6784]{1,0:T(8,128)(2,1)}, bf16[128,6784]{1,0:T(8,128)(2,1)}, u32[]{:S(2)}, u32[]{:S(2)}) collective-permute-start(bf16[128,6784]{1,0:T(8,128)(2,1)} %get-tuple-element.104.refs_4_.rest_4_), channel_id=1, source_target_pairs={{0,8},{8,0},{16,24},{24,16},{1,9},{9,1},{17,25},{25,17},{2,10},{10... | collective-permute-start | bytes 5210120 | tf_op jit(solution)/shard_map/ppermute | solution.py:163
  52.7 41.0 %collective-permute-start.6 = (bf16[128,6784]{1,0:T(8,128)(2,1)}, bf16[128,6784]{1,0:T(8,128)(2,1)}, u32[]{:S(2)}, u32[]{:S(2)}) collective-permute-start(bf16[128,6784]{1,0:T(8,128)(2,1)} %get-tuple-element.104.refs_4_.rest_4_), channel_id=1, source_target_pairs={{0,1},{2,0},{4,2},{6,4},{7,6},{5,7},{3,5},{1,3},{8,9},{10,8},{12,1... | collective-permute-start | bytes 5210120 | tf_op jit(solution)/shard_map/ppermute | solution.py:104
  56.2 57.7 %all-to-all-start = ((bf16[8,16,3456]{2,1,0:T(8,128)(2,1)}), bf16[8,16,3456]{2,1,0:T(8,128)(2,1)}, u32[]{:S(2)}, u32[]{:S(2)}) async-start(bf16[8,16,3456]{2,1,0:T(8,128)(2,1)} %copy.213), calls=%async_computation | async-start | bytes 1769472 | tf_op jit(solution)/shard_map/all_to_all | solution.py:918
  93.8 51.4 %collective-permute-start.10 = (bf16[128,6784]{1,0:T(8,128)(2,1)}, bf16[128,6784]{1,0:T(8,128)(2,1)S(1)}, u32[]{:S(2)}, u32[]{:S(2)}) collective-permute-start(bf16[128,6784]{1,0:T(8,128)(2,1)} %get-tuple-element.106.refs_8_.rest_8_), channel_id=1, source_target_pairs={{0,1},{2,0},{4,2},{6,4},{7,6},{5,7},{3,5},{1,3},{8,9},{10,8},{12,1... | collective-permute-start | bytes 5210120 | tf_op jit(solution)/shard_map/ppermute | solution.py:104
  94.3 50.8 %collective-permute-start.7 = (bf16[128,6784]{1,0:T(8,128)(2,1)}, bf16[128,6784]{1,0:T(8,128)(2,1)}, u32[]{:S(2)}, u32[]{:S(2)}) collective-permute-start(bf16[128,6784]{1,0:T(8,128)(2,1)} %get-tuple-element.105.refs_6_.rest_6_), channel_id=1, source_target_pairs={{0,8},{8,0},{16,24},{24,16},{1,9},{9,1},{17,25},{25,17},{2,10},{10... | collective-permute-start | bytes 5210120 | tf_op jit(solution)/shard_map/ppermute | solution.py:163
  94.3 50.8 %collective-permute-start.8 = (bf16[128,6784]{1,0:T(8,128)(2,1)}, bf16[128,6784]{1,0:T(8,128)(2,1)}, u32[]{:S(2)}, u32[]{:S(2)}) collective-permute-start(bf16[128,6784]{1,0:T(8,128)(2,1)} %get-tuple-element.106.refs_8_.rest_8_), channel_id=1, source_target_pairs={{0,8},{8,0},{16,24},{24,16},{1,9},{9,1},{17,25},{25,17},{2,10},{10... | collective-permute-start | bytes 5210120 | tf_op jit(solution)/shard_map/ppermute | solution.py:163
  94.9 50.3 %collective-permute-start.9 = (bf16[128,6784]{1,0:T(8,128)(2,1)}, bf16[128,6784]{1,0:T(8,128)(2,1)}, u32[]{:S(2)}, u32[]{:S(2)}) collective-permute-start(bf16[128,6784]{1,0:T(8,128)(2,1)} %get-tuple-element.105.refs_6_.rest_6_), channel_id=1, source_target_pairs={{0,2},{2,4},{4,6},{6,7},{7,5},{5,3},{3,1},{1,0},{8,10},{10,12},{12... | collective-permute-start | bytes 5210120 | tf_op jit(solution)/shard_map/ppermute | solution.py:101
  115.8 73.8 %all-to-all-start.1 = ((bf16[8,16,3456]{2,1,0:T(8,128)(2,1)}), bf16[8,16,3456]{2,1,0:T(8,128)(2,1)}, u32[]{:S(2)}, u32[]{:S(2)}) async-start(bf16[8,16,3456]{2,1,0:T(8,128)(2,1)} %broadcast_in_dim.19), calls=%async_computation.1 | async-start | bytes 1769472 | tf_op jit(solution)/shard_map/all_to_all | solution.py:921
  158.6 33.7 %collective-permute-start.11 = (bf16[128,6784]{1,0:T(8,128)(2,1)}, bf16[128,6784]{1,0:T(8,128)(2,1)}, u32[]{:S(2)}, u32[]{:S(2)}) collective-permute-start(bf16[128,6784]{1,0:T(8,128)(2,1)} %get-tuple-element.107.refs_10_.rest_10_), channel_id=1, source_target_pairs={{0,8},{8,0},{16,24},{24,16},{1,9},{9,1},{17,25},{25,17},{2,10},{10... | collective-permute-start | bytes 5210120 | tf_op jit(solution)/shard_map/ppermute | solution.py:163
  158.6 33.7 %collective-permute-start.12 = (bf16[128,6784]{1,0:T(8,128)(2,1)S(1)}, bf16[128,6784]{1,0:T(8,128)(2,1)}, u32[]{:S(2)}, u32[]{:S(2)}) collective-permute-start(bf16[128,6784]{1,0:T(8,128)(2,1)S(1)} %copy-done.4), channel_id=1, source_target_pairs={{0,8},{8,0},{16,24},{24,16},{1,9},{9,1},{17,25},{25,17},{2,10},{10... | collective-permute-start | bytes 5210120 | tf_op jit(solution)/shard_map/ppermute | solution.py:163
  262.5 45.5 %collective-permute-start.25 = (bf16[256,2048]{1,0:T(8,128)(2,1)}, bf16[256,2048]{1,0:T(8,128)(2,1)}, u32[]{:S(2)}, u32[]{:S(2)}) collective-permute-start(bf16[256,2048]{1,0:T(8,128)(2,1)} %gate.34), channel_id=1, source_target_pairs={{0,2},{2,4},{4,6},{6,7},{7,5},{5,3},{3,1},{1,0},{8,10},{10,12},{12... | collective-permute-start | bytes 3145736 | tf_op jit(solution)/shard_map/ppermute | solution.py:101
  263.2 44.8 %collective-permute-start.26 = (bf16[256,2048]{1,0:T(8,128)(2,1)}, bf16[256,2048]{1,0:T(8,128)(2,1)}, u32[]{:S(2)}, u32[]{:S(2)}) collective-permute-start(bf16[256,2048]{1,0:T(8,128)(2,1)} %gate.34), channel_id=1, source_target_pairs={{0,1},{2,0},{4,2},{6,4},{7,6},{5,7},{3,5},{1,3},{8,9},{10,8},{12,1... | collective-permute-start | bytes 3145736 | tf_op jit(solution)/shard_map/ppermute | solution.py:104
  264.5 54.8 %all-to-all-start.2 = ((bf16[8,128,768]{2,1,0:T(8,128)(2,1)}), bf16[8,128,768]{2,1,0:T(8,128)(2,1)}, u32[]{:S(2)}, u32[]{:S(2)}) async-start(bf16[8,128,768]{2,1,0:T(8,128)(2,1)} %gate.36), calls=%async_computation.2 | async-start | bytes 3145728 | tf_op jit(solution)/shard_map/all_to_all | solution.py:986
  319.3 32.4 %collective-permute-start.27 = (bf16[8,128,768]{2,1,0:T(8,128)(2,1)}, bf16[8,128,768]{2,1,0:T(8,128)(2,1)}, u32[]{:S(2)}, u32[]{:S(2)}) collective-permute-start(bf16[8,128,768]{2,1,0:T(8,128)(2,1)} %all-to-all-done.2), channel_id=1, source_target_pairs={{0,8},{8,0},{16,24},{24,16},{1,9},{9,1},{17,25},{25,17},{2,10},{10... | collective-permute-start | bytes 4718600 | tf_op jit(solution)/shard_map/ppermute | solution.py:163
  319.6 28.0 %collective-permute-start.28 = (bf16[256,2048]{1,0:T(8,128)(2,1)S(1)}, bf16[256,2048]{1,0:T(8,128)(2,1)}, u32[]{:S(2)}, u32[]{:S(2)}) collective-permute-start(bf16[256,2048]{1,0:T(8,128)(2,1)S(1)} %multiply_convert_fusion.rest_0_), channel_id=1, source_target_pairs={{0,2},{2,4},{4,6},{6,7},{7,5},{5,3},{3,1},{1,0},{8,10},{10,12},{12... | collective-permute-start | bytes 3145736 | tf_op jit(solution)/shard_map/ppermute | solution.py:101
  319.6 27.9 %collective-permute-start.29 = (bf16[256,2048]{1,0:T(8,128)(2,1)S(1)}, bf16[256,2048]{1,0:T(8,128)(2,1)}, u32[]{:S(2)}, u32[]{:S(2)}) collective-permute-start(bf16[256,2048]{1,0:T(8,128)(2,1)S(1)} %multiply_convert_fusion.rest_0_), channel_id=1, source_target_pairs={{0,1},{2,0},{4,2},{6,4},{7,6},{5,7},{3,5},{1,3},{8,9},{10,8},{12,1... | collective-permute-start | bytes 3145736 | tf_op jit(solution)/shard_map/ppermute | solution.py:104
  349.7 56.9 %collective-permute-start.32 = (bf16[256,2048]{1,0:T(8,128)(2,1)}, bf16[256,2048]{1,0:T(8,128)(2,1)}, u32[]{:S(2)}, u32[]{:S(2)}) collective-permute-start(bf16[256,2048]{1,0:T(8,128)(2,1)} %get-tuple-element.125.rest_2_), channel_id=1, source_target_pairs={{0,2},{2,4},{4,6},{6,7},{7,5},{5,3},{3,1},{1,0},{8,10},{10,12},{12... | collective-permute-start | bytes 3145736 | tf_op jit(solution)/shard_map/ppermute | solution.py:101
  349.8 56.8 %collective-permute-start.33 = (bf16[256,2048]{1,0:T(8,128)(2,1)}, bf16[256,2048]{1,0:T(8,128)(2,1)}, u32[]{:S(2)}, u32[]{:S(2)}) collective-permute-start(bf16[256,2048]{1,0:T(8,128)(2,1)} %get-tuple-element.126.rest_3_), channel_id=1, source_target_pairs={{0,1},{2,0},{4,2},{6,4},{7,6},{5,7},{3,5},{1,3},{8,9},{10,8},{12,1... | collective-permute-start | bytes 3145736 | tf_op jit(solution)/shard_map/ppermute | solution.py:104
  406.6 59.2 %collective-permute-start.38 = (bf16[256,2048]{1,0:T(8,128)(2,1)}, bf16[256,2048]{1,0:T(8,128)(2,1)}, u32[]{:S(2)}, u32[]{:S(2)}) collective-permute-start(bf16[256,2048]{1,0:T(8,128)(2,1)} %get-tuple-element.136.rest_2_), channel_id=1, source_target_pairs={{0,2},{2,4},{4,6},{6,7},{7,5},{5,3},{3,1},{1,0},{8,10},{10,12},{12... | collective-permute-start | bytes 3145736 | tf_op jit(solution)/shard_map/ppermute | solution.py:101
  407.1 58.7 %collective-permute-start.39 = (bf16[256,2048]{1,0:T(8,128)(2,1)}, bf16[256,2048]{1,0:T(8,128)(2,1)}, u32[]{:S(2)}, u32[]{:S(2)}) collective-permute-start(bf16[256,2048]{1,0:T(8,128)(2,1)} %get-tuple-element.137.rest_3_), channel_id=1, source_target_pairs={{0,1},{2,0},{4,2},{6,4},{7,6},{5,7},{3,5},{1,3},{8,9},{10,8},{12,1... | collective-permute-start | bytes 3145736 | tf_op jit(solution)/shard_map/ppermute | solution.py:104
  467.7 39.5 %collective-permute-start.40 = (bf16[128,2048]{1,0:T(8,128)(2,1)}, bf16[128,2048]{1,0:T(8,128)(2,1)S(1)}, u32[]{:S(2)}, u32[]{:S(2)}) collective-permute-start(bf16[128,2048]{1,0:T(8,128)(2,1)} %slice.355), channel_id=1, source_target_pairs={{0,2},{2,4},{4,6},{6,7},{7,5},{5,3},{3,1},{1,0},{8,10},{10,12},{12... | collective-permute-start | bytes 1572872 | tf_op jit(solution)/shard_map/ppermute | solution.py:101
  471.6 35.6 %collective-permute-start.41 = (bf16[128,2048]{1,0:T(8,128)(2,1)}, bf16[128,2048]{1,0:T(8,128)(2,1)S(1)}, u32[]{:S(2)}, u32[]{:S(2)}) collective-permute-start(bf16[128,2048]{1,0:T(8,128)(2,1)} %slice.356), channel_id=1, source_target_pairs={{0,1},{2,0},{4,2},{6,4},{7,6},{5,7},{3,5},{1,3},{8,9},{10,8},{12,1... | collective-permute-start | bytes 1572872 | tf_op jit(solution)/shard_map/ppermute | solution.py:104
  471.6 33.3 %collective-permute-start.36 = (bf16[128,2048]{1,0:T(8,128)(2,1)}, bf16[128,2048]{1,0:T(8,128)(2,1)}, u32[]{:S(2)}, u32[]{:S(2)}) collective-permute-start(bf16[128,2048]{1,0:T(8,128)(2,1)} %slice.353), channel_id=1, source_target_pairs={{0,2},{2,4},{4,6},{6,7},{7,5},{5,3},{3,1},{1,0},{8,10},{10,12},{12... | collective-permute-start | bytes 1572872 | tf_op jit(solution)/shard_map/ppermute | solution.py:101
  473.7 31.3 %collective-permute-start.37 = (bf16[128,2048]{1,0:T(8,128)(2,1)S(1)}, bf16[128,2048]{1,0:T(8,128)(2,1)}, u32[]{:S(2)}, u32[]{:S(2)}) collective-permute-start(bf16[128,2048]{1,0:T(8,128)(2,1)S(1)} %copy-done.50), channel_id=1, source_target_pairs={{0,1},{2,0},{4,2},{6,4},{7,6},{5,7},{3,5},{1,3},{8,9},{10,8},{12,1... | collective-permute-start | bytes 1572872 | tf_op jit(solution)/shard_map/ppermute | solution.py:104
  696.6 31.4 %collective-permute-start.52 = (bf16[256,2048]{1,0:T(8,128)(2,1)}, bf16[256,2048]{1,0:T(8,128)(2,1)}, u32[]{:S(2)}, u32[]{:S(2)}) collective-permute-start(bf16[256,2048]{1,0:T(8,128)(2,1)} %pad_maximum_fusion.5), channel_id=1, source_target_pairs={{0,2},{2,4},{4,6},{6,7},{7,5},{5,3},{3,1},{1,0},{8,10},{10,12},{12... | collective-permute-start | bytes 3145736 | tf_op jit(solution)/shard_map/ppermute | solution.py:101
  697.8 31.8 %collective-permute-start.53 = (bf16[256,2048]{1,0:T(8,128)(2,1)}, bf16[256,2048]{1,0:T(8,128)(2,1)}, u32[]{:S(2)}, u32[]{:S(2)}) collective-permute-start(bf16[256,2048]{1,0:T(8,128)(2,1)} %pad_maximum_fusion.6), channel_id=1, source_target_pairs={{0,1},{2,0},{4,2},{6,4},{7,6},{5,7},{3,5},{1,3},{8,9},{10,8},{12,1... | collective-permute-start | bytes 3145736 | tf_op jit(solution)/shard_map/ppermute | solution.py:104
  855.0 28.5 %all-to-all-start.4 = ((bf16[8,1,16,3456]{3,2,1,0:T(8,128)(2,1)}), bf16[8,1,16,3456]{3,2,1,0:T(8,128)(2,1)}, u32[]{:S(2)}, u32[]{:S(2)}) async-start(bf16[8,1,16,3456]{3,2,1,0:T(8,128)(2,1)} %bitcast.212), calls=%async_computation.4 | async-start | bytes 1769472 | tf_op jit(solution)/shard_map/all_to_all | solution.py:864
  (141 other events, 1495.0 us)

commit v2 on v1

--- a/solution.py
+++ b/solution.py
@@ -700,22 +700,14 @@
     slots,
     experts,
 ):
-    blocks = rest[:-8]
-    out_ref, dout_ref, gu_up_ref, gu_down_ref, dn_up_ref, dn_down_ref, x_ref, g_ref = rest[-8:]
-    c = pl.program_id(0)
     chunks, count = len(offs), info.shape[0] - 1
-    spot = sum(jnp.where(c == i, off % count, 0) for i, off in enumerate(offs))
-    owner = info[1 + spot]
-    for i in range(chunks):
-
-        @pl.when(c == i)
-        def _(i=i):
-            x_ref[...] = blocks[i][...]
-            g_ref[...] = blocks[chunks + i][...]
-
+    blocks = rest[: 2 * chunks]
+    out_ref, dout_ref, gu_up_ref, gu_down_ref, dn_up_ref, dn_down_ref = rest[2 * chunks :]
     local = y_ref.shape[0]
     half = dn_ref.shape[0]
-    x, g = x_ref[...], g_ref[...]
+    tokens = blocks[0].shape[0]
+    x = jnp.concatenate([ref[...] for ref in blocks[:chunks]], 0)
+    g = jnp.concatenate([ref[...] for ref in blocks[chunks:]], 0)
     proj = dot(x, wi_ref[...])
     r = proj[:, 2 * half :].astype(bf16)
     prob = router_probs(proj[:, 2 * half :], experts)
@@ -730,65 +722,55 @@
     dboth = jnp.concatenate([dinner * up * slope, dinner * silu], 1).astype(bf16)
     dr = dot(dboth, u_ref[...], NT)
 
-    pick = jnp.concatenate([picks(slot_ref[owner, e : e + 1, :], slots) for e in range(local)], 0)
-    rows = lambda ref: jnp.concatenate([ref[e] for e in range(local)], 0)
-    out = dot(jnp.concatenate([inner, rdn], 1), wo_ref[...]) + dot(pick, rows(y_ref), TN)
-    out_ref[0] = out.astype(bf16)
-    pulls = dot(pick, rows(pull_ref), TN)
+    def rows(ref, c, a, b):
+        return jnp.concatenate([ref[e, c * slots : (c + 1) * slots, a:b] for e in range(local)], 0)
+
+    chosen, pulls = [], []
+    for c in range(chunks):
+        owner = info[1 + offs[c] % count]
+        pick = [picks(slot_ref[owner, e : e + 1, :], slots) for e in range(local)]
+        chosen.append(jnp.concatenate(pick, 0))
+        pulls.append(dot(chosen[c], rows(pull_ref, c, 0, LANES), TN))
+    pulls = jnp.concatenate(pulls, 0)
     dlogit = pulls - prob * jnp.sum(pulls, axis=1, keepdims=True)
-    dsmall = (dr + dlogit).astype(bf16)
-    dx = dot(jnp.concatenate([dboth, dsmall], 1), wi_ref[...], NT)
-    dout_ref[0] = (dx + dot(pick, rows(dx_ref), TN)).astype(bf16)
-
-    @pl.when(c == 0)
-    def _():
-        gu_up_ref[...] = jnp.zeros_like(gu_up_ref)
-        gu_down_ref[...] = jnp.zeros_like(gu_down_ref)
-        dn_up_ref[...] = jnp.zeros_like(dn_up_ref)
-        dn_down_ref[...] = jnp.zeros_like(dn_down_ref)
-
-    gu_up_ref[...] += dot(r, dboth, TN)
-    gu_down_ref[...] += dot(dr.astype(bf16), x, TN)
-    dn_up_ref[...] += dot(rdn, g, TN)
-    dn_down_ref[...] += dot(drdn, inner, TN)
+    both = jnp.concatenate([inner, rdn], 1)
+    dall = jnp.concatenate([dboth, (dr + dlogit).astype(bf16)], 1)
+    step = 4 * LANES
+    for a in range(0, D, step):
+        out = dot(both, wo_ref[:, a : a + step])
+        dx = dot(dall, wi_ref[a : a + step, :], NT)
+        for c in range(chunks):
+            at = slice(c * tokens, (c + 1) * tokens)
+            put = lambda ref: dot(chosen[c], rows(ref, c, a, a + step), TN)
+            out_ref[c, :, a : a + step] = (out[at] + put(y_ref)).astype(bf16)
+            dout_ref[c, :, a : a + step] = (dx[at] + put(dx_ref)).astype(bf16)
+    gu_up_ref[...] = dot(r, dboth, TN)
+    gu_down_ref[...] = dot(dr.astype(bf16), x, TN)
+    dn_up_ref[...] = dot(rdn, g, TN)
+    dn_down_ref[...] = dot(drdn, inner, TN)
 
 
 def shared(info, offs, xs, gs, slot_all, experts, y, dx, pull, wi, wo, u, dn):
     chunks, tokens = len(xs), xs[0].shape[0]
-    local = y.shape[0]
     slots = tokens // 2
     half = dn.shape[0]
-    whole = lambda a: pl.BlockSpec(a.shape, lambda c, s: (0,) * a.ndim)
-    one = pl.BlockSpec((1, tokens, D), lambda c, s: (c, 0, 0))
-    rows = lambda a: pl.BlockSpec((local, slots, a.shape[2]), lambda c, s: (0, c, 0))
-    still = lambda *shape: pl.BlockSpec(shape, lambda c, s: (0, 0))
+    once = pl.Buffered(1)
+    whole = lambda a: pl.BlockSpec(a.shape, lambda c, s: (0,) * a.ndim, pipeline_mode=once)
+    still = lambda *shape: pl.BlockSpec(shape, lambda c, s: (0,) * len(shape))
     operands = [slot_all, y, dx, pull, wi, wo, u, dn, *xs, *gs]
-    specs = [whole(slot_all), rows(y), rows(dx), rows(pull)]
-    specs += [whole(a) for a in operands[4:]]
+    shapes = [(chunks, tokens, D)] * 2
+    shapes += [(LANES, 2 * half), (LANES, D), (LANES, D), (LANES, half)]
     spec = pltpu.PrefetchScalarGridSpec(
         num_scalar_prefetch=1,
-        grid=(chunks,),
-        in_specs=specs,
-        out_specs=[
-            one,
-            one,
-            still(LANES, 2 * half),
-            still(LANES, D),
-            still(LANES, D),
-            still(LANES, half),
-        ],
-        scratch_shapes=[pltpu.VMEM((tokens, D), bf16)] * 2,
+        grid=(1,),
+        in_specs=[whole(a) for a in operands],
+        out_specs=[still(*shape) for shape in shapes],
     )
     return pl.pallas_call(
         functools.partial(shared_kernel, offs=offs, slots=slots, experts=experts),
         grid_spec=spec,
         out_shape=[
-            jax.ShapeDtypeStruct((chunks, tokens, D), bf16),
-            jax.ShapeDtypeStruct((chunks, tokens, D), bf16),
-            jax.ShapeDtypeStruct((LANES, 2 * half), f32),
-            jax.ShapeDtypeStruct((LANES, D), f32),
-            jax.ShapeDtypeStruct((LANES, D), f32),
-            jax.ShapeDtypeStruct((LANES, half), f32),
+            jax.ShapeDtypeStruct(shape, bf16 if i < 2 else f32) for i, shape in enumerate(shapes)
         ],
         compiler_params=params(1),
         cost_estimate=cost(chunks * 4e9, chunks * 8e6),
@@ -944,7 +926,7 @@
     in_scale = rms_scale(inputs)
     hb = (inputs * in_scale * attn_gain).astype(bf16)
     swap1 = w_swaps.swap(w_walk.pairs[0])
-    w3 = w_walk.hop(*swap1, ready, hb)
+    w3 = w_walk.hop(*swap1, ready[0, :16], hb[:16])
     swap2 = w_swaps.swap(w_walk.pairs[1])
     w4 = w_walk.hop(*swap2, ids)
     u_q = pad_rows(a_quq, LANES)

time: 901 us -> 887 us (0.984)
  Pallas kernels: 354 us -> 337 us
    ppermute x28, waiting for transfers between devices: 124 us -> 145 us  [send_right(): return lax.ppermute(v, 'shard', self.right)]
    pallas_call x4, Pallas kernels: 86.8 us -> 69.5 us  [shared(): pl.pallas_call(functools.partial(shared_kernel, offs=offs, slots=slots, e...]
    all_to_all x2, waiting for transfers between devices: 16.9 us -> 0.01 us  [body(): lax.all_to_all(dealt, 'shard', split_axis=0, concat_axis=0, tiled=True)]
    unnamed x232 -> x238, local copies, waits for them, and re-layouts: 37.1 us -> 32.6 us
  transfers between devices with their start and end apart: 71 -> 71, of which waited for: 34 -> 33; matrix products, arithmetic and copies ran while one was open for 16% -> 16% of each run, Pallas kernels for 28% -> 27%
where the time goes in v2:
time: 887 us; the launch traced here: 876 us
  Pallas kernels  337 us (38%)
  waiting for transfers between devices  232 us (26%)
  starting transfers between devices  99.6 us (11%)
  local copies, waits for them, and re-layouts  87.2 us (10%)
  other arithmetic  71.5 us (8%)
  matrix products  31.8 us (4%)
  blocking collectives  12.2 us (1%)
    ppermute x28, waiting for transfers between devices, send_right(): return lax.ppermute(v, 'shard', self.right)  145 us
    pallas_call x4, Pallas kernels, routed(): pl.pallas_call(functools.partial(routed_kernel, offs=offs, slots=slots, w...  128 us
    pallas_call x4, Pallas kernels, shared(): pl.pallas_call(functools.partial(shared_kernel, offs=offs, slots=slots, e...  69.5 us
    ppermute x28, waiting for transfers between devices, send_left(): return lax.ppermute(v, 'shard', self.left)  68.2 us
    pallas_call x2, Pallas kernels, attend_back(): pl.pallas_call(attend_back_kernel, grid_spec=spec, out_shape=[jax.ShapeDt...  54.8 us
    ppermute x28, starting transfers between devices, send_right(): return lax.ppermute(v, 'shard', self.right)  44.8 us
    pallas_call x1, Pallas kernels, attend(): pl.pallas_call(attend_kernel, grid=(HEADS // PER_STEP,), in_specs=[pl.Blo...  33.1 us
    unnamed x238, local copies, waits for them, and re-layouts  32.6 us
  transfers between devices with their start and end apart: 71, of which 33 were waited for; matrix products, arithmetic and copies ran while one was open for 16% of the time, Pallas kernels for 27%

profile of v2, /device:TPU:0, one launch (start us, length us, event | category | flops | bytes accessed | tf_op | source)
XLA Modules:
  0.0 875.6 jit_solution(1269512260799849953)
XLA Ops:
  12.2 6.3 all-to-all-start
  18.4 31.2 %collective-permute-done.1.refs_0_ = bf16[128,6784]{1,0:T(8,128)(2,1)} collective-permute-done((bf16[128,6784]{1,0:T(8,128)(2,1)}, bf16[128,6784]{1,0:T(8,128)(2,1)}, u32[]{:S(2)}, u32[]{:S(2)}) %collective-permute-start.1) | collective-permute-done | bytes 1736736 | tf_op jit(solution)/shard_map/ppermute | solution.py:101
  75.5 24.0 %collective-permute-done.5.refs_0_ = bf16[128,6784]{1,0:T(8,128)(2,1)} collective-permute-done((bf16[128,6784]{1,0:T(8,128)(2,1)}, bf16[128,6784]{1,0:T(8,128)(2,1)}, u32[]{:S(2)}, u32[]{:S(2)}) %collective-permute-start.5) | collective-permute-done | bytes 1736736 | tf_op jit(solution)/shard_map/ppermute | solution.py:101
  102.7 6.0 collective-permute-start.9
  116.8 5.5 all-reduce.20.refs_4_
  122.3 25.3 %collective-permute-done.10.refs_1_ = bf16[128,6784]{1,0:T(8,128)(2,1)S(1)} collective-permute-done((bf16[128,6784]{1,0:T(8,128)(2,1)}, bf16[128,6784]{1,0:T(8,128)(2,1)S(1)}, u32[]{:S(2)}, u32[]{:S(2)}) %collective-permute-start.10) | collective-permute-done | bytes 1736736 | tf_op jit(solution)/shard_map/ppermute | solution.py:104
  156.6 22.6 %collective-permute-done.13.refs_14_.rest_14_ = bf16[64,6784]{1,0:T(8,128)(2,1)S(1)} collective-permute-done((bf16[64,6784]{1,0:T(8,128)(2,1)}, bf16[64,6784]{1,0:T(8,128)(2,1)S(1)}, u32[]{:S(2)}, u32[]{:S(2)}) %collective-permute-start.13) | collective-permute-done | bytes 868384 | tf_op jit(solution)/shard_map/ppermute | solution.py:101
  203.2 6.6 collective-permute-start.17
  213.9 6.5 place_rows.4.refs_2_
  248.6 13.6 %query_heads.1.q_ref = bf16[16,256,256]{2,1,0:T(8,128)(2,1)} custom-call(s32[9]{0:T(128)} %get-tuple-element.246.info, bf16[256,2048]{1,0:T(8,128)(2,1)} %gate.33.hb_ref, bf16[256,128]{1,0:T(8,128)(2,1)} %pad.87.clone.r_ref, bf16[128,3072]{1,0:T(8,128)(2,1)} %pad.85.refs_2_.up_ref, f32[256,128]{1,0:T(8,128)} %get-tuple-element.254.cos_ref, ...), custom_call_target="tpu_custom_call" | custom-call | flops 3221225472 | bytes 12582912 | tf_op jit(solution)/shard_map/query_heads/pallas_call | solution.py:347
  276.0 33.1 %attend.1 = (bf16[256,2048]{1,0:T(8,128)(2,1)}, f32[16,8,256]{2,1,0:T(8,128)}, bf16[2048,4096]{1,0:T(8,128)(2,1)}) custom-call(bf16[2048,640]{1,0:T(8,128)(2,1)} %all_latents.1.l_ref, bf16[16,4,32,1024]{3,2,1,0:T(8,128)(2,1)} %bitcast.192, bf16[128,4096]{1,0:T(8,128)(2,1)} %pad.86.refs_3_.u_ref, bf16[16,256,256]{2,1,0:T(8,128)(2,1)} %query_heads.1.q_ref), custom_call_target="tpu_custom_call" | custom-call | flops 19327352832 | bytes 8000000 | tf_op jit(solution)/shard_map/attend/pallas_call | solution.py:460
  311.4 5.9 multiply_reduce_fusion.2
  324.0 24.9 %routed.4 = (bf16[2,128,2048]{2,1,0:T(8,128)(2,1)}, bf16[2,128,2048]{2,1,0:T(8,128)(2,1)}, bf16[2,128,128]{2,1,0:T(8,128)(2,1)}) custom-call(s32[9]{0:T(128)} %get-tuple-element.245.info, s32[8,2,256]{2,1,0:T(2,128)} %copy_select_fusion.slot_ref, bf16[2048,128]{1,0:T(8,128)(2,1)} %pad.90.wr_ref, bf16[2,2048,2816]{2,1,0:T(8,128)(2,1)} %w_in.7, ...), custom_call_target="tpu_custom_call" | custom-call | flops 8858370048 | bytes 34603008 | tf_op jit(solution)/shard_map/routed/pallas_call | solution.py:676
  357.5 11.1 %shared.4 = (bf16[1,256,2048]{2,1,0:T(8,128)(2,1)}, bf16[1,256,2048]{2,1,0:T(8,128)(2,1)}, f32[128,768]{1,0:T(8,128)}, f32[128,2048]{1,0:T(8,128)}, f32[128,2048]{1,0:T(8,128)}, /*index=5*/f32[128,384]{1,0:T(8,128)}) custom-call(s32[9]{0:T(128)} %get-tuple-element.245.info, s32[8,2,256]{2,1,0:T(2,128)} %copy_select_fusion.slot_ref, ...), custom_call_target="tpu_custom_call" | custom-call | flops 4000000000 | bytes 8000000 | tf_op jit(solution)/shard_map/shared/pallas_call | solution.py:769
  368.6 6.7 collective-permute-done.30.refs_0_
  375.4 30.4 %routed.5 = (bf16[2,256,2048]{2,1,0:T(8,128)(2,1)}, bf16[2,256,2048]{2,1,0:T(8,128)(2,1)}, bf16[2,256,128]{2,1,0:T(8,128)(2,1)}) custom-call(s32[9]{0:T(128)} %get-tuple-element.245.info, s32[8,2,256]{2,1,0:T(2,128)} %copy_select_fusion.slot_ref, bf16[2048,128]{1,0:T(8,128)(2,1)} %pad.90.wr_ref, bf16[2,2048,2816]{2,1,0:T(8,128)(2,1)} %w_in.7, ...), custom_call_target="tpu_custom_call" | custom-call | flops 17716740096 | bytes 34603008 | tf_op jit(solution)/shard_map/routed/pallas_call | solution.py:676
  410.1 17.3 %shared.5 = (bf16[2,256,2048]{2,1,0:T(8,128)(2,1)}, bf16[2,256,2048]{2,1,0:T(8,128)(2,1)}, f32[128,768]{1,0:T(8,128)}, f32[128,2048]{1,0:T(8,128)}, f32[128,2048]{1,0:T(8,128)}, /*index=5*/f32[128,384]{1,0:T(8,128)}) custom-call(s32[9]{0:T(128)} %get-tuple-element.245.info, s32[8,2,256]{2,1,0:T(2,128)} %copy_select_fusion.slot_ref, ...), custom_call_target="tpu_custom_call" | custom-call | flops 8000000000 | bytes 16000000 | tf_op jit(solution)/shard_map/shared/pallas_call | solution.py:769
  432.5 30.5 %routed.6 = (bf16[2,256,2048]{2,1,0:T(8,128)(2,1)}, bf16[2,256,2048]{2,1,0:T(8,128)(2,1)}, bf16[2,256,128]{2,1,0:T(8,128)(2,1)}) custom-call(s32[9]{0:T(128)} %get-tuple-element.245.info, s32[8,2,256]{2,1,0:T(2,128)} %copy_select_fusion.slot_ref, bf16[2048,128]{1,0:T(8,128)(2,1)} %pad.90.wr_ref, bf16[2,2048,2816]{2,1,0:T(8,128)(2,1)} %w_in.7, ...), custom_call_target="tpu_custom_call" | custom-call | flops 17716740096 | bytes 34603008 | tf_op jit(solution)/shard_map/routed/pallas_call | solution.py:676
  475.1 17.4 %shared.6 = (bf16[2,256,2048]{2,1,0:T(8,128)(2,1)}, bf16[2,256,2048]{2,1,0:T(8,128)(2,1)}, f32[128,768]{1,0:T(8,128)}, f32[128,2048]{1,0:T(8,128)}, f32[128,2048]{1,0:T(8,128)}, /*index=5*/f32[128,384]{1,0:T(8,128)}) custom-call(s32[9]{0:T(128)} %get-tuple-element.245.info, s32[8,2,256]{2,1,0:T(2,128)} %copy_select_fusion.slot_ref, ...), custom_call_target="tpu_custom_call" | custom-call | flops 8000000000 | bytes 16000000 | tf_op jit(solution)/shard_map/shared/pallas_call | solution.py:769
  496.0 42.0 %routed.7 = (bf16[2,384,2048]{2,1,0:T(8,128)(2,1)}, bf16[2,384,2048]{2,1,0:T(8,128)(2,1)}, bf16[2,384,128]{2,1,0:T(8,128)(2,1)}) custom-call(s32[9]{0:T(128)} %get-tuple-element.245.info, s32[8,2,256]{2,1,0:T(2,128)} %copy_select_fusion.slot_ref, bf16[2048,128]{1,0:T(8,128)(2,1)} %pad.90.wr_ref, bf16[2,2048,2816]{2,1,0:T(8,128)(2,1)} %w_in.7, ...), custom_call_target="tpu_custom_call" | custom-call | flops 26575110144 | bytes 34603008 | tf_op jit(solution)/shard_map/routed/pallas_call | solution.py:676
  538.0 23.7 %shared.7 = (bf16[3,256,2048]{2,1,0:T(8,128)(2,1)}, bf16[3,256,2048]{2,1,0:T(8,128)(2,1)}, f32[128,768]{1,0:T(8,128)}, f32[128,2048]{1,0:T(8,128)}, f32[128,2048]{1,0:T(8,128)}, /*index=5*/f32[128,384]{1,0:T(8,128)}) custom-call(s32[9]{0:T(128)} %get-tuple-element.245.info, s32[8,2,256]{2,1,0:T(2,128)} %copy_select_fusion.slot_ref, ...), custom_call_target="tpu_custom_call" | custom-call | flops 12000000000 | bytes 24000000 | tf_op jit(solution)/shard_map/shared/pallas_call | solution.py:769
  565.9 9.3 %collective-permute-done.42 = bf16[128,2048]{1,0:T(8,128)(2,1)S(1)} collective-permute-done((bf16[128,2048]{1,0:T(8,128)(2,1)S(1)}, bf16[128,2048]{1,0:T(8,128)(2,1)S(1)}, u32[]{:S(2)}, u32[]{:S(2)}) %collective-permute-start.42) | collective-permute-done | bytes 524320 | tf_op jit(solution)/shard_map/ppermute | solution.py:101
  584.3 19.9 %collective-permute-done.47 = bf16[256,2048]{1,0:T(8,128)(2,1)S(1)} collective-permute-done((bf16[256,2048]{1,0:T(8,128)(2,1)S(1)}, bf16[256,2048]{1,0:T(8,128)(2,1)S(1)}, u32[]{:S(2)}, u32[]{:S(2)}) %collective-permute-start.47) | collective-permute-done | bytes 1048608 | tf_op jit(solution)/shard_map/ppermute | solution.py:104
  608.2 20.0 %collective-permute-done.44 = bf16[256,2048]{1,0:T(8,128)(2,1)S(1)} collective-permute-done((bf16[256,2048]{1,0:T(8,128)(2,1)S(1)}, bf16[256,2048]{1,0:T(8,128)(2,1)S(1)}, u32[]{:S(2)}, u32[]{:S(2)}) %collective-permute-start.44) | collective-permute-done | bytes 1048608 | tf_op jit(solution)/shard_map/ppermute | solution.py:101
  640.9 13.1 %collective-permute-done.45 = bf16[256,2048]{1,0:T(8,128)(2,1)} collective-permute-done((bf16[256,2048]{1,0:T(8,128)(2,1)}, bf16[256,2048]{1,0:T(8,128)(2,1)}, u32[]{:S(2)}, u32[]{:S(2)}) %collective-permute-start.45) | collective-permute-done | bytes 1048608 | tf_op jit(solution)/shard_map/ppermute | solution.py:101
  667.1 5.9 fusion.8.dm_ref
  687.1 26.9 %attend_back.2 = (bf16[8,256,256]{2,1,0:T(8,128)(2,1)}, bf16[8,256,640]{2,1,0:T(8,128)(2,1)}, f32[128,2048]{1,0:T(8,128)}) custom-call(s32[9]{0:T(128)} %get-tuple-element.246.info, bf16[2048,640]{1,0:T(8,128)(2,1)} %all_latents.1.l_ref, bf16[128,2048]{1,0:T(8,128)(2,1)} %bitcast.226, bf16[16,4,32,1024]{3,2,1,0:T(8,128)(2,1)} %bitcast.193, ...), custom_call_target="tpu_custom_call" | custom-call | flops 13958643712 | bytes 30000000 | tf_op jit(solution)/shard_map/attend_back/pallas_call | solution.py:579
  716.9 27.8 %attend_back.3 = (bf16[8,256,256]{2,1,0:T(8,128)(2,1)}, bf16[8,256,640]{2,1,0:T(8,128)(2,1)}, f32[128,2048]{1,0:T(8,128)}) custom-call(s32[9]{0:T(128)} %get-tuple-element.246.info, bf16[2048,640]{1,0:T(8,128)(2,1)} %all_latents.1.l_ref, bf16[128,2048]{1,0:T(8,128)(2,1)} %bitcast.227, bf16[16,4,32,1024]{3,2,1,0:T(8,128)(2,1)} %bitcast.194, ...), custom_call_target="tpu_custom_call" | custom-call | flops 13958643712 | bytes 30000000 | tf_op jit(solution)/shard_map/attend_back/pallas_call | solution.py:579
  756.4 13.8 %query_back.1 = (f32[256,2048]{1,0:T(8,128)}, f32[256,128]{1,0:T(8,128)}, f32[128,3072]{1,0:T(8,128)}) custom-call(s32[9]{0:T(128)} %get-tuple-element.246.info, bf16[16,256,256]{2,1,0:T(8,128)(2,1)} %pad_maximum_fusion.1.dq_ref, bf16[128,3072]{1,0:T(8,128)(2,1)} %pad.85.refs_2_.up_ref, bf16[128,256]{1,0:T(8,128)(2,1)} %pad_bitcast_fusion.rt_ref, ...), custom_call_target="tpu_custom_call" | custom-call | flops 3221225472 | bytes 12582912 | tf_op jit(solution)/shard_map/query_back/pallas_call | solution.py:404
  832.6 6.8 all-gather
  841.0 5.6 all-to-all-start.4
  855.0 14.4 %all-to-all-done.4 = bf16[8,1,16,3456]{3,2,1,0:T(8,128)(2,1)} async-done(((bf16[8,1,16,3456]{3,2,1,0:T(8,128)(2,1)}), bf16[8,1,16,3456]{3,2,1,0:T(8,128)(2,1)}, u32[]{:S(2)}, u32[]{:S(2)}) %all-to-all-start.4) | async-done | bytes 884768 | tf_op jit(solution)/shard_map/all_to_all | solution.py:846
  (557 shorter events, 317.1 us)
Async XLA Ops:
  7.6 42.0 %collective-permute-start.1 = (bf16[128,6784]{1,0:T(8,128)(2,1)}, bf16[128,6784]{1,0:T(8,128)(2,1)}, u32[]{:S(2)}, u32[]{:S(2)}) collective-permute-start(bf16[128,6784]{1,0:T(8,128)(2,1)} %pack_weights.1.refs_0_.rest_0_), channel_id=1, source_target_pairs={{0,2},{2,4},{4,6},{6,7},{7,5},{5,3},{3,1},{1,0},{8,10},{10,12},{12... | collective-permute-start | bytes 5210120 | tf_op jit(solution)/shard_map/ppermute | solution.py:101
  10.7 41.1 %collective-permute-start.2 = (bf16[128,6784]{1,0:T(8,128)(2,1)}, bf16[128,6784]{1,0:T(8,128)(2,1)}, u32[]{:S(2)}, u32[]{:S(2)}) collective-permute-start(bf16[128,6784]{1,0:T(8,128)(2,1)} %pack_weights.1.refs_0_.rest_0_), channel_id=1, source_target_pairs={{0,1},{2,0},{4,2},{6,4},{7,6},{5,7},{3,5},{1,3},{8,9},{10,8},{12,1... | collective-permute-start | bytes 5210120 | tf_op jit(solution)/shard_map/ppermute | solution.py:104
  10.7 41.7 %collective-permute-start = (bf16[128,6784]{1,0:T(8,128)(2,1)}, bf16[128,6784]{1,0:T(8,128)(2,1)}, u32[]{:S(2)}, u32[]{:S(2)}) collective-permute-start(bf16[128,6784]{1,0:T(8,128)(2,1)} %pack_weights.1.refs_0_.rest_0_), channel_id=1, source_target_pairs={{0,8},{8,0},{16,24},{24,16},{1,9},{9,1},{17,25},{25,17},{2,10},{10... | collective-permute-start | bytes 5210120 | tf_op jit(solution)/shard_map/ppermute | solution.py:163
  12.2 97.2 %all-to-all-start = ((bf16[8,16,3456]{2,1,0:T(8,128)(2,1)}), bf16[8,16,3456]{2,1,0:T(8,128)(2,1)}, u32[]{:S(2)}, u32[]{:S(2)}) async-start(bf16[8,16,3456]{2,1,0:T(8,128)(2,1)} %copy.213), calls=%async_computation | async-start | bytes 1769472 | tf_op jit(solution)/shard_map/all_to_all | solution.py:900
  52.4 47.1 %collective-permute-start.5 = (bf16[128,6784]{1,0:T(8,128)(2,1)}, bf16[128,6784]{1,0:T(8,128)(2,1)}, u32[]{:S(2)}, u32[]{:S(2)}) collective-permute-start(bf16[128,6784]{1,0:T(8,128)(2,1)} %get-tuple-element.103.refs_2_.rest_2_), channel_id=1, source_target_pairs={{0,2},{2,4},{4,6},{6,7},{7,5},{5,3},{3,1},{1,0},{8,10},{10,12},{12... | collective-permute-start | bytes 5210120 | tf_op jit(solution)/shard_map/ppermute | solution.py:101
  54.2 47.8 %collective-permute-start.6 = (bf16[128,6784]{1,0:T(8,128)(2,1)}, bf16[128,6784]{1,0:T(8,128)(2,1)}, u32[]{:S(2)}, u32[]{:S(2)}) collective-permute-start(bf16[128,6784]{1,0:T(8,128)(2,1)} %get-tuple-element.104.refs_4_.rest_4_), channel_id=1, source_target_pairs={{0,1},{2,0},{4,2},{6,4},{7,6},{5,7},{3,5},{1,3},{8,9},{10,8},{12,1... | collective-permute-start | bytes 5210120 | tf_op jit(solution)/shard_map/ppermute | solution.py:104
  102.0 45.6 %collective-permute-start.10 = (bf16[128,6784]{1,0:T(8,128)(2,1)}, bf16[128,6784]{1,0:T(8,128)(2,1)S(1)}, u32[]{:S(2)}, u32[]{:S(2)}) collective-permute-start(bf16[128,6784]{1,0:T(8,128)(2,1)} %get-tuple-element.106.refs_8_.rest_8_), channel_id=1, source_target_pairs={{0,1},{2,0},{4,2},{6,4},{7,6},{5,7},{3,5},{1,3},{8,9},{10,8},{12,1... | collective-permute-start | bytes 5210120 | tf_op jit(solution)/shard_map/ppermute | solution.py:104
  102.2 45.4 %collective-permute-start.7 = (bf16[128,6784]{1,0:T(8,128)(2,1)}, bf16[128,6784]{1,0:T(8,128)(2,1)}, u32[]{:S(2)}, u32[]{:S(2)}) collective-permute-start(bf16[128,6784]{1,0:T(8,128)(2,1)} %get-tuple-element.105.refs_6_.rest_6_), channel_id=1, source_target_pairs={{0,8},{8,0},{16,24},{24,16},{1,9},{9,1},{17,25},{25,17},{2,10},{10... | collective-permute-start | bytes 5210120 | tf_op jit(solution)/shard_map/ppermute | solution.py:163
  102.2 45.4 %collective-permute-start.8 = (bf16[128,6784]{1,0:T(8,128)(2,1)}, bf16[128,6784]{1,0:T(8,128)(2,1)}, u32[]{:S(2)}, u32[]{:S(2)}) collective-permute-start(bf16[128,6784]{1,0:T(8,128)(2,1)} %get-tuple-element.106.refs_8_.rest_8_), channel_id=1, source_target_pairs={{0,8},{8,0},{16,24},{24,16},{1,9},{9,1},{17,25},{25,17},{2,10},{10... | collective-permute-start | bytes 5210120 | tf_op jit(solution)/shard_map/ppermute | solution.py:163
  102.7 45.2 %collective-permute-start.9 = (bf16[128,6784]{1,0:T(8,128)(2,1)}, bf16[128,6784]{1,0:T(8,128)(2,1)}, u32[]{:S(2)}, u32[]{:S(2)}) collective-permute-start(bf16[128,6784]{1,0:T(8,128)(2,1)} %get-tuple-element.105.refs_6_.rest_6_), channel_id=1, source_target_pairs={{0,2},{2,4},{4,6},{6,7},{7,5},{5,3},{3,1},{1,0},{8,10},{10,12},{12... | collective-permute-start | bytes 5210120 | tf_op jit(solution)/shard_map/ppermute | solution.py:101
  111.2 76.0 %all-to-all-start.1 = ((bf16[8,16,3456]{2,1,0:T(8,128)(2,1)}), bf16[8,16,3456]{2,1,0:T(8,128)(2,1)}, u32[]{:S(2)}, u32[]{:S(2)}) async-start(bf16[8,16,3456]{2,1,0:T(8,128)(2,1)} %broadcast_in_dim.19), calls=%async_computation.1 | async-start | bytes 1769472 | tf_op jit(solution)/shard_map/all_to_all | solution.py:903
  151.2 28.1 %collective-permute-start.13 = (bf16[64,6784]{1,0:T(8,128)(2,1)}, bf16[64,6784]{1,0:T(8,128)(2,1)S(1)}, u32[]{:S(2)}, u32[]{:S(2)}) collective-permute-start(bf16[64,6784]{1,0:T(8,128)(2,1)} %slice.337), channel_id=1, source_target_pairs={{0,2},{2,4},{4,6},{6,7},{7,5},{5,3},{3,1},{1,0},{8,10},{10,12},{12... | collective-permute-start | bytes 2605064 | tf_op jit(solution)/shard_map/ppermute | solution.py:101
  154.9 36.7 %collective-permute-start.11 = (bf16[128,6784]{1,0:T(8,128)(2,1)}, bf16[128,6784]{1,0:T(8,128)(2,1)}, u32[]{:S(2)}, u32[]{:S(2)}) collective-permute-start(bf16[128,6784]{1,0:T(8,128)(2,1)} %get-tuple-element.107.refs_10_.rest_10_), channel_id=1, source_target_pairs={{0,8},{8,0},{16,24},{24,16},{1,9},{9,1},{17,25},{25,17},{2,10},{10... | collective-permute-start | bytes 5210120 | tf_op jit(solution)/shard_map/ppermute | solution.py:163
  154.9 36.7 %collective-permute-start.12 = (bf16[128,6784]{1,0:T(8,128)(2,1)S(1)}, bf16[128,6784]{1,0:T(8,128)(2,1)}, u32[]{:S(2)}, u32[]{:S(2)}) collective-permute-start(bf16[128,6784]{1,0:T(8,128)(2,1)S(1)} %copy-done.4), channel_id=1, source_target_pairs={{0,8},{8,0},{16,24},{24,16},{1,9},{9,1},{17,25},{25,17},{2,10},{10... | collective-permute-start | bytes 5210120 | tf_op jit(solution)/shard_map/ppermute | solution.py:163
  263.6 45.5 %collective-permute-start.25 = (bf16[256,2048]{1,0:T(8,128)(2,1)}, bf16[256,2048]{1,0:T(8,128)(2,1)}, u32[]{:S(2)}, u32[]{:S(2)}) collective-permute-start(bf16[256,2048]{1,0:T(8,128)(2,1)} %gate.34), channel_id=1, source_target_pairs={{0,2},{2,4},{4,6},{6,7},{7,5},{5,3},{3,1},{1,0},{8,10},{10,12},{12... | collective-permute-start | bytes 3145736 | tf_op jit(solution)/shard_map/ppermute | solution.py:101
  264.6 44.5 %collective-permute-start.26 = (bf16[256,2048]{1,0:T(8,128)(2,1)}, bf16[256,2048]{1,0:T(8,128)(2,1)}, u32[]{:S(2)}, u32[]{:S(2)}) collective-permute-start(bf16[256,2048]{1,0:T(8,128)(2,1)} %gate.34), channel_id=1, source_target_pairs={{0,1},{2,0},{4,2},{6,4},{7,6},{5,7},{3,5},{1,3},{8,9},{10,8},{12,1... | collective-permute-start | bytes 3145736 | tf_op jit(solution)/shard_map/ppermute | solution.py:104
  265.6 55.0 %all-to-all-start.2 = ((bf16[8,128,768]{2,1,0:T(8,128)(2,1)}), bf16[8,128,768]{2,1,0:T(8,128)(2,1)}, u32[]{:S(2)}, u32[]{:S(2)}) async-start(bf16[8,128,768]{2,1,0:T(8,128)(2,1)} %gate.36), calls=%async_computation.2 | async-start | bytes 3145728 | tf_op jit(solution)/shard_map/all_to_all | solution.py:968
  320.6 32.4 %collective-permute-start.27 = (bf16[8,128,768]{2,1,0:T(8,128)(2,1)}, bf16[8,128,768]{2,1,0:T(8,128)(2,1)}, u32[]{:S(2)}, u32[]{:S(2)}) collective-permute-start(bf16[8,128,768]{2,1,0:T(8,128)(2,1)} %all-to-all-done.2), channel_id=1, source_target_pairs={{0,8},{8,0},{16,24},{24,16},{1,9},{9,1},{17,25},{25,17},{2,10},{10... | collective-permute-start | bytes 4718600 | tf_op jit(solution)/shard_map/ppermute | solution.py:163
  320.9 28.0 %collective-permute-start.28 = (bf16[256,2048]{1,0:T(8,128)(2,1)S(1)}, bf16[256,2048]{1,0:T(8,128)(2,1)}, u32[]{:S(2)}, u32[]{:S(2)}) collective-permute-start(bf16[256,2048]{1,0:T(8,128)(2,1)S(1)} %multiply_convert_fusion.rest_0_), channel_id=1, source_target_pairs={{0,2},{2,4},{4,6},{6,7},{7,5},{5,3},{3,1},{1,0},{8,10},{10,12},{12... | collective-permute-start | bytes 3145736 | tf_op jit(solution)/shard_map/ppermute | solution.py:101
  320.9 27.9 %collective-permute-start.29 = (bf16[256,2048]{1,0:T(8,128)(2,1)S(1)}, bf16[256,2048]{1,0:T(8,128)(2,1)}, u32[]{:S(2)}, u32[]{:S(2)}) collective-permute-start(bf16[256,2048]{1,0:T(8,128)(2,1)S(1)} %multiply_convert_fusion.rest_0_), channel_id=1, source_target_pairs={{0,1},{2,0},{4,2},{6,4},{7,6},{5,7},{3,5},{1,3},{8,9},{10,8},{12,1... | collective-permute-start | bytes 3145736 | tf_op jit(solution)/shard_map/ppermute | solution.py:104
  348.9 26.4 %collective-permute-start.30 = (bf16[256,2048]{1,0:T(8,128)(2,1)}, bf16[256,2048]{1,0:T(8,128)(2,1)}, u32[]{:S(2)}, u32[]{:S(2)}) collective-permute-start(bf16[256,2048]{1,0:T(8,128)(2,1)} %get-tuple-element.120.refs_0_), channel_id=1, source_target_pairs={{0,2},{2,4},{4,6},{6,7},{7,5},{5,3},{3,1},{1,0},{8,10},{10,12},{12... | collective-permute-start | bytes 3145736 | tf_op jit(solution)/shard_map/ppermute | solution.py:101
  349.1 26.4 %collective-permute-start.31 = (bf16[256,2048]{1,0:T(8,128)(2,1)}, bf16[256,2048]{1,0:T(8,128)(2,1)}, u32[]{:S(2)}, u32[]{:S(2)}) collective-permute-start(bf16[256,2048]{1,0:T(8,128)(2,1)} %get-tuple-element.121.refs_1_), channel_id=1, source_target_pairs={{0,1},{2,0},{4,2},{6,4},{7,6},{5,7},{3,5},{1,3},{8,9},{10,8},{12,1... | collective-permute-start | bytes 3145736 | tf_op jit(solution)/shard_map/ppermute | solution.py:104
  351.0 56.9 %collective-permute-start.32 = (bf16[256,2048]{1,0:T(8,128)(2,1)}, bf16[256,2048]{1,0:T(8,128)(2,1)}, u32[]{:S(2)}, u32[]{:S(2)}) collective-permute-start(bf16[256,2048]{1,0:T(8,128)(2,1)} %get-tuple-element.125.rest_2_), channel_id=1, source_target_pairs={{0,2},{2,4},{4,6},{6,7},{7,5},{5,3},{3,1},{1,0},{8,10},{10,12},{12... | collective-permute-start | bytes 3145736 | tf_op jit(solution)/shard_map/ppermute | solution.py:101
  351.1 56.8 %collective-permute-start.33 = (bf16[256,2048]{1,0:T(8,128)(2,1)}, bf16[256,2048]{1,0:T(8,128)(2,1)}, u32[]{:S(2)}, u32[]{:S(2)}) collective-permute-start(bf16[256,2048]{1,0:T(8,128)(2,1)} %get-tuple-element.126.rest_3_), channel_id=1, source_target_pairs={{0,1},{2,0},{4,2},{6,4},{7,6},{5,7},{3,5},{1,3},{8,9},{10,8},{12,1... | collective-permute-start | bytes 3145736 | tf_op jit(solution)/shard_map/ppermute | solution.py:104
  405.8 26.5 %collective-permute-start.34 = (bf16[256,2048]{1,0:T(8,128)(2,1)}, bf16[256,2048]{1,0:T(8,128)(2,1)}, u32[]{:S(2)}, u32[]{:S(2)}) collective-permute-start(bf16[256,2048]{1,0:T(8,128)(2,1)} %get-tuple-element.131.refs_0_.refs_2_), channel_id=1, source_target_pairs={{0,2},{2,4},{4,6},{6,7},{7,5},{5,3},{3,1},{1,0},{8,10},{10,12},{12... | collective-permute-start | bytes 3145736 | tf_op jit(solution)/shard_map/ppermute | solution.py:101
  406.0 26.5 %collective-permute-start.35 = (bf16[256,2048]{1,0:T(8,128)(2,1)}, bf16[256,2048]{1,0:T(8,128)(2,1)}, u32[]{:S(2)}, u32[]{:S(2)}) collective-permute-start(bf16[256,2048]{1,0:T(8,128)(2,1)} %get-tuple-element.132.refs_1_.refs_3_), channel_id=1, source_target_pairs={{0,1},{2,0},{4,2},{6,4},{7,6},{5,7},{3,5},{1,3},{8,9},{10,8},{12,1... | collective-permute-start | bytes 3145736 | tf_op jit(solution)/shard_map/ppermute | solution.py:104
  407.9 58.9 %collective-permute-start.38 = (bf16[256,2048]{1,0:T(8,128)(2,1)}, bf16[256,2048]{1,0:T(8,128)(2,1)}, u32[]{:S(2)}, u32[]{:S(2)}) collective-permute-start(bf16[256,2048]{1,0:T(8,128)(2,1)} %get-tuple-element.136.rest_2_), channel_id=1, source_target_pairs={{0,2},{2,4},{4,6},{6,7},{7,5},{5,3},{3,1},{1,0},{8,10},{10,12},{12... | collective-permute-start | bytes 3145736 | tf_op jit(solution)/shard_map/ppermute | solution.py:101
  408.2 58.6 %collective-permute-start.39 = (bf16[256,2048]{1,0:T(8,128)(2,1)}, bf16[256,2048]{1,0:T(8,128)(2,1)}, u32[]{:S(2)}, u32[]{:S(2)}) collective-permute-start(bf16[256,2048]{1,0:T(8,128)(2,1)} %get-tuple-element.137.rest_3_), channel_id=1, source_target_pairs={{0,1},{2,0},{4,2},{6,4},{7,6},{5,7},{3,5},{1,3},{8,9},{10,8},{12,1... | collective-permute-start | bytes 3145736 | tf_op jit(solution)/shard_map/ppermute | solution.py:104
  682.5 31.5 %collective-permute-start.52 = (bf16[256,2048]{1,0:T(8,128)(2,1)}, bf16[256,2048]{1,0:T(8,128)(2,1)}, u32[]{:S(2)}, u32[]{:S(2)}) collective-permute-start(bf16[256,2048]{1,0:T(8,128)(2,1)} %pad_maximum_fusion.5), channel_id=1, source_target_pairs={{0,2},{2,4},{4,6},{6,7},{7,5},{5,3},{3,1},{1,0},{8,10},{10,12},{12... | collective-permute-start | bytes 3145736 | tf_op jit(solution)/shard_map/ppermute | solution.py:101
  683.6 31.8 %collective-permute-start.53 = (bf16[256,2048]{1,0:T(8,128)(2,1)}, bf16[256,2048]{1,0:T(8,128)(2,1)}, u32[]{:S(2)}, u32[]{:S(2)}) collective-permute-start(bf16[256,2048]{1,0:T(8,128)(2,1)} %pad_maximum_fusion.6), channel_id=1, source_target_pairs={{0,1},{2,0},{4,2},{6,4},{7,6},{5,7},{3,5},{1,3},{8,9},{10,8},{12,1... | collective-permute-start | bytes 3145736 | tf_op jit(solution)/shard_map/ppermute | solution.py:104
  824.0 27.9 %collective-permute-start.62 = (bf16[256,2048]{1,0:T(8,128)(2,1)}, bf16[256,2048]{1,0:T(8,128)(2,1)}, u32[]{:S(2)}, u32[]{:S(2)}) collective-permute-start(bf16[256,2048]{1,0:T(8,128)(2,1)} %get-tuple-element.220), channel_id=1, source_target_pairs={{0,2},{2,4},{4,6},{6,7},{7,5},{5,3},{3,1},{1,0},{8,10},{10,12},{12... | collective-permute-start | bytes 3145736 | tf_op jit(solution)/shard_map/ppermute | solution.py:101
  841.0 28.5 %all-to-all-start.4 = ((bf16[8,1,16,3456]{3,2,1,0:T(8,128)(2,1)}), bf16[8,1,16,3456]{3,2,1,0:T(8,128)(2,1)}, u32[]{:S(2)}, u32[]{:S(2)}) async-start(bf16[8,1,16,3456]{3,2,1,0:T(8,128)(2,1)} %bitcast.214), calls=%async_computation.4 | async-start | bytes 1769472 | tf_op jit(solution)/shard_map/all_to_all | solution.py:846
  (144 other events, 1420.0 us)

commit v3 on v2

--- a/solution.py
+++ b/solution.py
@@ -394,7 +394,11 @@
             still(*rt.shape),
         ]
         + [column(block) for block in blocks],
-        out_specs=[still(tokens, D), still(tokens, LANES), column(up)],
+        out_specs=[
+            still(tokens, D),
+            still(tokens, LANES),
+            pl.BlockSpec((rt.shape[0], width), lambda i, s: (0, i)),
+        ],
         scratch_shapes=[
             pltpu.VMEM((tokens, D), f32),
             pltpu.VMEM((tokens, LANES), f32),
@@ -407,7 +411,7 @@
         out_shape=[
             jax.ShapeDtypeStruct((tokens, D), f32),
             jax.ShapeDtypeStruct((tokens, LANES), f32),
-            jax.ShapeDtypeStruct((LANES, QW), f32),
+            jax.ShapeDtypeStruct((rt.shape[0], QW), f32),
         ],
         compiler_params=params(1),
         cost_estimate=cost(2 * tokens * D * QW, D * QW * 2),
@@ -419,6 +423,7 @@
 
 
 PER_STEP = 2
+SMALL = 2 * RANK
 
 
 def attend_kernel(l_ref, w_ref, u_ref, q_ref, mix_ref, lse_ref, kv_ref):
@@ -572,7 +577,7 @@
         out_specs=[
             pl.BlockSpec((PER_STEP, tokens, 2 * LANES), lambda h, s: (h, 0, 0)),
             pl.BlockSpec((count, length // count, LW), lambda h, s: (0, 0, 0)),
-            pl.BlockSpec((LANES, PER_STEP * wide), lambda h, s: (0, h)),
+            pl.BlockSpec((lt.shape[0], PER_STEP * wide), lambda h, s: (0, h)),
         ],
         scratch_shapes=[pltpu.VMEM((length, LW), f32)],
     )
@@ -582,7 +587,7 @@
         out_shape=[
             jax.ShapeDtypeStruct((heads, tokens, 2 * LANES), bf16),
             jax.ShapeDtypeStruct((count, length // count, LW), bf16),
-            jax.ShapeDtypeStruct((LANES, heads * wide), f32),
+            jax.ShapeDtypeStruct((lt.shape[0], heads * wide), f32),
         ],
         compiler_params=params(1),
         cost_estimate=cost(heads * 2 * length * (LW * 256 + tokens * 1024), 30e6),
@@ -744,10 +749,11 @@
             put = lambda ref: dot(chosen[c], rows(ref, c, a, a + step), TN)
             out_ref[c, :, a : a + step] = (out[at] + put(y_ref)).astype(bf16)
             dout_ref[c, :, a : a + step] = (dx[at] + put(dx_ref)).astype(bf16)
-    gu_up_ref[...] = dot(r, dboth, TN)
-    gu_down_ref[...] = dot(dr.astype(bf16), x, TN)
-    dn_up_ref[...] = dot(rdn, g, TN)
-    dn_down_ref[...] = dot(drdn, inner, TN)
+    few = gu_up_ref.shape[0]
+    gu_up_ref[...] = dot(r, dboth, TN)[:few]
+    gu_down_ref[...] = dot(dr.astype(bf16), x, TN)[:few]
+    dn_up_ref[...] = dot(rdn, g, TN)[:few]
+    dn_down_ref[...] = dot(drdn, inner, TN)[:few]
 
 
 def shared(info, offs, xs, gs, slot_all, experts, y, dx, pull, wi, wo, u, dn):
@@ -759,7 +765,8 @@
     still = lambda *shape: pl.BlockSpec(shape, lambda c, s: (0,) * len(shape))
     operands = [slot_all, y, dx, pull, wi, wo, u, dn, *xs, *gs]
     shapes = [(chunks, tokens, D)] * 2
-    shapes += [(LANES, 2 * half), (LANES, D), (LANES, D), (LANES, half)]
+    few = round_up(experts + RANK, RANK)
+    shapes += [(few, 2 * half), (few, D), (few, D), (few, half)]
     spec = pltpu.PrefetchScalarGridSpec(
         num_scalar_prefetch=1,
         grid=(1,),
@@ -1081,7 +1088,7 @@
     g_out_down = dot(dr_out, mixture, TN)
     delta = (dmix.astype(f32) * mixture.astype(f32)).reshape(tokens, HEADS, VDIM).sum(-1).T
     delta = jnp.broadcast_to(delta[:, None, :], (HEADS, 8, tokens))
-    lt = l_all[:, LATENT:].T
+    lt = l_all[:, LATENT + ROPE : LATENT + ROPE + SMALL].T
     parts = []
 
     def back(*marks):
@@ -1113,7 +1120,7 @@
 
     def query_grads(r, l):
         dq = jnp.concatenate([part[0] for part in parts], 0)
-        seen["q"] = query_back(spots, dq, w_at, w_blocks, u_q, pad_lanes(r_qa, LANES).T)
+        seen["q"] = query_back(spots, dq, w_at, w_blocks, u_q, pad_lanes(r_qa, SMALL).T)
         return (seen["q"][1],)
 
     def dl_arrived(r, l):
@@ -1131,7 +1138,7 @@
     )
     block_out = (after_attn + out_sum).astype(bf16)
     g_ku = jnp.concatenate([part[2] for part in parts], 1)
-    g_kvb_up = g_ku[ROPE : ROPE + RANK]
+    g_kvb_up = g_ku[:RANK]
     dhb_q, dr_q, g_qu = seen["q"]
     dl_own = seen["dl"]
     dr_kv = dl_own[:, LATENT + ROPE : LATENT + ROPE + RANK].astype(bf16)

time: 887 us -> 881 us (level)
    unnamed x238 -> x250, local copies, waits for them, and re-layouts: 32.6 us -> 32.2 us
  transfers between devices with their start and end apart: 71 -> 71, of which waited for: 33 -> 33; matrix products, arithmetic and copies ran while one was open for 16% -> 15% of each run, Pallas kernels for 27% -> 27%
where the time goes in v3:
time: 881 us; the launch traced here: 869 us
  Pallas kernels  333 us (38%)
  waiting for transfers between devices  236 us (27%)
  starting transfers between devices  97.5 us (11%)
  local copies, waits for them, and re-layouts  87.4 us (10%)
  other arithmetic  66.2 us (8%)
  matrix products  31.9 us (4%)
  blocking collectives  12.2 us (1%)
    ppermute x28, waiting for transfers between devices, send_right(): return lax.ppermute(v, 'shard', self.right)  152 us
    pallas_call x4, Pallas kernels, routed(): pl.pallas_call(functools.partial(routed_kernel, offs=offs, slots=slots, w...  128 us
    pallas_call x4, Pallas kernels, shared(): pl.pallas_call(functools.partial(shared_kernel, offs=offs, slots=slots, e...  66.9 us
    ppermute x28, waiting for transfers between devices, send_left(): return lax.ppermute(v, 'shard', self.left)  65.3 us
    pallas_call x2, Pallas kernels, attend_back(): pl.pallas_call(attend_back_kernel, grid_spec=spec, out_shape=[jax.ShapeDt...  53.9 us
    ppermute x28, starting transfers between devices, send_right(): return lax.ppermute(v, 'shard', self.right)  43.9 us
    pallas_call x1, Pallas kernels, attend(): pl.pallas_call(attend_kernel, grid=(HEADS // PER_STEP,), in_specs=[pl.Blo...  33.1 us
    unnamed x250, local copies, waits for them, and re-layouts  32.2 us
  transfers between devices with their start and end apart: 71, of which 33 were waited for; matrix products, arithmetic and copies ran while one was open for 15% of the time, Pallas kernels for 27%

profile of v3, /device:TPU:0, one launch (start us, length us, event | category | flops | bytes accessed | tf_op | source)
XLA Modules:
  0.0 869.1 jit_solution(13180960654966106915)
XLA Ops:
  12.1 6.3 all-to-all-start
  18.4 31.2 %collective-permute-done.1.refs_0_ = bf16[128,6784]{1,0:T(8,128)(2,1)} collective-permute-done((bf16[128,6784]{1,0:T(8,128)(2,1)}, bf16[128,6784]{1,0:T(8,128)(2,1)}, u32[]{:S(2)}, u32[]{:S(2)}) %collective-permute-start.1) | collective-permute-done | bytes 1736736 | tf_op jit(solution)/shard_map/ppermute | solution.py:101
  75.5 24.1 %collective-permute-done.5.refs_0_ = bf16[128,6784]{1,0:T(8,128)(2,1)} collective-permute-done((bf16[128,6784]{1,0:T(8,128)(2,1)}, bf16[128,6784]{1,0:T(8,128)(2,1)}, u32[]{:S(2)}, u32[]{:S(2)}) %collective-permute-start.5) | collective-permute-done | bytes 1736736 | tf_op jit(solution)/shard_map/ppermute | solution.py:101
  102.7 6.0 collective-permute-start.9
  116.8 5.5 all-reduce.21.refs_4_
  122.3 25.3 %collective-permute-done.10.refs_1_ = bf16[128,6784]{1,0:T(8,128)(2,1)S(1)} collective-permute-done((bf16[128,6784]{1,0:T(8,128)(2,1)}, bf16[128,6784]{1,0:T(8,128)(2,1)S(1)}, u32[]{:S(2)}, u32[]{:S(2)}) %collective-permute-start.10) | collective-permute-done | bytes 1736736 | tf_op jit(solution)/shard_map/ppermute | solution.py:104
  156.6 22.6 %collective-permute-done.13.refs_14_.rest_14_ = bf16[64,6784]{1,0:T(8,128)(2,1)S(1)} collective-permute-done((bf16[64,6784]{1,0:T(8,128)(2,1)}, bf16[64,6784]{1,0:T(8,128)(2,1)S(1)}, u32[]{:S(2)}, u32[]{:S(2)}) %collective-permute-start.13) | collective-permute-done | bytes 868384 | tf_op jit(solution)/shard_map/ppermute | solution.py:101
  203.2 6.6 collective-permute-start.17
  213.9 6.5 place_rows.4.refs_2_
  248.6 13.6 %query_heads.1.q_ref = bf16[16,256,256]{2,1,0:T(8,128)(2,1)} custom-call(s32[9]{0:T(128)} %get-tuple-element.246.info, bf16[256,2048]{1,0:T(8,128)(2,1)} %gate.33.hb_ref, bf16[256,128]{1,0:T(8,128)(2,1)} %pad.90.clone.r_ref, bf16[128,3072]{1,0:T(8,128)(2,1)} %pad.88.refs_2_.up_ref, f32[256,128]{1,0:T(8,128)} %get-tuple-element.254.cos_ref, ...), custom_call_target="tpu_custom_call" | custom-call | flops 3221225472 | bytes 12582912 | tf_op jit(solution)/shard_map/query_heads/pallas_call | solution.py:347
  276.0 33.1 %attend.1 = (bf16[256,2048]{1,0:T(8,128)(2,1)}, f32[16,8,256]{2,1,0:T(8,128)}, bf16[2048,4096]{1,0:T(8,128)(2,1)}) custom-call(bf16[2048,640]{1,0:T(8,128)(2,1)} %all_latents.1.l_ref, bf16[16,4,32,1024]{3,2,1,0:T(8,128)(2,1)} %bitcast.192, bf16[128,4096]{1,0:T(8,128)(2,1)} %pad.89.refs_3_.u_ref, bf16[16,256,256]{2,1,0:T(8,128)(2,1)} %query_heads.1.q_ref), custom_call_target="tpu_custom_call" | custom-call | flops 19327352832 | bytes 8000000 | tf_op jit(solution)/shard_map/attend/pallas_call | solution.py:465
  311.3 5.9 multiply_reduce_fusion.2
  324.0 24.9 %routed.4 = (bf16[2,128,2048]{2,1,0:T(8,128)(2,1)}, bf16[2,128,2048]{2,1,0:T(8,128)(2,1)}, bf16[2,128,128]{2,1,0:T(8,128)(2,1)}) custom-call(s32[9]{0:T(128)} %get-tuple-element.245.info, s32[8,2,256]{2,1,0:T(2,128)} %copy_select_fusion.slot_ref, bf16[2048,128]{1,0:T(8,128)(2,1)} %pad.93.wr_ref, bf16[2,2048,2816]{2,1,0:T(8,128)(2,1)} %w_in.7, ...), custom_call_target="tpu_custom_call" | custom-call | flops 8858370048 | bytes 34603008 | tf_op jit(solution)/shard_map/routed/pallas_call | solution.py:681
  357.5 10.5 %shared.4 = (bf16[1,256,2048]{2,1,0:T(8,128)(2,1)}, bf16[1,256,2048]{2,1,0:T(8,128)(2,1)}, f32[32,768]{1,0:T(8,128)}, f32[32,2048]{1,0:T(8,128)}, f32[32,2048]{1,0:T(8,128)}, /*index=5*/f32[32,384]{1,0:T(8,128)}) custom-call(s32[9]{0:T(128)} %get-tuple-element.245.info, s32[8,2,256]{2,1,0:T(2,128)} %copy_select_fusion.slot_ref, ...), custom_call_target="tpu_custom_call" | custom-call | flops 4000000000 | bytes 8000000 | tf_op jit(solution)/shard_map/shared/pallas_call | solution.py:776
  368.0 7.4 collective-permute-done.30.refs_0_
  375.4 30.4 %routed.5 = (bf16[2,256,2048]{2,1,0:T(8,128)(2,1)}, bf16[2,256,2048]{2,1,0:T(8,128)(2,1)}, bf16[2,256,128]{2,1,0:T(8,128)(2,1)}) custom-call(s32[9]{0:T(128)} %get-tuple-element.245.info, s32[8,2,256]{2,1,0:T(2,128)} %copy_select_fusion.slot_ref, bf16[2048,128]{1,0:T(8,128)(2,1)} %pad.93.wr_ref, bf16[2,2048,2816]{2,1,0:T(8,128)(2,1)} %w_in.7, ...), custom_call_target="tpu_custom_call" | custom-call | flops 17716740096 | bytes 34603008 | tf_op jit(solution)/shard_map/routed/pallas_call | solution.py:681
  410.1 16.7 %shared.5 = (bf16[2,256,2048]{2,1,0:T(8,128)(2,1)}, bf16[2,256,2048]{2,1,0:T(8,128)(2,1)}, f32[32,768]{1,0:T(8,128)}, f32[32,2048]{1,0:T(8,128)}, f32[32,2048]{1,0:T(8,128)}, /*index=5*/f32[32,384]{1,0:T(8,128)}) custom-call(s32[9]{0:T(128)} %get-tuple-element.245.info, s32[8,2,256]{2,1,0:T(2,128)} %copy_select_fusion.slot_ref, ...), custom_call_target="tpu_custom_call" | custom-call | flops 8000000000 | bytes 16000000 | tf_op jit(solution)/shard_map/shared/pallas_call | solution.py:776
  432.5 30.6 %routed.6 = (bf16[2,256,2048]{2,1,0:T(8,128)(2,1)}, bf16[2,256,2048]{2,1,0:T(8,128)(2,1)}, bf16[2,256,128]{2,1,0:T(8,128)(2,1)}) custom-call(s32[9]{0:T(128)} %get-tuple-element.245.info, s32[8,2,256]{2,1,0:T(2,128)} %copy_select_fusion.slot_ref, bf16[2048,128]{1,0:T(8,128)(2,1)} %pad.93.wr_ref, bf16[2,2048,2816]{2,1,0:T(8,128)(2,1)} %w_in.7, ...), custom_call_target="tpu_custom_call" | custom-call | flops 17716740096 | bytes 34603008 | tf_op jit(solution)/shard_map/routed/pallas_call | solution.py:681
  475.3 16.7 %shared.6 = (bf16[2,256,2048]{2,1,0:T(8,128)(2,1)}, bf16[2,256,2048]{2,1,0:T(8,128)(2,1)}, f32[32,768]{1,0:T(8,128)}, f32[32,2048]{1,0:T(8,128)}, f32[32,2048]{1,0:T(8,128)}, /*index=5*/f32[32,384]{1,0:T(8,128)}) custom-call(s32[9]{0:T(128)} %get-tuple-element.245.info, s32[8,2,256]{2,1,0:T(2,128)} %copy_select_fusion.slot_ref, ...), custom_call_target="tpu_custom_call" | custom-call | flops 8000000000 | bytes 16000000 | tf_op jit(solution)/shard_map/shared/pallas_call | solution.py:776
  495.5 42.0 %routed.7 = (bf16[2,384,2048]{2,1,0:T(8,128)(2,1)}, bf16[2,384,2048]{2,1,0:T(8,128)(2,1)}, bf16[2,384,128]{2,1,0:T(8,128)(2,1)}) custom-call(s32[9]{0:T(128)} %get-tuple-element.245.info, s32[8,2,256]{2,1,0:T(2,128)} %copy_select_fusion.slot_ref, bf16[2048,128]{1,0:T(8,128)(2,1)} %pad.93.wr_ref, bf16[2,2048,2816]{2,1,0:T(8,128)(2,1)} %w_in.7, ...), custom_call_target="tpu_custom_call" | custom-call | flops 26575110144 | bytes 34603008 | tf_op jit(solution)/shard_map/routed/pallas_call | solution.py:681
  537.5 23.0 %shared.7 = (bf16[3,256,2048]{2,1,0:T(8,128)(2,1)}, bf16[3,256,2048]{2,1,0:T(8,128)(2,1)}, f32[32,768]{1,0:T(8,128)}, f32[32,2048]{1,0:T(8,128)}, f32[32,2048]{1,0:T(8,128)}, /*index=5*/f32[32,384]{1,0:T(8,128)}) custom-call(s32[9]{0:T(128)} %get-tuple-element.245.info, s32[8,2,256]{2,1,0:T(2,128)} %copy_select_fusion.slot_ref, ...), custom_call_target="tpu_custom_call" | custom-call | flops 12000000000 | bytes 24000000 | tf_op jit(solution)/shard_map/shared/pallas_call | solution.py:776
  564.6 9.3 %collective-permute-done.42 = bf16[128,2048]{1,0:T(8,128)(2,1)S(1)} collective-permute-done((bf16[128,2048]{1,0:T(8,128)(2,1)S(1)}, bf16[128,2048]{1,0:T(8,128)(2,1)S(1)}, u32[]{:S(2)}, u32[]{:S(2)}) %collective-permute-start.42) | collective-permute-done | bytes 524320 | tf_op jit(solution)/shard_map/ppermute | solution.py:101
  583.0 20.0 %collective-permute-done.47 = bf16[256,2048]{1,0:T(8,128)(2,1)S(1)} collective-permute-done((bf16[256,2048]{1,0:T(8,128)(2,1)S(1)}, bf16[256,2048]{1,0:T(8,128)(2,1)S(1)}, u32[]{:S(2)}, u32[]{:S(2)}) %collective-permute-start.47) | collective-permute-done | bytes 1048608 | tf_op jit(solution)/shard_map/ppermute | solution.py:104
  606.9 20.0 %collective-permute-done.44 = bf16[256,2048]{1,0:T(8,128)(2,1)S(1)} collective-permute-done((bf16[256,2048]{1,0:T(8,128)(2,1)S(1)}, bf16[256,2048]{1,0:T(8,128)(2,1)S(1)}, u32[]{:S(2)}, u32[]{:S(2)}) %collective-permute-start.44) | collective-permute-done | bytes 1048608 | tf_op jit(solution)/shard_map/ppermute | solution.py:101
  640.3 12.1 %collective-permute-done.45 = bf16[256,2048]{1,0:T(8,128)(2,1)} collective-permute-done((bf16[256,2048]{1,0:T(8,128)(2,1)}, bf16[256,2048]{1,0:T(8,128)(2,1)}, u32[]{:S(2)}, u32[]{:S(2)}) %collective-permute-start.45) | collective-permute-done | bytes 1048608 | tf_op jit(solution)/shard_map/ppermute | solution.py:101
  665.4 5.9 fusion.8.dm_ref
  685.4 26.4 %attend_back.2 = (bf16[8,256,256]{2,1,0:T(8,128)(2,1)}, bf16[8,256,640]{2,1,0:T(8,128)(2,1)}, f32[32,2048]{1,0:T(8,128)}) custom-call(s32[9]{0:T(128)} %get-tuple-element.246.info, bf16[2048,640]{1,0:T(8,128)(2,1)} %all_latents.1.l_ref, bf16[32,2048]{1,0:T(8,128)(2,1)} %bitcast.226, bf16[16,4,32,1024]{3,2,1,0:T(8,128)(2,1)} %bitcast.193, ...), custom_call_target="tpu_custom_call" | custom-call | flops 13958643712 | bytes 30000000 | tf_op jit(solution)/shard_map/attend_back/pallas_call | solution.py:584
  714.8 27.4 %attend_back.3 = (bf16[8,256,256]{2,1,0:T(8,128)(2,1)}, bf16[8,256,640]{2,1,0:T(8,128)(2,1)}, f32[32,2048]{1,0:T(8,128)}) custom-call(s32[9]{0:T(128)} %get-tuple-element.246.info, bf16[2048,640]{1,0:T(8,128)(2,1)} %all_latents.1.l_ref, bf16[32,2048]{1,0:T(8,128)(2,1)} %bitcast.227, bf16[16,4,32,1024]{3,2,1,0:T(8,128)(2,1)} %bitcast.194, ...), custom_call_target="tpu_custom_call" | custom-call | flops 13958643712 | bytes 30000000 | tf_op jit(solution)/shard_map/attend_back/pallas_call | solution.py:584
  754.1 13.4 %query_back.1 = (f32[256,2048]{1,0:T(8,128)}, f32[256,128]{1,0:T(8,128)}, f32[32,3072]{1,0:T(8,128)}) custom-call(s32[9]{0:T(128)} %get-tuple-element.246.info, bf16[16,256,256]{2,1,0:T(8,128)(2,1)} %pad_maximum_fusion.1.dq_ref, bf16[128,3072]{1,0:T(8,128)(2,1)} %pad.88.refs_2_.up_ref, bf16[32,256]{1,0:T(8,128)(2,1)} %pad_bitcast_fusion.rt_ref, ...), custom_call_target="tpu_custom_call" | custom-call | flops 3221225472 | bytes 12582912 | tf_op jit(solution)/shard_map/query_back/pallas_call | solution.py:408
  776.4 5.8 collective-permute-done.60.refs_0_
  827.2 6.7 all-gather
  848.6 14.4 %all-to-all-done.4 = bf16[8,1,16,3456]{3,2,1,0:T(8,128)(2,1)} async-done(((bf16[8,1,16,3456]{3,2,1,0:T(8,128)(2,1)}), bf16[8,1,16,3456]{3,2,1,0:T(8,128)(2,1)}, u32[]{:S(2)}, u32[]{:S(2)}) %all-to-all-start.4) | async-done | bytes 884768 | tf_op jit(solution)/shard_map/all_to_all | solution.py:853
  (568 shorter events, 314.6 us)
Async XLA Ops:
  7.6 42.0 %collective-permute-start.1 = (bf16[128,6784]{1,0:T(8,128)(2,1)}, bf16[128,6784]{1,0:T(8,128)(2,1)}, u32[]{:S(2)}, u32[]{:S(2)}) collective-permute-start(bf16[128,6784]{1,0:T(8,128)(2,1)} %pack_weights.1.refs_0_.rest_0_), channel_id=1, source_target_pairs={{0,2},{2,4},{4,6},{6,7},{7,5},{5,3},{3,1},{1,0},{8,10},{10,12},{12... | collective-permute-start | bytes 5210120 | tf_op jit(solution)/shard_map/ppermute | solution.py:101
  10.7 41.1 %collective-permute-start.2 = (bf16[128,6784]{1,0:T(8,128)(2,1)}, bf16[128,6784]{1,0:T(8,128)(2,1)}, u32[]{:S(2)}, u32[]{:S(2)}) collective-permute-start(bf16[128,6784]{1,0:T(8,128)(2,1)} %pack_weights.1.refs_0_.rest_0_), channel_id=1, source_target_pairs={{0,1},{2,0},{4,2},{6,4},{7,6},{5,7},{3,5},{1,3},{8,9},{10,8},{12,1... | collective-permute-start | bytes 5210120 | tf_op jit(solution)/shard_map/ppermute | solution.py:104
  10.7 41.7 %collective-permute-start = (bf16[128,6784]{1,0:T(8,128)(2,1)}, bf16[128,6784]{1,0:T(8,128)(2,1)}, u32[]{:S(2)}, u32[]{:S(2)}) collective-permute-start(bf16[128,6784]{1,0:T(8,128)(2,1)} %pack_weights.1.refs_0_.rest_0_), channel_id=1, source_target_pairs={{0,8},{8,0},{16,24},{24,16},{1,9},{9,1},{17,25},{25,17},{2,10},{10... | collective-permute-start | bytes 5210120 | tf_op jit(solution)/shard_map/ppermute | solution.py:163
  12.1 97.2 %all-to-all-start = ((bf16[8,16,3456]{2,1,0:T(8,128)(2,1)}), bf16[8,16,3456]{2,1,0:T(8,128)(2,1)}, u32[]{:S(2)}, u32[]{:S(2)}) async-start(bf16[8,16,3456]{2,1,0:T(8,128)(2,1)} %copy.213), calls=%async_computation | async-start | bytes 1769472 | tf_op jit(solution)/shard_map/all_to_all | solution.py:907
  52.4 47.1 %collective-permute-start.5 = (bf16[128,6784]{1,0:T(8,128)(2,1)}, bf16[128,6784]{1,0:T(8,128)(2,1)}, u32[]{:S(2)}, u32[]{:S(2)}) collective-permute-start(bf16[128,6784]{1,0:T(8,128)(2,1)} %get-tuple-element.103.refs_2_.rest_2_), channel_id=1, source_target_pairs={{0,2},{2,4},{4,6},{6,7},{7,5},{5,3},{3,1},{1,0},{8,10},{10,12},{12... | collective-permute-start | bytes 5210120 | tf_op jit(solution)/shard_map/ppermute | solution.py:101
  54.2 47.8 %collective-permute-start.6 = (bf16[128,6784]{1,0:T(8,128)(2,1)}, bf16[128,6784]{1,0:T(8,128)(2,1)}, u32[]{:S(2)}, u32[]{:S(2)}) collective-permute-start(bf16[128,6784]{1,0:T(8,128)(2,1)} %get-tuple-element.104.refs_4_.rest_4_), channel_id=1, source_target_pairs={{0,1},{2,0},{4,2},{6,4},{7,6},{5,7},{3,5},{1,3},{8,9},{10,8},{12,1... | collective-permute-start | bytes 5210120 | tf_op jit(solution)/shard_map/ppermute | solution.py:104
  102.0 45.6 %collective-permute-start.10 = (bf16[128,6784]{1,0:T(8,128)(2,1)}, bf16[128,6784]{1,0:T(8,128)(2,1)S(1)}, u32[]{:S(2)}, u32[]{:S(2)}) collective-permute-start(bf16[128,6784]{1,0:T(8,128)(2,1)} %get-tuple-element.106.refs_8_.rest_8_), channel_id=1, source_target_pairs={{0,1},{2,0},{4,2},{6,4},{7,6},{5,7},{3,5},{1,3},{8,9},{10,8},{12,1... | collective-permute-start | bytes 5210120 | tf_op jit(solution)/shard_map/ppermute | solution.py:104
  102.2 45.4 %collective-permute-start.7 = (bf16[128,6784]{1,0:T(8,128)(2,1)}, bf16[128,6784]{1,0:T(8,128)(2,1)}, u32[]{:S(2)}, u32[]{:S(2)}) collective-permute-start(bf16[128,6784]{1,0:T(8,128)(2,1)} %get-tuple-element.105.refs_6_.rest_6_), channel_id=1, source_target_pairs={{0,8},{8,0},{16,24},{24,16},{1,9},{9,1},{17,25},{25,17},{2,10},{10... | collective-permute-start | bytes 5210120 | tf_op jit(solution)/shard_map/ppermute | solution.py:163
  102.2 45.4 %collective-permute-start.8 = (bf16[128,6784]{1,0:T(8,128)(2,1)}, bf16[128,6784]{1,0:T(8,128)(2,1)}, u32[]{:S(2)}, u32[]{:S(2)}) collective-permute-start(bf16[128,6784]{1,0:T(8,128)(2,1)} %get-tuple-element.106.refs_8_.rest_8_), channel_id=1, source_target_pairs={{0,8},{8,0},{16,24},{24,16},{1,9},{9,1},{17,25},{25,17},{2,10},{10... | collective-permute-start | bytes 5210120 | tf_op jit(solution)/shard_map/ppermute | solution.py:163
  102.7 45.2 %collective-permute-start.9 = (bf16[128,6784]{1,0:T(8,128)(2,1)}, bf16[128,6784]{1,0:T(8,128)(2,1)}, u32[]{:S(2)}, u32[]{:S(2)}) collective-permute-start(bf16[128,6784]{1,0:T(8,128)(2,1)} %get-tuple-element.105.refs_6_.rest_6_), channel_id=1, source_target_pairs={{0,2},{2,4},{4,6},{6,7},{7,5},{5,3},{3,1},{1,0},{8,10},{10,12},{12... | collective-permute-start | bytes 5210120 | tf_op jit(solution)/shard_map/ppermute | solution.py:101
  111.2 76.0 %all-to-all-start.1 = ((bf16[8,16,3456]{2,1,0:T(8,128)(2,1)}), bf16[8,16,3456]{2,1,0:T(8,128)(2,1)}, u32[]{:S(2)}, u32[]{:S(2)}) async-start(bf16[8,16,3456]{2,1,0:T(8,128)(2,1)} %broadcast_in_dim.19), calls=%async_computation.1 | async-start | bytes 1769472 | tf_op jit(solution)/shard_map/all_to_all | solution.py:910
  151.2 28.1 %collective-permute-start.13 = (bf16[64,6784]{1,0:T(8,128)(2,1)}, bf16[64,6784]{1,0:T(8,128)(2,1)S(1)}, u32[]{:S(2)}, u32[]{:S(2)}) collective-permute-start(bf16[64,6784]{1,0:T(8,128)(2,1)} %slice.337), channel_id=1, source_target_pairs={{0,2},{2,4},{4,6},{6,7},{7,5},{5,3},{3,1},{1,0},{8,10},{10,12},{12... | collective-permute-start | bytes 2605064 | tf_op jit(solution)/shard_map/ppermute | solution.py:101
  154.9 36.6 %collective-permute-start.11 = (bf16[128,6784]{1,0:T(8,128)(2,1)}, bf16[128,6784]{1,0:T(8,128)(2,1)}, u32[]{:S(2)}, u32[]{:S(2)}) collective-permute-start(bf16[128,6784]{1,0:T(8,128)(2,1)} %get-tuple-element.107.refs_10_.rest_10_), channel_id=1, source_target_pairs={{0,8},{8,0},{16,24},{24,16},{1,9},{9,1},{17,25},{25,17},{2,10},{10... | collective-permute-start | bytes 5210120 | tf_op jit(solution)/shard_map/ppermute | solution.py:163
  154.9 36.6 %collective-permute-start.12 = (bf16[128,6784]{1,0:T(8,128)(2,1)S(1)}, bf16[128,6784]{1,0:T(8,128)(2,1)}, u32[]{:S(2)}, u32[]{:S(2)}) collective-permute-start(bf16[128,6784]{1,0:T(8,128)(2,1)S(1)} %copy-done.4), channel_id=1, source_target_pairs={{0,8},{8,0},{16,24},{24,16},{1,9},{9,1},{17,25},{25,17},{2,10},{10... | collective-permute-start | bytes 5210120 | tf_op jit(solution)/shard_map/ppermute | solution.py:163
  263.6 45.5 %collective-permute-start.25 = (bf16[256,2048]{1,0:T(8,128)(2,1)}, bf16[256,2048]{1,0:T(8,128)(2,1)}, u32[]{:S(2)}, u32[]{:S(2)}) collective-permute-start(bf16[256,2048]{1,0:T(8,128)(2,1)} %gate.34), channel_id=1, source_target_pairs={{0,2},{2,4},{4,6},{6,7},{7,5},{5,3},{3,1},{1,0},{8,10},{10,12},{12... | collective-permute-start | bytes 3145736 | tf_op jit(solution)/shard_map/ppermute | solution.py:101
  264.6 44.5 %collective-permute-start.26 = (bf16[256,2048]{1,0:T(8,128)(2,1)}, bf16[256,2048]{1,0:T(8,128)(2,1)}, u32[]{:S(2)}, u32[]{:S(2)}) collective-permute-start(bf16[256,2048]{1,0:T(8,128)(2,1)} %gate.34), channel_id=1, source_target_pairs={{0,1},{2,0},{4,2},{6,4},{7,6},{5,7},{3,5},{1,3},{8,9},{10,8},{12,1... | collective-permute-start | bytes 3145736 | tf_op jit(solution)/shard_map/ppermute | solution.py:104
  265.6 55.0 %all-to-all-start.2 = ((bf16[8,128,768]{2,1,0:T(8,128)(2,1)}), bf16[8,128,768]{2,1,0:T(8,128)(2,1)}, u32[]{:S(2)}, u32[]{:S(2)}) async-start(bf16[8,128,768]{2,1,0:T(8,128)(2,1)} %gate.36), calls=%async_computation.2 | async-start | bytes 3145728 | tf_op jit(solution)/shard_map/all_to_all | solution.py:975
  320.6 32.4 %collective-permute-start.27 = (bf16[8,128,768]{2,1,0:T(8,128)(2,1)}, bf16[8,128,768]{2,1,0:T(8,128)(2,1)}, u32[]{:S(2)}, u32[]{:S(2)}) collective-permute-start(bf16[8,128,768]{2,1,0:T(8,128)(2,1)} %all-to-all-done.2), channel_id=1, source_target_pairs={{0,8},{8,0},{16,24},{24,16},{1,9},{9,1},{17,25},{25,17},{2,10},{10... | collective-permute-start | bytes 4718600 | tf_op jit(solution)/shard_map/ppermute | solution.py:163
  320.9 28.0 %collective-permute-start.28 = (bf16[256,2048]{1,0:T(8,128)(2,1)S(1)}, bf16[256,2048]{1,0:T(8,128)(2,1)}, u32[]{:S(2)}, u32[]{:S(2)}) collective-permute-start(bf16[256,2048]{1,0:T(8,128)(2,1)S(1)} %multiply_convert_fusion.rest_0_), channel_id=1, source_target_pairs={{0,2},{2,4},{4,6},{6,7},{7,5},{5,3},{3,1},{1,0},{8,10},{10,12},{12... | collective-permute-start | bytes 3145736 | tf_op jit(solution)/shard_map/ppermute | solution.py:101
  321.0 28.0 %collective-permute-start.29 = (bf16[256,2048]{1,0:T(8,128)(2,1)S(1)}, bf16[256,2048]{1,0:T(8,128)(2,1)}, u32[]{:S(2)}, u32[]{:S(2)}) collective-permute-start(bf16[256,2048]{1,0:T(8,128)(2,1)S(1)} %multiply_convert_fusion.rest_0_), channel_id=1, source_target_pairs={{0,1},{2,0},{4,2},{6,4},{7,6},{5,7},{3,5},{1,3},{8,9},{10,8},{12,1... | collective-permute-start | bytes 3145736 | tf_op jit(solution)/shard_map/ppermute | solution.py:104
  349.0 26.4 %collective-permute-start.30 = (bf16[256,2048]{1,0:T(8,128)(2,1)}, bf16[256,2048]{1,0:T(8,128)(2,1)}, u32[]{:S(2)}, u32[]{:S(2)}) collective-permute-start(bf16[256,2048]{1,0:T(8,128)(2,1)} %get-tuple-element.120.refs_0_), channel_id=1, source_target_pairs={{0,2},{2,4},{4,6},{6,7},{7,5},{5,3},{3,1},{1,0},{8,10},{10,12},{12... | collective-permute-start | bytes 3145736 | tf_op jit(solution)/shard_map/ppermute | solution.py:101
  349.1 26.3 %collective-permute-start.31 = (bf16[256,2048]{1,0:T(8,128)(2,1)}, bf16[256,2048]{1,0:T(8,128)(2,1)}, u32[]{:S(2)}, u32[]{:S(2)}) collective-permute-start(bf16[256,2048]{1,0:T(8,128)(2,1)} %get-tuple-element.121.refs_1_), channel_id=1, source_target_pairs={{0,1},{2,0},{4,2},{6,4},{7,6},{5,7},{3,5},{1,3},{8,9},{10,8},{12,1... | collective-permute-start | bytes 3145736 | tf_op jit(solution)/shard_map/ppermute | solution.py:104
  351.0 56.9 %collective-permute-start.32 = (bf16[256,2048]{1,0:T(8,128)(2,1)}, bf16[256,2048]{1,0:T(8,128)(2,1)}, u32[]{:S(2)}, u32[]{:S(2)}) collective-permute-start(bf16[256,2048]{1,0:T(8,128)(2,1)} %get-tuple-element.125.rest_2_), channel_id=1, source_target_pairs={{0,2},{2,4},{4,6},{6,7},{7,5},{5,3},{3,1},{1,0},{8,10},{10,12},{12... | collective-permute-start | bytes 3145736 | tf_op jit(solution)/shard_map/ppermute | solution.py:101
  351.1 56.8 %collective-permute-start.33 = (bf16[256,2048]{1,0:T(8,128)(2,1)}, bf16[256,2048]{1,0:T(8,128)(2,1)}, u32[]{:S(2)}, u32[]{:S(2)}) collective-permute-start(bf16[256,2048]{1,0:T(8,128)(2,1)} %get-tuple-element.126.rest_3_), channel_id=1, source_target_pairs={{0,1},{2,0},{4,2},{6,4},{7,6},{5,7},{3,5},{1,3},{8,9},{10,8},{12,1... | collective-permute-start | bytes 3145736 | tf_op jit(solution)/shard_map/ppermute | solution.py:104
  405.8 26.5 %collective-permute-start.34 = (bf16[256,2048]{1,0:T(8,128)(2,1)}, bf16[256,2048]{1,0:T(8,128)(2,1)}, u32[]{:S(2)}, u32[]{:S(2)}) collective-permute-start(bf16[256,2048]{1,0:T(8,128)(2,1)} %get-tuple-element.131.refs_0_.refs_2_), channel_id=1, source_target_pairs={{0,2},{2,4},{4,6},{6,7},{7,5},{5,3},{3,1},{1,0},{8,10},{10,12},{12... | collective-permute-start | bytes 3145736 | tf_op jit(solution)/shard_map/ppermute | solution.py:101
  406.0 26.5 %collective-permute-start.35 = (bf16[256,2048]{1,0:T(8,128)(2,1)}, bf16[256,2048]{1,0:T(8,128)(2,1)}, u32[]{:S(2)}, u32[]{:S(2)}) collective-permute-start(bf16[256,2048]{1,0:T(8,128)(2,1)} %get-tuple-element.132.refs_1_.refs_3_), channel_id=1, source_target_pairs={{0,1},{2,0},{4,2},{6,4},{7,6},{5,7},{3,5},{1,3},{8,9},{10,8},{12,1... | collective-permute-start | bytes 3145736 | tf_op jit(solution)/shard_map/ppermute | solution.py:104
  407.9 59.0 %collective-permute-start.38 = (bf16[256,2048]{1,0:T(8,128)(2,1)}, bf16[256,2048]{1,0:T(8,128)(2,1)}, u32[]{:S(2)}, u32[]{:S(2)}) collective-permute-start(bf16[256,2048]{1,0:T(8,128)(2,1)} %get-tuple-element.136.rest_2_), channel_id=1, source_target_pairs={{0,2},{2,4},{4,6},{6,7},{7,5},{5,3},{3,1},{1,0},{8,10},{10,12},{12... | collective-permute-start | bytes 3145736 | tf_op jit(solution)/shard_map/ppermute | solution.py:101
  408.2 58.7 %collective-permute-start.39 = (bf16[256,2048]{1,0:T(8,128)(2,1)}, bf16[256,2048]{1,0:T(8,128)(2,1)}, u32[]{:S(2)}, u32[]{:S(2)}) collective-permute-start(bf16[256,2048]{1,0:T(8,128)(2,1)} %get-tuple-element.137.rest_3_), channel_id=1, source_target_pairs={{0,1},{2,0},{4,2},{6,4},{7,6},{5,7},{3,5},{1,3},{8,9},{10,8},{12,1... | collective-permute-start | bytes 3145736 | tf_op jit(solution)/shard_map/ppermute | solution.py:104
  680.9 30.9 %collective-permute-start.52 = (bf16[256,2048]{1,0:T(8,128)(2,1)}, bf16[256,2048]{1,0:T(8,128)(2,1)}, u32[]{:S(2)}, u32[]{:S(2)}) collective-permute-start(bf16[256,2048]{1,0:T(8,128)(2,1)} %pad_maximum_fusion.5), channel_id=1, source_target_pairs={{0,2},{2,4},{4,6},{6,7},{7,5},{5,3},{3,1},{1,0},{8,10},{10,12},{12... | collective-permute-start | bytes 3145736 | tf_op jit(solution)/shard_map/ppermute | solution.py:101
  682.0 31.3 %collective-permute-start.53 = (bf16[256,2048]{1,0:T(8,128)(2,1)}, bf16[256,2048]{1,0:T(8,128)(2,1)}, u32[]{:S(2)}, u32[]{:S(2)}) collective-permute-start(bf16[256,2048]{1,0:T(8,128)(2,1)} %pad_maximum_fusion.6), channel_id=1, source_target_pairs={{0,1},{2,0},{4,2},{6,4},{7,6},{5,7},{3,5},{1,3},{8,9},{10,8},{12,1... | collective-permute-start | bytes 3145736 | tf_op jit(solution)/shard_map/ppermute | solution.py:104
  818.6 26.8 %collective-permute-start.62 = (bf16[256,2048]{1,0:T(8,128)(2,1)}, bf16[256,2048]{1,0:T(8,128)(2,1)}, u32[]{:S(2)}, u32[]{:S(2)}) collective-permute-start(bf16[256,2048]{1,0:T(8,128)(2,1)} %get-tuple-element.220), channel_id=1, source_target_pairs={{0,2},{2,4},{4,6},{6,7},{7,5},{5,3},{3,1},{1,0},{8,10},{10,12},{12... | collective-permute-start | bytes 3145736 | tf_op jit(solution)/shard_map/ppermute | solution.py:101
  835.6 27.4 %all-to-all-start.4 = ((bf16[8,1,16,3456]{3,2,1,0:T(8,128)(2,1)}), bf16[8,1,16,3456]{3,2,1,0:T(8,128)(2,1)}, u32[]{:S(2)}, u32[]{:S(2)}) async-start(bf16[8,1,16,3456]{3,2,1,0:T(8,128)(2,1)} %bitcast.214), calls=%async_computation.4 | async-start | bytes 1769472 | tf_op jit(solution)/shard_map/all_to_all | solution.py:853
  (149 other events, 1438.5 us)
